TPU v7x, 768 devices: a whole 4x8x12 slice. The times are simulated.
768 devices in a mesh: dp: 24 (over z, core), ctx: 32 (over y, x).
Axes of the slice: x: 4, y: 8, z: 12, core: 2. Of those that a mesh axis runs over, the one named last changes fastest.
Arguments:
- hidden: bfloat16 [202752, 5120], P(('dp', 'ctx')), may hold values from -6 to 6
- value_weight: bfloat16 [5120, 128], replicated, may hold values from -0.078125 to 0.078125
- queries: bfloat16 [202752, 1024], P(('dp', 'ctx'))
- keys: bfloat16 [202752, 128], P(('dp', 'ctx'))
- attn_grad: bfloat16 [202752, 1024], P(('dp', 'ctx')), may hold values from -6 to 6
- segment_ids: int32 [24, 8192], P('dp', 'ctx'), may hold values from 0 to 3, never falling along the last dimension, each value on 1 to 4096 neighbouring positions
- partner: int32 [24], replicated, may hold values from 0 to 23, as said below
Outputs:
- attn_out: bfloat16 [202752, 1024], P(('dp', 'ctx'))
- value_grad: bfloat16 [202752, 128], P(('dp', 'ctx'))
- grad_value_weight: float32 [5120, 128], P('ctx')
Inputs may be any that keep to these rules, and one draw needn't show every extreme that they name: Pairs the data groups: partner[partner[g]] == g and partner[g] != g for every g.
All inputs are finite; a program needn't handle non-finite values.
Results may differ from a plain program's by a relative error of at most 0.0057.
Values may be sent and summed in bfloat16 or wider, within the bound.
No kernel may reach another device: no remote copies, remote signals or barrier semaphores. Data moves between devices by JAX's collectives and lax.ppermute only.
A program may use at most 64 MiB of HBM per device.

v0:
```python
import math

import jax
import jax.numpy as jnp
from jax import lax
from jax.sharding import PartitionSpec as P

big_negative = -1e30


def body(hidden, value_weight, queries, keys, attn_grad, segment_ids, partner):
    tok_rows = segment_ids.shape[1]
    spare_rows = hidden.shape[0] - tok_rows
    head_width = keys.shape[1]
    head_count = queries.shape[1] // head_width
    group_size = lax.axis_size("ctx")
    my_index = lax.axis_index("ctx")
    seq_total = tok_rows * group_size
    spare_total = spare_rows * group_size
    block_rows = math.gcd(seq_total, 512)
    score_scale = head_width ** (-0.5)
    values = jnp.dot(hidden, value_weight, preferred_element_type=jnp.float32).astype(jnp.bfloat16)
    own_labels = segment_ids.reshape(tok_rows).astype(jnp.bfloat16)
    key_rows, value_rows, key_labels, spare_keys, spare_values = (
        lax.all_gather(keys[:tok_rows], "ctx", axis=0, tiled=True),
        lax.all_gather(values[:tok_rows], "ctx", axis=0, tiled=True),
        lax.all_gather(own_labels, "ctx", axis=0, tiled=True),
        lax.all_gather(keys[tok_rows:], "ctx", axis=0, tiled=True),
        lax.all_gather(values[tok_rows:], "ctx", axis=0, tiled=True),
    )
    key_segments = key_labels.astype(jnp.int32)
    query_heads = queries[:tok_rows].reshape(tok_rows, head_count, head_width)
    grad_heads = attn_grad[:tok_rows].reshape(tok_rows, head_count, head_width)
    empty_acc = jnp.zeros((seq_total, head_width), jnp.float32)
    first_pos = my_index * tok_rows
    value_acc = empty_acc
    row_count = query_heads.shape[0]
    query_pos = first_pos + jnp.arange(row_count, dtype=jnp.int32)
    query_segs = lax.dynamic_slice_in_dim(key_segments, first_pos, row_count, 0)
    seg_begin = jnp.sum((key_segments < query_segs[0]).astype(jnp.int32))
    first_block = seg_begin // block_rows
    last_block = (first_pos + row_count - 1) // block_rows + 1

    def scores_at(block_index):
        key_begin = block_index * block_rows
        key_block = lax.dynamic_slice_in_dim(key_rows, key_begin, block_rows, 0)
        seg_block = lax.dynamic_slice_in_dim(key_segments, key_begin, block_rows, 0)
        key_pos = key_begin + jnp.arange(block_rows, dtype=jnp.int32)
        scores = (
            jnp.einsum("qhd,kd->hqk", query_heads, key_block, preferred_element_type=jnp.float32)
            * score_scale
        )
        allowed = (query_segs[:, None] == seg_block[None, :]) & (
            key_pos[None, :] <= query_pos[:, None]
        )
        return (scores, allowed[None], key_begin)

    def stat_step(block_index, running):
        running_max, running_sum = running
        scores, allowed, _ = scores_at(block_index)
        new_max = jnp.maximum(
            running_max, jnp.max(jnp.where(allowed, scores, big_negative), axis=-1)
        )
        running_sum = running_sum * jnp.exp(running_max - new_max) + jnp.sum(
            jnp.where(allowed, jnp.exp(scores - new_max[..., None]), 0.0), axis=-1
        )
        return (new_max, running_sum)

    initial = (
        jnp.full((head_count, row_count), big_negative, jnp.float32),
        jnp.zeros((head_count, row_count), jnp.float32),
    )
    final_max, final_sum = lax.fori_loop(first_block, last_block, stat_step, initial)
    log_total = final_max + jnp.log(final_sum)

    def weight_step(block_index, running):
        out_acc, value_part = running
        scores, allowed, key_begin = scores_at(block_index)
        weights = jnp.where(allowed, jnp.exp(scores - log_total[..., None]), 0.0).astype(
            jnp.bfloat16
        )
        value_block = lax.dynamic_slice_in_dim(value_rows, key_begin, block_rows, 0)
        out_acc = out_acc + jnp.einsum(
            "hqk,kd->qhd", weights, value_block, preferred_element_type=jnp.float32
        )
        key_terms = jnp.einsum(
            "hqk,qhd->kd", weights, grad_heads, preferred_element_type=jnp.float32
        )
        current = lax.dynamic_slice_in_dim(value_part, key_begin, block_rows, 0)
        value_part = lax.dynamic_update_slice_in_dim(value_part, current + key_terms, key_begin, 0)
        return (out_acc, value_part)

    out_zero = jnp.zeros((row_count, head_count, head_width), jnp.float32)
    out_sum, value_acc = lax.fori_loop(first_block, last_block, weight_step, (out_zero, value_acc))
    main_out, value_acc = (
        out_sum.reshape(row_count, head_count * head_width).astype(jnp.bfloat16),
        value_acc,
    )
    spare_heads = queries[tok_rows:].reshape(spare_rows, head_count, head_width)
    spare_grads = attn_grad[tok_rows:].reshape(spare_rows, head_count, head_width)
    spare_pos = my_index * spare_rows + jnp.arange(spare_rows, dtype=jnp.int32)
    spare_scores = (
        jnp.einsum("qhd,kd->hqk", spare_heads, spare_keys, preferred_element_type=jnp.float32)
        * score_scale
    )
    spare_allowed = (jnp.arange(spare_total, dtype=jnp.int32)[None, :] <= spare_pos[:, None])[None]
    spare_max = jnp.max(
        jnp.where(spare_allowed, spare_scores, big_negative), axis=-1, keepdims=True
    )
    spare_log = spare_max + jnp.log(
        jnp.sum(
            jnp.where(spare_allowed, jnp.exp(spare_scores - spare_max), 0.0), axis=-1, keepdims=True
        )
    )
    spare_weights = jnp.where(spare_allowed, jnp.exp(spare_scores - spare_log), 0.0).astype(
        jnp.bfloat16
    )
    spare_out = jnp.einsum(
        "hqk,kd->qhd", spare_weights, spare_values, preferred_element_type=jnp.float32
    )
    spare_out = spare_out.reshape(spare_rows, head_count * head_width).astype(jnp.bfloat16)
    spare_terms = jnp.einsum(
        "hqk,qhd->kd", spare_weights, spare_grads, preferred_element_type=jnp.float32
    )
    main_sum, spare_sum = (
        lax.psum_scatter(value_acc, "ctx", scatter_dimension=0, tiled=True),
        lax.psum_scatter(spare_terms, "ctx", scatter_dimension=0, tiled=True),
    )
    main_grad = main_sum.astype(jnp.bfloat16)
    spare_grad = spare_sum.astype(jnp.bfloat16)
    group_count = lax.axis_size("dp")
    my_partner = partner[lax.axis_index("dp")]
    slot_mask = (jnp.arange(group_count, dtype=jnp.int32) == my_partner)[:, None, None]
    out_slots = jnp.where(slot_mask, spare_out[None], jnp.zeros((), jnp.bfloat16))
    grad_slots = jnp.where(slot_mask, spare_grad[None], jnp.zeros((), jnp.bfloat16))
    got_out, got_grad = (
        lax.all_to_all(out_slots, "dp", split_axis=0, concat_axis=0, tiled=True),
        lax.all_to_all(grad_slots, "dp", split_axis=0, concat_axis=0, tiled=True),
    )
    partner_out = lax.dynamic_index_in_dim(got_out, my_partner, 0, keepdims=False)
    partner_grad = lax.dynamic_index_in_dim(got_grad, my_partner, 0, keepdims=False)
    attn_out = jnp.concatenate([main_out, partner_out], axis=0)
    value_grad = jnp.concatenate([main_grad, partner_grad], axis=0)
    home_grad = jnp.concatenate([main_grad, spare_grad], axis=0)
    share_rows = value_weight.shape[0] // group_size
    local_term = lax.dot_general(
        hidden, home_grad, (((0,), (0,)), ((), ())), preferred_element_type=jnp.float32
    )
    summed = lax.psum(local_term, ("dp", "ctx"))
    weight_grad = lax.dynamic_slice_in_dim(summed, my_index * share_rows, share_rows, 0)
    return (attn_out, value_grad, weight_grad)


def solution(mesh):
    placed = (
        P(("dp", "ctx"), None),
        P(),
        P(("dp", "ctx"), None),
        P(("dp", "ctx"), None),
        P(("dp", "ctx"), None),
        P("dp", "ctx"),
        P(),
    )
    return jax.shard_map(
        body,
        mesh=mesh,
        in_specs=placed,
        out_specs=(P(("dp", "ctx"), None), P(("dp", "ctx"), None), P("ctx", None)),
        check_vma=False,
    )
```

profile of v0, /device:TPU:1, one launch (start us, length us, event | category | flops | bytes accessed | tf_op | source)
XLA Modules:
  0.0 1013.4 jit_solution(17080295816023823587)
XLA Ops:
  7.2 0.0 copy-start
  7.2 0.0 all-gather.6.cloned.1.call-start
  7.2 1.6 slice.29
  8.9 0.0 all-gather.6.cloned.1.call-update
  8.9 0.0 all-gather.4.cloned.1.call-start
  8.9 0.0 copy-done
  9.0 2.2 convolution_convert_fusion
  11.2 0.6 slice.37
  11.8 0.0 all-gather.4.cloned.1.call-update
  11.9 0.0 reduce-scatter.2.cloned.1.call-start
  11.9 32.9 %all-gather = bf16[1,8192]{1,0:T(2,128)(2,1)S(1)} all-gather(bf16[1,256]{1,0:T(2,128)(2,1)S(1)} %convert_element_type.46), channel_id=2, replica_groups=mesh['dp'=24,'ctx'=32] {'ctx'}, dimensions={1}, use_global_device_ids=true | all-gather | bytes 16896 | tf_op jit(solution)/shard_map/all_gather | solution.py:27
  44.9 0.6 constant_dynamic-slice_fusion
  45.5 1.3 convert_reduce_fusion
  49.6 1.0 copy.40
  50.6 1.3 copy.32
  51.9 1.9 slice.31
  53.8 2.0 copy.41
  55.8 2.0 copy.33
  57.9 47.1 %all-gather.6.cloned.1.call-done = bf16[8192,128]{1,0:T(8,128)(2,1)} async-done(((bf16[256,128]{1,0:T(8,128)(2,1)}), bf16[8192,128]{1,0:T(8,128)(2,1)}) %all-gather.6.cloned.1.call-update) | async-done | bytes 2097168 | tf_op jit(solution)/shard_map/all_gather | solution.py:25
  105.0 2.9 while.26
  105.0 0.1 dynamic_slice.71
  105.1 0.2 compare_and_fusion.4
  105.3 1.7 fusion.59
  107.0 0.9 fusion.60
  107.9 87.7 %all-gather.4.cloned.1.call-done = bf16[8192,128]{1,0:T(8,128)(2,1)} async-done(((bf16[256,128]{1,0:T(8,128)(2,1)}), bf16[8192,128]{1,0:T(8,128)(2,1)}) %all-gather.4.cloned.1.call-update) | async-done | bytes 2097168 | tf_op jit(solution)/shard_map/all_gather | solution.py:26
  195.6 1.1 broadcast_in_dim.120
  196.7 2.2 broadcast_in_dim.121
  198.9 6.5 while.27
  198.9 0.1 dynamic_slice.75
  199.0 0.2 compare_and_fusion.5
  199.2 2.1 fusion.67
  201.4 1.5 fusion.68
  202.9 2.6 fusion.69
  205.5 0.0 reduce-scatter.2.cloned.1.call-update
  205.5 0.6 slice-done.1
  206.1 85.9 %all_gather.19 = bf16[256,128]{1,0:T(8,128)(2,1)S(1)} all-gather(bf16[8,128]{1,0:T(8,128)(2,1)S(1)} %slice-done.1), channel_id=1, replica_groups=mesh['dp'=24,'ctx'=32] {'ctx'}, dimensions={0}, use_global_device_ids=true | all-gather | bytes 67584 | tf_op jit(solution)/shard_map/all_gather | solution.py:28
  292.1 0.1 iota_compare_fusion
  292.2 0.2 select_reduce_fusion.1
  292.4 0.2 select_reduce_fusion
  292.6 0.7 slice_bitcast_fusion
  293.3 0.1 select_convert_fusion
  293.4 0.2 convolution_bitcast_fusion.3
  293.6 1.3 dynamic-slice.1
  295.6 0.6 dynamic_slice.36
  296.1 113.1 %all-reduce.5 = bf16[256,128]{1,0:T(8,128)(2,1)S(1)} all-reduce(f32[256,128]{1,0:T(8,128)S(1)} %convolution_bitcast_fusion.3), channel_id=4, replica_groups=mesh['dp'=24,'ctx'=32] {'ctx'}, use_global_device_ids=true, to_apply=%region_10.11.clone | all-reduce | flops 32768 | bytes 196608
  409.3 0.6 iota_compare_fusion.1
  410.0 0.7 broadcast_select_fusion.1
  410.7 54.2 %all-to-all-start.1 = ((bf16[24,8,128]{2,1,0:T(8,128)(2,1)}), bf16[24,8,128]{2,1,0:T(8,128)(2,1)S(1)}, u32[]{:S(2)}, u32[]{:S(2)}) async-start(bf16[24,8,128]{2,1,0:T(8,128)(2,1)} %broadcast_select_fusion.1), calls=%async_computation.2 | async-start | bytes 98304 | tf_op jit(solution)/shard_map/all_to_all | solution.py:138
  464.9 35.6 %all_gather.18 = bf16[256,128]{1,0:T(8,128)(2,1)S(1)} all-gather(bf16[8,128]{1,0:T(8,128)(2,1)S(1)} %slice.38), channel_id=1, replica_groups=mesh['dp'=24,'ctx'=32] {'ctx'}, dimensions={0}, use_global_device_ids=true | all-gather | bytes 67584 | tf_op jit(solution)/shard_map/all_gather | solution.py:29
  500.5 0.1 fusion.25
  500.6 0.9 broadcast_select_fusion
  501.5 0.9 convert_element_type.57
  502.4 19.6 %all-to-all-start = ((bf16[24,8,1024]{2,1,0:T(8,128)(2,1)}), bf16[24,8,1024]{2,1,0:T(8,128)(2,1)S(1)}, u32[]{:S(2)}, u32[]{:S(2)}) async-start(bf16[24,8,1024]{2,1,0:T(8,128)(2,1)} %broadcast_select_fusion), calls=%async_computation | async-start | bytes 786432 | tf_op jit(solution)/shard_map/all_to_all | solution.py:137
  522.0 0.0 all-reduce.4.cloned.1.call-start
  522.0 2.5 convolution_bitcast_fusion.2
  524.5 0.0 all-reduce.4.cloned.1.call-update
  526.5 13.7 %all-to-all-done = bf16[24,8,1024]{2,1,0:T(8,128)(2,1)S(1)} async-done(((bf16[24,8,1024]{2,1,0:T(8,128)(2,1)}), bf16[24,8,1024]{2,1,0:T(8,128)(2,1)S(1)}, u32[]{:S(2)}, u32[]{:S(2)}) %all-to-all-start) | async-done | bytes 393248 | tf_op jit(solution)/shard_map/all_to_all | solution.py:137
  540.2 1.3 convert_element_type.51
  541.5 1.0 copy.38
  542.5 1.9 pad_maximum_fusion
  544.4 0.6 pad_maximum_fusion.1
  545.0 460.0 %all-reduce.4.cloned.1.call-done = f32[5120,128]{0,1:T(8,128)} async-done(((f32[5120,128]{0,1:T(8,128)}), f32[5120,128]{0,1:T(8,128)}) %all-reduce.4.cloned.1.call-update) | async-done | bytes 2621456 | tf_op jit(solution)/shard_map/psum | solution.py:149
  1005.1 1.0 constant_dynamic-slice_fusion.2
  1006.1 0.7 copy.36
  (37 shorter events, 0.2 us)
Async XLA Ops:
  7.2 1.8 copy-start
  7.2 97.8 %all-gather.6.cloned.1.call-start = ((), (), s32[]{:S(2)}) async-start(), calls=%async_computation.4 | async-start | bytes 2162688 | tf_op jit(solution)/shard_map/all_gather | solution.py:25
  8.9 3.0 copy-start.5
  8.9 40.7 %slice-start = ((bf16[264,1024]{1,0:T(8,128)(2,1)}), bf16[256,1024]{1,0:T(8,128)(2,1)S(1)}, s32[]{:S(2)}) async-start(bf16[264,1024]{1,0:T(8,128)(2,1)} %param.13), calls=%async_computation.7 | async-start | bytes 1048576 | tf_op jit(solution)/shard_map/slice | solution.py:32
  8.9 186.7 %all-gather.4.cloned.1.call-start = ((), (), s32[]{:S(2)}) async-start(), calls=%async_computation.3 | async-start | bytes 2162688 | tf_op jit(solution)/shard_map/all_gather | solution.py:26
  11.9 489.6 %reduce-scatter.2.cloned.1.call-start = ((), (), s32[]{:S(2)}) async-start(), calls=%async_computation.5 | async-start | bytes 4325376 | tf_op jit(solution)/shard_map/reduce_scatter | solution.py:126
  199.2 2.1 copy-start.1
  201.4 1.5 copy-start.3
  202.8 2.6 copy-start.2
  205.5 0.7 slice-start.1
  205.5 86.7 %copy-start.4 = (bf16[264,1024]{1,0:T(8,128)(2,1)S(1)}, bf16[264,1024]{1,0:T(8,128)(2,1)}, u32[]{:S(2)}) copy-start(bf16[264,1024]{1,0:T(8,128)(2,1)} %param.13) | copy-start | bytes 1622020
  205.5 90.1 %copy-start.6 = (s32[24]{0:T(128)S(1)}, s32[24]{0:T(128)}, u32[]{:S(2)}) copy-start(s32[24]{0:T(128)} %param.17) | copy-start | bytes 292
  410.7 91.7 %all-to-all-start.1 = ((bf16[24,8,128]{2,1,0:T(8,128)(2,1)}), bf16[24,8,128]{2,1,0:T(8,128)(2,1)S(1)}, u32[]{:S(2)}, u32[]{:S(2)}) async-start(bf16[24,8,128]{2,1,0:T(8,128)(2,1)} %broadcast_select_fusion.1), calls=%async_computation.2 | async-start | bytes 98304 | tf_op jit(solution)/shard_map/all_to_all | solution.py:138
  502.4 37.8 %all-to-all-start = ((bf16[24,8,1024]{2,1,0:T(8,128)(2,1)}), bf16[24,8,1024]{2,1,0:T(8,128)(2,1)S(1)}, u32[]{:S(2)}, u32[]{:S(2)}) async-start(bf16[24,8,1024]{2,1,0:T(8,128)(2,1)} %broadcast_select_fusion), calls=%async_computation | async-start | bytes 786432 | tf_op jit(solution)/shard_map/all_to_all | solution.py:137
  522.0 483.1 %all-reduce.4.cloned.1.call-start = ((), (), s32[]{:S(2)}) async-start(), calls=%async_computation.6 | async-start | bytes 5242880 | tf_op jit(solution)/shard_map/psum | solution.py:149
Sparse Core Ops, SparseCore 0:
  12.3 92.5 all-gather.5
  109.3 86.2 all-gather.3
  205.6 280.2 reduce-scatter.1
  528.8 476.2 all-reduce.3
where the time goes:
time: 1020 us; the launch traced here: 1010 us
  waiting for transfers between devices  609 us (60%)
  blocking collectives  268 us (26%)
  starting transfers between devices  73.9 us (7%)
  local copies, waits for them, and re-layouts  20.7 us (2%)
  between operations  19.3 us (2%)
  matrix products  13.1 us (1%)
    psum x1, waiting for transfers between devices, body(): summed = lax.psum(local_term, ('dp', 'ctx'))  460 us
    unnamed x1, blocking collectives  113 us
    all_gather x1, waiting for transfers between devices, body(): lax.all_gather(values[:tok_rows], 'ctx', axis=0, tiled=True)  87.7 us
    all_gather x1, blocking collectives, body(): lax.all_gather(keys[tok_rows:], 'ctx', axis=0, tiled=True)  85.9 us
    all_to_all x1, starting transfers between devices, body(): lax.all_to_all(grad_slots, 'dp', split_axis=0, concat_axis=0, tiled=True)  54.2 us
    all_gather x1, waiting for transfers between devices, body(): lax.all_gather(keys[:tok_rows], 'ctx', axis=0, tiled=True)  47.1 us
    all_gather x1, blocking collectives, body(): lax.all_gather(values[tok_rows:], 'ctx', axis=0, tiled=True)  35.6 us
    all_gather x1, blocking collectives, body(): lax.all_gather(own_labels, 'ctx', axis=0, tiled=True)  32.9 us
  transfers between devices with their start and end apart: 6, of which 4 were waited for; matrix products, arithmetic and copies ran while one was open for 3% of the time, Pallas kernels for 0%

commit v1 on v0

v1 whole, which is shorter than its diff:
```python
import functools
import math

import jax
import jax.numpy as jnp
from jax import lax
from jax.experimental import pallas as pl
from jax.experimental.pallas import tpu as pltpu
from jax.sharding import Mesh
from jax.sharding import PartitionSpec as P

BF16 = jnp.bfloat16
F32 = jnp.float32
NEG = -1e30
BIG = 1e30

NZ, NK, NY, NX = 12, 2, 8, 4
MAX_SEG = 4096


def dot(a, b, dims):
    return lax.dot_general(a, b, (dims, ((), ())), preferred_element_type=F32)


def project_kernel(hidden_ref, weight_ref, keys_ref, ids_ref, main_ref, extra_ref):
    tok = main_ref.shape[0]
    width = keys_ref.shape[1]
    values = dot(hidden_ref[...], weight_ref[...], ((1,), (0,)))
    keys = keys_ref[...].astype(F32)
    ids = ids_ref[...]
    level = lax.broadcasted_iota(jnp.int32, (8, tok), 0)
    below = jnp.sum((jnp.broadcast_to(ids, (8, tok)) < level).astype(F32), axis=1, keepdims=True)
    counts = jnp.broadcast_to(below, (8, 2 * width))
    spare = jnp.concatenate([keys[tok:], values[tok:]], axis=1)
    main_ref[...] = jnp.concatenate([keys[:tok], values[:tok]], axis=1).astype(BF16)
    extra_ref[...] = jnp.concatenate([spare, counts], axis=0).astype(BF16)


def attend_kernel(
    place_ref,
    extra_ref,
    ids_ref,
    q_ref,
    do_ref,
    qs_ref,
    dos_ref,
    kv_ref,
    kv1_ref,
    kv2_ref,
    kv3_ref,
    out_ref,
    outs_ref,
    dv_ref,
    bias_ref,
    mask_max,
    mid_max,
    mid_shift,
    total_ref,
    acc_ref,
    p_ref,
    grad_ref,
    pack_ref,
    copy_sems,
    *,
    back,
):
    tok = ids_ref.shape[1]
    width = kv_ref.shape[1] // 2
    heads = q_ref.shape[1] // width
    rows = heads * tok
    group = NY * NX
    spare = extra_ref.shape[0] // group - 8
    spare_heads = qs_ref.shape[0]
    factor = width ** (-0.5) * math.log2(math.e)
    y_at, x_at = place_ref[0], place_ref[1]
    own = y_at * NX + x_at

    copies = []
    for s, piece in enumerate((kv_ref, kv1_ref, kv2_ref, kv3_ref)):
        column = lax.rem(x_at - s + NX, NX)
        start = jnp.where((column < x_at) & (s > 0), tok, 0)
        target = pack_ref.at[column, pl.ds(pl.multiple_of(start, tok), piece.shape[0])]
        copies.append(pltpu.make_async_copy(piece, target, copy_sems.at[s]))
    for copy in copies:
        copy.start()

    dv_ref[...] = jnp.zeros_like(dv_ref)
    mask_max[...] = jnp.full_like(mask_max, NEG)
    mid_max[...] = jnp.full_like(mid_max, NEG)
    total_ref[...] = jnp.zeros_like(total_ref)
    acc_ref[...] = jnp.zeros_like(acc_ref)

    extra = extra_ref[...].astype(F32).reshape(group, spare + 8, 2 * width)
    counts = jnp.sum(extra[:, spare:, :], axis=0)[:, :tok]
    ids = ids_ref[...]
    begin = jnp.zeros((1, tok), F32)
    for v in range(1, 4):
        begin = jnp.where(ids == v, counts[v : v + 1, :], begin)
    first = jnp.min(begin).astype(jnp.int32)
    begin = begin.astype(jnp.int32)
    in_first = begin == first

    base = (y_at - back) * NX
    last = back * NX + x_at
    low = jnp.maximum(first // tok - base, x_at)
    low = jnp.minimum(low, last)

    def set_bias(n):
        position = (base + n) * tok + lax.broadcasted_iota(jnp.int32, (tok, tok), 0)
        query = own * tok + lax.broadcasted_iota(jnp.int32, (tok, tok), 1)
        allowed = (position >= begin) & (position <= query)
        bias_ref[...] = jnp.where(allowed, 0.0, NEG)

    def chunk(n, part):
        start = pl.multiple_of(lax.div(n, NX) * tok, tok)
        return pack_ref[lax.rem(n, NX), pl.ds(start, tok), part]

    def scores(key_block, h):
        return dot(key_block, q_ref[:tok, h * width : (h + 1) * width], ((1,), (1,)))

    def fold(a):
        return a.reshape(tok // 8, 8, tok)

    def max_masked(n):
        set_bias(n)
        key_block = chunk(n, slice(0, width))
        for h in range(heads):
            at = slice(h * tok, (h + 1) * tok)
            s = scores(key_block, h) * factor + bias_ref[...]
            mask_max[:, at] = jnp.maximum(mask_max[:, at], jnp.max(fold(s), axis=0))

    def max_mid(n, carry):
        key_block = chunk(n, slice(0, width))
        for h in range(heads):
            at = slice(h * tok, (h + 1) * tok)
            s = scores(key_block, h)
            mid_max[:, at] = jnp.maximum(mid_max[:, at], jnp.max(fold(s), axis=0))
        return carry

    for copy in copies:
        copy.wait()

    pl.when(low < last)(lambda: max_masked(low))
    lax.fori_loop(low + 1, last, max_mid, 0)
    max_masked(last)
    first_rows = jnp.concatenate([in_first] * heads, axis=1)
    top = jnp.max(mask_max[...], axis=0, keepdims=True)
    mid_top = jnp.max(mid_max[...], axis=0, keepdims=True) * factor
    top = jnp.where(first_rows, jnp.maximum(top, mid_top), top)
    mask_max[...] = jnp.broadcast_to(top, mask_max.shape)
    mid_shift[...] = jnp.broadcast_to(jnp.where(first_rows, top, BIG), mid_shift.shape)

    def weigh(n, shift_ref, masked):
        key_block = chunk(n, slice(0, width))
        value_t = chunk(n, slice(width, 2 * width)).astype(F32).T.astype(BF16)
        for h in range(heads):
            at = slice(h * tok, (h + 1) * tok)
            s = scores(key_block, h) * factor
            if masked:
                s = s + bias_ref[...]
            p = jnp.exp2(s - shift_ref[0:1, at])
            total_ref[:, at] += jnp.sum(fold(p), axis=0)
            p = p.astype(BF16)
            p_ref[n - x_at, :, at] = p
            acc_ref[:, at] += dot(value_t, p, ((1,), (0,)))

    def weigh_mid(n, carry):
        weigh(n, mid_shift, False)
        return carry

    weigh(last, mask_max, True)
    lax.fori_loop(low + 1, last, weigh_mid, 0)

    @pl.when(low < last)
    def _():
        set_bias(low)
        weigh(low, mask_max, True)

    share = 1.0 / jnp.sum(total_ref[...], axis=0, keepdims=True)
    for h in range(heads):
        at = slice(h * tok, (h + 1) * tok)
        part = slice(h * width, (h + 1) * width)
        head_share = jnp.broadcast_to(share[:, at], (width, tok))
        out_ref[:tok, part] = (acc_ref[:, at] * head_share).T.astype(BF16)
        grad_ref[at, :] = (do_ref[:tok, part].astype(F32) * head_share.T).astype(BF16)

    def spread(n, carry):
        got = dot(p_ref[n - x_at], grad_ref[...], ((1,), (0,)))
        column = lax.rem(n, NX)
        row = lax.div(n, NX)
        dv_ref[column, pl.ds(pl.multiple_of(row * tok, tok), tok), :] = got.astype(BF16)
        return carry

    lax.fori_loop(low, last + 1, spread, 0)

    spare_total = group * spare
    block = extra[:, :spare, :].reshape(spare_total, 2 * width).astype(BF16)
    s = dot(block[:, :width], qs_ref[...], ((1,), (1,))) * factor
    key_at = lax.broadcasted_iota(jnp.int32, (spare_total, spare_heads), 0)
    query_at = own * spare + lax.div(
        lax.broadcasted_iota(jnp.int32, (spare_total, spare_heads), 1), heads
    )
    allowed = key_at <= query_at
    s = jnp.where(allowed, s, NEG)
    p = jnp.where(allowed, jnp.exp2(s - jnp.max(s, axis=0, keepdims=True)), 0.0)
    p = (p * (1.0 / jnp.sum(p, axis=0, keepdims=True))).astype(BF16)
    outs_ref[...] = dot(p, block[:, width:], ((0,), (0,))).astype(BF16)
    got = dot(p, dos_ref[...], ((1,), (0,))).reshape(NY, NX, spare, width)
    for xx in range(NX):
        dv_ref[xx, (back + 1) * tok :, :] = got[:, xx].reshape(NY * spare, width).astype(BF16)


VMEM = pl.BlockSpec(memory_space=pltpu.VMEM)
SMEM = pl.BlockSpec(memory_space=pltpu.SMEM)
LIMIT = pltpu.CompilerParams(vmem_limit_bytes=50 * 1024 * 1024)


def project(hidden, value_weight, keys, segment_ids):
    tok = segment_ids.shape[1]
    width = keys.shape[1]
    return pl.pallas_call(
        project_kernel,
        out_shape=(
            jax.ShapeDtypeStruct((tok, 2 * width), BF16),
            jax.ShapeDtypeStruct((16, 2 * width), BF16),
        ),
        in_specs=[VMEM] * 4,
        out_specs=(VMEM, VMEM),
        compiler_params=LIMIT,
        name="project",
    )(hidden, value_weight, keys, segment_ids)


def attend(place, extra, segment_ids, queries, attn_grad, spare_q, spare_do, pieces, back):
    tok = segment_ids.shape[1]
    width = pieces[0].shape[1] // 2
    heads = queries.shape[1] // width
    spare = extra.shape[0] // (NY * NX) - 8
    rows = heads * tok
    return pl.pallas_call(
        functools.partial(attend_kernel, back=back),
        out_shape=(
            jax.ShapeDtypeStruct(queries.shape, BF16),
            jax.ShapeDtypeStruct(spare_q.shape, BF16),
            jax.ShapeDtypeStruct((NX, (back + 1) * tok + NY * spare, width), BF16),
        ),
        in_specs=[SMEM] + [VMEM] * 6 + [pl.BlockSpec(memory_space=pl.ANY)] * NX,
        out_specs=(VMEM, VMEM, VMEM),
        scratch_shapes=[
            pltpu.VMEM((tok, tok), F32),
            pltpu.VMEM((8, rows), F32),
            pltpu.VMEM((8, rows), F32),
            pltpu.VMEM((8, rows), F32),
            pltpu.VMEM((8, rows), F32),
            pltpu.VMEM((width, rows), F32),
            pltpu.VMEM((back * NX + 1, tok, rows), BF16),
            pltpu.VMEM((rows, width), BF16),
            pltpu.VMEM((NX, (back + 1) * tok, 2 * width), BF16),
            pltpu.SemaphoreType.DMA((NX,)),
        ],
        compiler_params=LIMIT,
        name="attend",
    )(place, extra, segment_ids, queries, attn_grad, spare_q, spare_do, *pieces)


def shift(array, axis, size, step):
    return lax.ppermute(array, axis, [(i, (i + step) % size) for i in range(size)])


def body(hidden, value_weight, queries, keys, attn_grad, segment_ids, partner):
    tok = segment_ids.shape[1]
    spare = hidden.shape[0] - tok
    width = keys.shape[1]
    heads = queries.shape[1] // width
    back = MAX_SEG // (tok * NX)
    y_at, x_at, k_at = lax.axis_index("y"), lax.axis_index("x"), lax.axis_index("k")

    main, extra = project(hidden, value_weight, keys, segment_ids)
    spare_q = queries[tok:].reshape(spare * heads, width)
    spare_do = attn_grad[tok:].reshape(spare * heads, width)

    rows = [shift(main, "y", NY, k) for k in range(back, 0, -1)] + [main]
    extras = lax.all_to_all(
        jnp.broadcast_to(extra[None], (NY * NX,) + extra.shape), ("y", "x"), 0, 0, tiled=True
    ).reshape(NY * NX * extra.shape[0], 2 * width)
    column = jnp.concatenate(rows, axis=0)
    early, late = column[: back * tok], column[tok:]
    pieces = [column]
    for s in range(1, NX):
        send = jnp.where(x_at + s < NX, late, early)
        pieces.append(shift(send, "x", NX, s))

    place = jnp.stack([y_at, x_at]).astype(jnp.int32)
    main_out, spare_out, sums = attend(
        place, extras, segment_ids, queries, attn_grad, spare_q, spare_do, pieces, back
    )

    got = lax.all_to_all(sums, "x", 0, 0, tiled=True)
    got = jnp.sum(got.astype(F32), axis=0).astype(BF16)
    main_part = got[: (back + 1) * tok].reshape(back + 1, tok, width)
    main_part = jnp.concatenate(
        [main_part, jnp.zeros((NY - back - 1, tok, width), BF16)], axis=0
    )
    main_part = jnp.concatenate([main_part, main_part], axis=0)
    main_part = lax.dynamic_slice_in_dim(main_part, (back - y_at + NY) % NY, NY, 0)
    spare_part = got[(back + 1) * tok :].reshape(NY, spare, width)
    got = lax.all_to_all(jnp.concatenate([main_part, spare_part], axis=1), "y", 0, 0, tiled=True)
    home = jnp.sum(got.astype(F32), axis=0).astype(BF16)

    term = dot(hidden, home, ((0,), (0,))).reshape(NY * NX, NK, -1, width)
    mine = lax.dynamic_index_in_dim(term, k_at, 1, keepdims=False)
    other = lax.dynamic_index_in_dim(term, 1 - k_at, 1, keepdims=False).astype(BF16)
    both = (mine + shift(other, "k", NK, 1).astype(F32)).astype(BF16)
    got = lax.all_to_all(both, ("y", "x"), 0, 0, tiled=True)
    share = jnp.sum(got.astype(F32), axis=0).astype(BF16)

    bundle = jnp.concatenate([share, home[tok:], spare_out], axis=0)
    every = lax.all_gather(bundle, ("z", "k"), axis=0)
    count = share.shape[0]
    weight_grad = jnp.sum(
        every[:, :count].astype(F32).reshape(NZ, NK * count, width), axis=0
    )
    my_partner = partner[lax.axis_index("z") * NK + k_at]
    traded = lax.dynamic_index_in_dim(every[:, count:], my_partner, 0, keepdims=False)
    attn_out = lax.dynamic_update_slice(
        main_out, traded[spare:].reshape(spare, heads * width), (tok, 0)
    )
    value_grad = jnp.concatenate([home[:tok], traded[:spare]], axis=0)
    return (attn_out, value_grad, weight_grad)


def solution(mesh):
    grid = Mesh(mesh.devices.reshape(NZ, NK, NY, NX), ("z", "k", "y", "x"))
    everywhere = P(("z", "k", "y", "x"), None)
    placed = (
        everywhere,
        P(),
        everywhere,
        everywhere,
        everywhere,
        P(("z", "k"), ("y", "x")),
        P(),
    )
    return jax.shard_map(
        body,
        mesh=grid,
        in_specs=placed,
        out_specs=(everywhere, everywhere, P(("y", "x"), None)),
        check_vma=False,
    )
```

time: 1020 us -> 244 us (0.24)
  waiting for transfers between devices: 609 us -> 81.3 us
  blocking collectives: 268 us -> 40.4 us
  between operations: 19.3 us -> 2.96 us
  starting transfers between devices: 73.9 us -> 87.9 us
  local copies, waits for them, and re-layouts: 20.7 us -> 9.78 us
    psum x1 -> x0, waiting for transfers between devices: 460 us -> none  [body(): summed = lax.psum(local_term, ('dp', 'ctx'))]
    all_gather x2 -> x0, waiting for transfers between devices: 135 us -> none  [the longest x1 87.7 us: body(): lax.all_gather(values[:tok_rows], 'ctx', axis=0, tiled=True)]
    all_gather x3 -> x1, blocking collectives: 154 us -> 40.4 us  [body(): every = lax.all_gather(bundle, ('z', 'k'), axis=0)]
    unnamed x1 -> x0, blocking collectives: 113 us -> none
    all_to_all x2 -> x4, waiting for transfers between devices: 13.7 us -> 64.4 us  [the longest x1 17.9 us: body(): got = lax.all_to_all(sums, 'x', 0, 0, tiled=True)]
    ppermute x0 -> x8, starting transfers between devices: none -> 28.5 us  [shift(): lax.ppermute(array, axis, [(i, (i + step) % size) for i in range(size)])]
    ppermute x0 -> x8, waiting for transfers between devices: none -> 17 us  [shift(): lax.ppermute(array, axis, [(i, (i + step) % size) for i in range(size)])]
    all_to_all x2 -> x4, starting transfers between devices: 73.7 us -> 59.4 us  [the longest x1 35.9 us: body(): lax.all_to_all(jnp.concatenate([main_part, spare_part], axis=1), 'y', 0,...]
  transfers between devices with their start and end apart: 6 -> 12, of which waited for: 4 -> 8; matrix products, arithmetic and copies ran while one was open for 3% -> 1% of each run, Pallas kernels for 0% -> 0%
where the time goes in v1:
time: 244 us; the launch traced here: 243 us
  starting transfers between devices  87.9 us (36%)
  waiting for transfers between devices  81.3 us (33%)
  blocking collectives  40.4 us (17%)
  local copies, waits for them, and re-layouts  9.78 us (4%)
  Pallas kernels  9.57 us (4%)
  other arithmetic  6.81 us (3%)
  matrix products  4.31 us (2%)
  between operations  2.96 us (1%)
    all_gather x1, blocking collectives, body(): every = lax.all_gather(bundle, ('z', 'k'), axis=0)  40.4 us
    all_to_all x1, starting transfers between devices, body(): lax.all_to_all(jnp.concatenate([main_part, spare_part], axis=1), 'y', 0,...  35.9 us
    ppermute x8, starting transfers between devices, shift(): lax.ppermute(array, axis, [(i, (i + step) % size) for i in range(size)])  28.5 us
    all_to_all x1, waiting for transfers between devices, body(): got = lax.all_to_all(sums, 'x', 0, 0, tiled=True)  17.9 us
    ppermute x8, waiting for transfers between devices, shift(): lax.ppermute(array, axis, [(i, (i + step) % size) for i in range(size)])  17 us
    all_to_all x1, waiting for transfers between devices, body(): got = lax.all_to_all(both, ('y', 'x'), 0, 0, tiled=True)  16.9 us
    all_to_all x1, waiting for transfers between devices, body(): lax.all_to_all(jnp.broadcast_to(extra[None], (NY * NX,) + extra.shape), (...  15.3 us
    all_to_all x1, waiting for transfers between devices, body(): lax.all_to_all(jnp.concatenate([main_part, spare_part], axis=1), 'y', 0,...  14.2 us
  transfers between devices with their start and end apart: 12, of which 8 were waited for; matrix products, arithmetic and copies ran while one was open for 1% of the time, Pallas kernels for 0%

profile of v1, /device:TPU:1, one launch (start us, length us, event | category | flops | bytes accessed | tf_op | source)
XLA Modules:
  0.0 243.1 jit_solution(11033330432030905674)
XLA Ops:
  0.6 0.0 copy-start
  0.6 1.3 copy-done
  1.9 0.0 copy-start.3
  1.9 0.9 copy-done.3
  2.8 0.0 copy-start.4
  2.8 0.7 copy-done.4
  3.5 2.6 %project.1 = (bf16[256,256]{1,0:T(8,128)(2,1)S(1)}, bf16[16,256]{1,0:T(8,128)(2,1)S(1)}) custom-call(bf16[264,5120]{1,0:T(8,128)(2,1)} %hidden_ref.1, bf16[5120,128]{1,0:T(8,128)(2,1)S(1)} %copy-done, bf16[264,128]{1,0:T(8,128)(2,1)S(1)} %copy-done.3, s32[1,256]{1,0:T(1,128)S(1)} %copy-done.4), custom_call_target="tpu_custom_call" | custom-call | tf_op jit(solution)/shard_map/project/pallas_call | solution.py:221
  6.2 8.3 %collective-permute-start = (bf16[256,256]{1,0:T(8,128)(2,1)S(1)}, bf16[256,256]{1,0:T(8,128)(2,1)S(1)}, u32[]{:S(2)}, u32[]{:S(2)}) collective-permute-start(bf16[256,256]{1,0:T(8,128)(2,1)S(1)} %get-tuple-element.9), channel_id=1, source_target_pairs={{0,16},{4,20},{8,24},{12,28},{16,0},{20,4},{24,8},{28,12},{1,17},{... | collective-permute-start | bytes 393224 | tf_op jit(solution)/shard_map/ppermute | solution.py:267
  14.4 2.5 %collective-permute-start.1 = (bf16[256,256]{1,0:T(8,128)(2,1)S(1)}, bf16[256,256]{1,0:T(8,128)(2,1)S(1)}, u32[]{:S(2)}, u32[]{:S(2)}) collective-permute-start(bf16[256,256]{1,0:T(8,128)(2,1)S(1)} %get-tuple-element.9), channel_id=1, source_target_pairs={{0,12},{4,16},{8,20},{12,24},{16,28},{20,0},{24,4},{28,8},{1,13},{... | collective-permute-start | bytes 393224 | tf_op jit(solution)/shard_map/ppermute | solution.py:267
  17.0 2.4 collective-permute-start.2
  19.4 3.2 %collective-permute-start.3 = (bf16[256,256]{1,0:T(8,128)(2,1)S(1)}, bf16[256,256]{1,0:T(8,128)(2,1)S(1)}, u32[]{:S(2)}, u32[]{:S(2)}) collective-permute-start(bf16[256,256]{1,0:T(8,128)(2,1)S(1)} %get-tuple-element.9), channel_id=1, source_target_pairs={{0,4},{4,8},{8,12},{12,16},{16,20},{20,24},{24,28},{28,0},{1,5},{5... | collective-permute-start | bytes 393224 | tf_op jit(solution)/shard_map/ppermute | solution.py:267
  22.6 0.0 collective-permute-done
  22.7 4.1 %collective-permute-done.1 = bf16[256,256]{1,0:T(8,128)(2,1)S(1)} collective-permute-done((bf16[256,256]{1,0:T(8,128)(2,1)S(1)}, bf16[256,256]{1,0:T(8,128)(2,1)S(1)}, u32[]{:S(2)}, u32[]{:S(2)}) %collective-permute-start.1) | collective-permute-done | bytes 131104 | tf_op jit(solution)/shard_map/ppermute | solution.py:267
  26.8 0.0 slice-start
  26.8 0.0 slice-start.1
  26.8 0.0 copy-start.1
  26.9 0.0 copy-start.2
  26.9 0.0 copy-start.5
  26.9 5.8 %collective-permute-done.2 = bf16[256,256]{1,0:T(8,128)(2,1)S(1)} collective-permute-done((bf16[256,256]{1,0:T(8,128)(2,1)S(1)}, bf16[256,256]{1,0:T(8,128)(2,1)S(1)}, u32[]{:S(2)}, u32[]{:S(2)}) %collective-permute-start.2) | collective-permute-done | bytes 131104 | tf_op jit(solution)/shard_map/ppermute | solution.py:267
  32.7 4.9 %collective-permute-done.3 = bf16[256,256]{1,0:T(8,128)(2,1)S(1)} collective-permute-done((bf16[256,256]{1,0:T(8,128)(2,1)S(1)}, bf16[256,256]{1,0:T(8,128)(2,1)S(1)}, u32[]{:S(2)}, u32[]{:S(2)}) %collective-permute-start.3) | collective-permute-done | bytes 131104 | tf_op jit(solution)/shard_map/ppermute | solution.py:267
  37.7 1.3 broadcast_select_fusion
  39.0 2.7 %collective-permute-start.4 = (bf16[1024,256]{1,0:T(8,128)(2,1)}, bf16[1024,256]{1,0:T(8,128)(2,1)S(1)}, u32[]{:S(2)}, u32[]{:S(2)}) collective-permute-start(bf16[1024,256]{1,0:T(8,128)(2,1)} %get-tuple-element.15), channel_id=1, source_target_pairs={{0,1},{1,2},{2,3},{3,0},{4,5},{5,6},{6,7},{7,4},{8,9},{9,10},{10,1... | collective-permute-start | bytes 1572872 | tf_op jit(solution)/shard_map/ppermute | solution.py:267
  41.7 4.4 %collective-permute-start.5 = (bf16[1024,256]{1,0:T(8,128)(2,1)}, bf16[1024,256]{1,0:T(8,128)(2,1)S(1)}, u32[]{:S(2)}, u32[]{:S(2)}) collective-permute-start(bf16[1024,256]{1,0:T(8,128)(2,1)} %get-tuple-element.14), channel_id=1, source_target_pairs={{0,2},{1,3},{2,0},{3,1},{4,6},{5,7},{6,4},{7,5},{8,10},{9,11},{10,... | collective-permute-start | bytes 1572872 | tf_op jit(solution)/shard_map/ppermute | solution.py:267
  46.1 3.1 %collective-permute-start.6 = (bf16[1024,256]{1,0:T(8,128)(2,1)}, bf16[1024,256]{1,0:T(8,128)(2,1)}, u32[]{:S(2)}, u32[]{:S(2)}) collective-permute-start(bf16[1024,256]{1,0:T(8,128)(2,1)} %get-tuple-element.13), channel_id=1, source_target_pairs={{0,3},{1,0},{2,1},{3,2},{4,7},{5,4},{6,5},{7,6},{8,11},{9,8},{10,9... | collective-permute-start | bytes 1572872 | tf_op jit(solution)/shard_map/ppermute | solution.py:267
  49.1 0.7 broadcast_in_dim.4
  49.9 6.3 %all-to-all-start = ((bf16[32,16,256]{2,1,0:T(8,128)(2,1)}), bf16[32,16,256]{2,1,0:T(8,128)(2,1)S(1)}, u32[]{:S(2)}, u32[]{:S(2)}) async-start(bf16[32,16,256]{2,1,0:T(8,128)(2,1)} %broadcast_in_dim.4), calls=%async_computation | async-start | bytes 524288 | tf_op jit(solution)/shard_map/all_to_all | solution.py:283
  56.2 0.0 slice-done
  56.2 0.0 slice-done.1
  56.2 0.1 pad_add_fusion.place_ref
  56.3 15.3 %all-to-all-done = bf16[32,16,256]{2,1,0:T(8,128)(2,1)S(1)} async-done(((bf16[32,16,256]{2,1,0:T(8,128)(2,1)}), bf16[32,16,256]{2,1,0:T(8,128)(2,1)S(1)}, u32[]{:S(2)}, u32[]{:S(2)}) %all-to-all-start) | async-done | bytes 262176 | tf_op jit(solution)/shard_map/all_to_all | solution.py:283
  71.6 0.0 collective-permute-done.4.kv1_ref
  71.6 0.0 collective-permute-done.5.kv2_ref
  71.6 0.0 collective-permute-done.6.kv3_ref
  71.6 0.0 copy-done.1
  71.6 0.0 copy-done.2
  71.6 0.0 copy-done.5
  71.6 6.9 %attend.1 = (bf16[264,1024]{1,0:T(8,128)(2,1)}, bf16[64,128]{1,0:T(8,128)(2,1)S(1)}, bf16[4,1344,128]{2,1,0:T(8,128)(2,1)}) custom-call(s32[2]{0:T(128)S(1)} %pad_add_fusion.place_ref, bf16[512,256]{1,0:T(8,128)(2,1)S(1)} %bitcast.25, s32[1,256]{1,0:T(1,128)S(1)} %copy-done.5, bf16[264,1024]{1,0:T(8,128)(2,1)S(1)} %copy-done.1, ...), custom_call_target="tpu_custom_call" | custom-call | tf_op jit(solution)/shard_map/attend/pallas_call | solution.py:240
  78.6 13.3 %all-to-all-start.1 = ((bf16[4,1344,128]{2,1,0:T(8,128)(2,1)}), bf16[4,1344,128]{2,1,0:T(8,128)(2,1)S(1)}, u32[]{:S(2)}, u32[]{:S(2)}) async-start(bf16[4,1344,128]{2,1,0:T(8,128)(2,1)} %get-tuple-element.11), calls=%async_computation.1 | async-start | bytes 2752512 | tf_op jit(solution)/shard_map/all_to_all | solution.py:298
  91.9 17.9 %all-to-all-done.1 = bf16[4,1344,128]{2,1,0:T(8,128)(2,1)S(1)} async-done(((bf16[4,1344,128]{2,1,0:T(8,128)(2,1)}), bf16[4,1344,128]{2,1,0:T(8,128)(2,1)S(1)}, u32[]{:S(2)}, u32[]{:S(2)}) %all-to-all-start.1) | async-done | bytes 1376288 | tf_op jit(solution)/shard_map/all_to_all | solution.py:298
  109.8 0.4 reduce_sum.45
  110.3 0.4 fusion.4
  110.7 0.9 pad_maximum_fusion
  111.5 35.9 %all-to-all-start.2 = ((bf16[8,264,128]{2,1,0:T(8,128)(2,1)}), bf16[8,264,128]{2,1,0:T(8,128)(2,1)S(1)}, u32[]{:S(2)}, u32[]{:S(2)}) async-start(bf16[8,264,128]{2,1,0:T(8,128)(2,1)} %pad_maximum_fusion), calls=%async_computation.2 | async-start | bytes 1081344 | tf_op jit(solution)/shard_map/all_to_all | solution.py:307
  147.4 14.2 %all-to-all-done.2 = bf16[8,264,128]{2,1,0:T(8,128)(2,1)S(1)} async-done(((bf16[8,264,128]{2,1,0:T(8,128)(2,1)}), bf16[8,264,128]{2,1,0:T(8,128)(2,1)S(1)}, u32[]{:S(2)}, u32[]{:S(2)}) %all-to-all-start.2) | async-done | bytes 540704 | tf_op jit(solution)/shard_map/all_to_all | solution.py:307
  161.7 0.1 reduce_sum.46
  161.7 0.0 copy-start.6
  161.8 4.3 %convolution_bitcast_fusion = f32[5120,128]{0,1:T(8,128)} fusion(bf16[264,128]{1,0:T(8,128)(2,1)S(1)} %reduce_sum.46, bf16[264,5120]{1,0:T(8,128)(2,1)} %hidden_ref.1), kind=kOutput, calls=%fused_computation | convolution fusion | flops 346030080 | bytes 5392384 | tf_op jit(solution)/shard_map/dot_general | solution.py:22
  166.1 3.2 %copy.11 = f32[5120,128]{1,0:T(8,128)} copy(f32[5120,128]{0,1:T(8,128)} %convolution_bitcast_fusion) | data formatting | bytes 5242880 | tf_op jit(solution)/shard_map/dot_general | solution.py:22
  169.3 1.4 fusion.1
  170.7 1.9 collective-permute-start.7
  172.6 2.1 collective-permute-done.7
  174.7 2.3 fusion
  177.0 3.9 %all-to-all-start.3 = ((bf16[32,80,128]{2,1,0:T(8,128)(2,1)}), bf16[32,80,128]{2,1,0:T(8,128)(2,1)S(1)}, u32[]{:S(2)}, u32[]{:S(2)}) async-start(bf16[32,80,128]{2,1,0:T(8,128)(2,1)} %fusion), calls=%async_computation.3 | async-start | bytes 1310720 | tf_op jit(solution)/shard_map/all_to_all | solution.py:314
  180.9 0.0 copy-done.7
  180.9 0.6 dynamic_slice.20
  183.5 0.0 copy-done.6
  183.5 0.0 slice-start.2
  183.5 16.9 %all-to-all-done.3 = bf16[32,80,128]{2,1,0:T(8,128)(2,1)S(1)} async-done(((bf16[32,80,128]{2,1,0:T(8,128)(2,1)}), bf16[32,80,128]{2,1,0:T(8,128)(2,1)S(1)}, u32[]{:S(2)}, u32[]{:S(2)}) %all-to-all-start.3) | async-done | bytes 655392 | tf_op jit(solution)/shard_map/all_to_all | solution.py:314
  200.4 0.1 reduce_sum.47
  200.6 40.4 %all-gather = bf16[3648,128]{1,0:T(8,128)(2,1)S(1)} all-gather(bf16[152,128]{1,0:T(8,128)(2,1)S(1)} %pad_maximum_fusion.2), channel_id=2, replica_groups=mesh['z'=12,'k'=2,'y'=8,'x'=4] {'z','k'}, dimensions={0}, use_global_device_ids=true | all-gather | bytes 972800 | tf_op jit(solution)/shard_map/all_gather | solution.py:318
  241.1 0.7 convert_reduce_fusion
  241.8 0.0 slice-done.2
  241.8 0.6 pad_maximum_fusion.1
  242.5 0.6 constant_dynamic-update-slice_fusion.13
  (18 shorter events, 0.3 us)
Async XLA Ops:
  0.6 1.3 copy-start
  1.9 0.9 copy-start.3
  2.8 0.7 copy-start.4
  6.2 16.5 %collective-permute-start = (bf16[256,256]{1,0:T(8,128)(2,1)S(1)}, bf16[256,256]{1,0:T(8,128)(2,1)S(1)}, u32[]{:S(2)}, u32[]{:S(2)}) collective-permute-start(bf16[256,256]{1,0:T(8,128)(2,1)S(1)} %get-tuple-element.9), channel_id=1, source_target_pairs={{0,16},{4,20},{8,24},{12,28},{16,0},{20,4},{24,8},{28,12},{1,17},{... | collective-permute-start | bytes 393224 | tf_op jit(solution)/shard_map/ppermute | solution.py:267
  14.4 12.4 %collective-permute-start.1 = (bf16[256,256]{1,0:T(8,128)(2,1)S(1)}, bf16[256,256]{1,0:T(8,128)(2,1)S(1)}, u32[]{:S(2)}, u32[]{:S(2)}) collective-permute-start(bf16[256,256]{1,0:T(8,128)(2,1)S(1)} %get-tuple-element.9), channel_id=1, source_target_pairs={{0,12},{4,16},{8,20},{12,24},{16,28},{20,0},{24,4},{28,8},{1,13},{... | collective-permute-start | bytes 393224 | tf_op jit(solution)/shard_map/ppermute | solution.py:267
  17.0 15.7 %collective-permute-start.2 = (bf16[256,256]{1,0:T(8,128)(2,1)S(1)}, bf16[256,256]{1,0:T(8,128)(2,1)S(1)}, u32[]{:S(2)}, u32[]{:S(2)}) collective-permute-start(bf16[256,256]{1,0:T(8,128)(2,1)S(1)} %get-tuple-element.9), channel_id=1, source_target_pairs={{0,8},{4,12},{8,16},{12,20},{16,24},{20,28},{24,0},{28,4},{1,9},{5... | collective-permute-start | bytes 393224 | tf_op jit(solution)/shard_map/ppermute | solution.py:267
  19.4 18.3 %collective-permute-start.3 = (bf16[256,256]{1,0:T(8,128)(2,1)S(1)}, bf16[256,256]{1,0:T(8,128)(2,1)S(1)}, u32[]{:S(2)}, u32[]{:S(2)}) collective-permute-start(bf16[256,256]{1,0:T(8,128)(2,1)S(1)} %get-tuple-element.9), channel_id=1, source_target_pairs={{0,4},{4,8},{8,12},{12,16},{16,20},{20,24},{24,28},{28,0},{1,5},{5... | collective-permute-start | bytes 393224 | tf_op jit(solution)/shard_map/ppermute | solution.py:267
  26.8 29.4 %slice-start = ((bf16[264,1024]{1,0:T(8,128)(2,1)}), bf16[8,1024]{1,0:T(8,128)(2,1)S(1)}, s32[]{:S(2)}) async-start(bf16[264,1024]{1,0:T(8,128)(2,1)} %q_ref.1), calls=%async_computation.4 | async-start | bytes 32768 | tf_op jit(solution)/shard_map/slice | solution.py:279
  26.8 29.4 %slice-start.1 = ((bf16[264,1024]{1,0:T(8,128)(2,1)}), bf16[8,1024]{1,0:T(8,128)(2,1)S(1)}, s32[]{:S(2)}) async-start(bf16[264,1024]{1,0:T(8,128)(2,1)} %do_ref.1), calls=%async_computation.5 | async-start | bytes 32768 | tf_op jit(solution)/shard_map/slice | solution.py:280
  26.8 44.7 %copy-start.1 = (bf16[264,1024]{1,0:T(8,128)(2,1)S(1)}, bf16[264,1024]{1,0:T(8,128)(2,1)}, u32[]{:S(2)}) copy-start(bf16[264,1024]{1,0:T(8,128)(2,1)} %q_ref.1) | copy-start | bytes 1622020
  26.9 44.7 %copy-start.2 = (bf16[264,1024]{1,0:T(8,128)(2,1)S(1)}, bf16[264,1024]{1,0:T(8,128)(2,1)}, u32[]{:S(2)}) copy-start(bf16[264,1024]{1,0:T(8,128)(2,1)} %do_ref.1) | copy-start | bytes 1622020
  26.9 44.7 %copy-start.5 = (s32[1,256]{1,0:T(1,128)S(1)}, s32[1,256]{1,0:T(1,128)}, u32[]{:S(2)}) copy-start(s32[1,256]{1,0:T(1,128)} %ids_ref.3) | copy-start | bytes 3076
  39.0 32.6 %collective-permute-start.4 = (bf16[1024,256]{1,0:T(8,128)(2,1)}, bf16[1024,256]{1,0:T(8,128)(2,1)S(1)}, u32[]{:S(2)}, u32[]{:S(2)}) collective-permute-start(bf16[1024,256]{1,0:T(8,128)(2,1)} %get-tuple-element.15), channel_id=1, source_target_pairs={{0,1},{1,2},{2,3},{3,0},{4,5},{5,6},{6,7},{7,4},{8,9},{9,10},{10,1... | collective-permute-start | bytes 1572872 | tf_op jit(solution)/shard_map/ppermute | solution.py:267
  41.7 29.9 %collective-permute-start.5 = (bf16[1024,256]{1,0:T(8,128)(2,1)}, bf16[1024,256]{1,0:T(8,128)(2,1)S(1)}, u32[]{:S(2)}, u32[]{:S(2)}) collective-permute-start(bf16[1024,256]{1,0:T(8,128)(2,1)} %get-tuple-element.14), channel_id=1, source_target_pairs={{0,2},{1,3},{2,0},{3,1},{4,6},{5,7},{6,4},{7,5},{8,10},{9,11},{10,... | collective-permute-start | bytes 1572872 | tf_op jit(solution)/shard_map/ppermute | solution.py:267
  46.1 25.5 %collective-permute-start.6 = (bf16[1024,256]{1,0:T(8,128)(2,1)}, bf16[1024,256]{1,0:T(8,128)(2,1)}, u32[]{:S(2)}, u32[]{:S(2)}) collective-permute-start(bf16[1024,256]{1,0:T(8,128)(2,1)} %get-tuple-element.13), channel_id=1, source_target_pairs={{0,3},{1,0},{2,1},{3,2},{4,7},{5,4},{6,5},{7,6},{8,11},{9,8},{10,9... | collective-permute-start | bytes 1572872 | tf_op jit(solution)/shard_map/ppermute | solution.py:267
  49.9 21.7 %all-to-all-start = ((bf16[32,16,256]{2,1,0:T(8,128)(2,1)}), bf16[32,16,256]{2,1,0:T(8,128)(2,1)S(1)}, u32[]{:S(2)}, u32[]{:S(2)}) async-start(bf16[32,16,256]{2,1,0:T(8,128)(2,1)} %broadcast_in_dim.4), calls=%async_computation | async-start | bytes 524288 | tf_op jit(solution)/shard_map/all_to_all | solution.py:283
  78.6 31.3 %all-to-all-start.1 = ((bf16[4,1344,128]{2,1,0:T(8,128)(2,1)}), bf16[4,1344,128]{2,1,0:T(8,128)(2,1)S(1)}, u32[]{:S(2)}, u32[]{:S(2)}) async-start(bf16[4,1344,128]{2,1,0:T(8,128)(2,1)} %get-tuple-element.11), calls=%async_computation.1 | async-start | bytes 2752512 | tf_op jit(solution)/shard_map/all_to_all | solution.py:298
  111.5 50.1 %all-to-all-start.2 = ((bf16[8,264,128]{2,1,0:T(8,128)(2,1)}), bf16[8,264,128]{2,1,0:T(8,128)(2,1)S(1)}, u32[]{:S(2)}, u32[]{:S(2)}) async-start(bf16[8,264,128]{2,1,0:T(8,128)(2,1)} %pad_maximum_fusion), calls=%async_computation.2 | async-start | bytes 1081344 | tf_op jit(solution)/shard_map/all_to_all | solution.py:307
  161.7 21.7 %copy-start.6 = (bf16[264,128]{1,0:T(8,128)(2,1)}, bf16[264,128]{1,0:T(8,128)(2,1)S(1)}, u32[]{:S(2)}) copy-start(bf16[264,128]{1,0:T(8,128)(2,1)S(1)} %reduce_sum.46) | copy-start | bytes 202756
  169.3 11.6 %copy-start.7 = (s32[24]{0:T(128)S(1)}, s32[24]{0:T(128)}, u32[]{:S(2)}) copy-start(s32[24]{0:T(128)} %param.13) | copy-start | bytes 292
  170.7 4.0 %collective-permute-start.7 = (bf16[32,80,128]{2,1,0:T(8,128)(2,1)S(1)}, bf16[32,80,128]{2,1,0:T(8,128)(2,1)S(1)}, u32[]{:S(2)}, u32[]{:S(2)}) collective-permute-start(bf16[32,80,128]{2,1,0:T(8,128)(2,1)S(1)} %fusion.1), channel_id=1, source_target_pairs={{0,32},{32,0},{1,33},{33,1},{2,34},{34,2},{3,35},{35,3},{4,36},{36... | collective-permute-start | bytes 1966088 | tf_op jit(solution)/shard_map/ppermute | solution.py:267
  177.0 23.4 %all-to-all-start.3 = ((bf16[32,80,128]{2,1,0:T(8,128)(2,1)}), bf16[32,80,128]{2,1,0:T(8,128)(2,1)S(1)}, u32[]{:S(2)}, u32[]{:S(2)}) async-start(bf16[32,80,128]{2,1,0:T(8,128)(2,1)} %fusion), calls=%async_computation.3 | async-start | bytes 1310720 | tf_op jit(solution)/shard_map/all_to_all | solution.py:314
  183.5 58.3 %slice-start.2 = ((bf16[264,128]{1,0:T(8,128)(2,1)}), bf16[256,128]{1,0:T(8,128)(2,1)S(1)}, s32[]{:S(2)}) async-start(bf16[264,128]{1,0:T(8,128)(2,1)} %copy-done.6), calls=%async_computation.6 | async-start | bytes 131072 | tf_op jit(solution)/shard_map/slice | solution.py:328

commit v2 on v1

--- a/solution.py
+++ b/solution.py
@@ -16,6 +16,8 @@
 
 NZ, NK, NY, NX = 12, 2, 8, 4
 MAX_SEG = 4096
+SAFE = 40.0
+MARGIN = 1.02
 
 
 def dot(a, b, dims):
@@ -30,7 +32,9 @@
     ids = ids_ref[...]
     level = lax.broadcasted_iota(jnp.int32, (8, tok), 0)
     below = jnp.sum((jnp.broadcast_to(ids, (8, tok)) < level).astype(F32), axis=1, keepdims=True)
-    counts = jnp.broadcast_to(below, (8, 2 * width))
+    longest = jnp.max(jnp.sum(keys * keys, axis=1, keepdims=True)) * MARGIN
+    line = lax.broadcasted_iota(jnp.int32, (8, 1), 0)
+    counts = jnp.broadcast_to(jnp.where(line == 4, longest, below), (8, 2 * width))
     spare = jnp.concatenate([keys[tok:], values[tok:]], axis=1)
     main_ref[...] = jnp.concatenate([keys[:tok], values[:tok]], axis=1).astype(BF16)
     extra_ref[...] = jnp.concatenate([spare, counts], axis=0).astype(BF16)
@@ -85,8 +89,6 @@
         copy.start()
 
     dv_ref[...] = jnp.zeros_like(dv_ref)
-    mask_max[...] = jnp.full_like(mask_max, NEG)
-    mid_max[...] = jnp.full_like(mid_max, NEG)
     total_ref[...] = jnp.zeros_like(total_ref)
     acc_ref[...] = jnp.zeros_like(acc_ref)
 
@@ -99,6 +101,15 @@
     first = jnp.min(begin).astype(jnp.int32)
     begin = begin.astype(jnp.int32)
     in_first = begin == first
+    first_rows = jnp.concatenate([in_first] * heads, axis=1)
+    key_bound = jnp.max(extra[:, spare + 4, :])
+    ones = jnp.ones((width, width), BF16)
+    lengths = []
+    for h in range(heads):
+        part = q_ref[:tok, h * width : (h + 1) * width].astype(F32)
+        lengths.append(jnp.max(dot((part * part).astype(BF16), ones, ((1,), (0,))), axis=0, keepdims=True))
+    query_bound = jnp.max(jnp.concatenate(lengths, axis=0)) * MARGIN
+    safe = key_bound * query_bound <= SAFE * SAFE * width
 
     base = (y_at - back) * NX
     last = back * NX + x_at
@@ -140,19 +151,27 @@
     for copy in copies:
         copy.wait()
 
-    pl.when(low < last)(lambda: max_masked(low))
-    lax.fori_loop(low + 1, last, max_mid, 0)
-    max_masked(last)
-    first_rows = jnp.concatenate([in_first] * heads, axis=1)
-    top = jnp.max(mask_max[...], axis=0, keepdims=True)
-    mid_top = jnp.max(mid_max[...], axis=0, keepdims=True) * factor
-    top = jnp.where(first_rows, jnp.maximum(top, mid_top), top)
-    mask_max[...] = jnp.broadcast_to(top, mask_max.shape)
-    mid_shift[...] = jnp.broadcast_to(jnp.where(first_rows, top, BIG), mid_shift.shape)
+    def set_shift(top):
+        mask_max[...] = jnp.broadcast_to(top, mask_max.shape)
+        mid_shift[...] = jnp.broadcast_to(jnp.where(first_rows, top, BIG), mid_shift.shape)
+
+    @pl.when(safe)
+    def _():
+        set_shift(jnp.zeros((1, rows), F32))
+
+    @pl.when(jnp.logical_not(safe))
+    def _():
+        mask_max[...] = jnp.full_like(mask_max, NEG)
+        mid_max[...] = jnp.full_like(mid_max, NEG)
+        pl.when(low < last)(lambda: max_masked(low))
+        lax.fori_loop(low + 1, last, max_mid, 0)
+        max_masked(last)
+        top = jnp.max(mask_max[...], axis=0, keepdims=True)
+        mid_top = jnp.max(mid_max[...], axis=0, keepdims=True) * factor
+        set_shift(jnp.where(first_rows, jnp.maximum(top, mid_top), top))
 
     def weigh(n, shift_ref, masked):
         key_block = chunk(n, slice(0, width))
-        value_t = chunk(n, slice(width, 2 * width)).astype(F32).T.astype(BF16)
         for h in range(heads):
             at = slice(h * tok, (h + 1) * tok)
             s = scores(key_block, h) * factor
@@ -160,14 +179,13 @@
                 s = s + bias_ref[...]
             p = jnp.exp2(s - shift_ref[0:1, at])
             total_ref[:, at] += jnp.sum(fold(p), axis=0)
-            p = p.astype(BF16)
-            p_ref[n - x_at, :, at] = p
-            acc_ref[:, at] += dot(value_t, p, ((1,), (0,)))
+            p_ref[n - low, :, at] = p.astype(BF16)
 
     def weigh_mid(n, carry):
         weigh(n, mid_shift, False)
         return carry
 
+    set_bias(last)
     weigh(last, mask_max, True)
     lax.fori_loop(low + 1, last, weigh_mid, 0)
 
@@ -175,6 +193,18 @@
     def _():
         set_bias(low)
         weigh(low, mask_max, True)
+
+    p_ref[last - low + 1] = jnp.zeros((tok, rows), BF16)
+
+    def gather_values(j, carry):
+        near = low + 2 * j
+        block = [chunk(n, slice(width, 2 * width)) for n in (near, jnp.minimum(near + 1, last))]
+        value_t = jnp.concatenate([b.astype(F32).T.astype(BF16) for b in block], axis=1)
+        weights = p_ref[pl.ds(2 * j, 2)].reshape(2 * tok, rows)
+        acc_ref[...] += dot(value_t, weights, ((1,), (0,)))
+        return carry
+
+    lax.fori_loop(0, lax.div(last - low + 2, 2), gather_values, 0)
 
     share = 1.0 / jnp.sum(total_ref[...], axis=0, keepdims=True)
     for h in range(heads):
@@ -185,7 +215,7 @@
         grad_ref[at, :] = (do_ref[:tok, part].astype(F32) * head_share.T).astype(BF16)
 
     def spread(n, carry):
-        got = dot(p_ref[n - x_at], grad_ref[...], ((1,), (0,)))
+        got = dot(p_ref[n - low], grad_ref[...], ((1,), (0,)))
         column = lax.rem(n, NX)
         row = lax.div(n, NX)
         dv_ref[column, pl.ds(pl.multiple_of(row * tok, tok), tok), :] = got.astype(BF16)
@@ -208,6 +238,21 @@
     got = dot(p, dos_ref[...], ((1,), (0,))).reshape(NY, NX, spare, width)
     for xx in range(NX):
         dv_ref[xx, (back + 1) * tok :, :] = got[:, xx].reshape(NY * spare, width).astype(BF16)
+
+
+def combine_kernel(place_ref, got_ref, hidden_ref, home_ref, mine_ref, other_ref):
+    home = jnp.sum(got_ref[...].astype(F32), axis=0)
+    home_ref[...] = home.astype(BF16)
+    home = home.astype(BF16)
+    first = place_ref[2] == 0
+    half = mine_ref.shape[1]
+    step = 4
+    for c in range(0, NY * NX, step):
+        columns = slice(2 * half * c, 2 * half * (c + step))
+        term = dot(hidden_ref[:, columns], home, ((0,), (0,)))
+        term = term.reshape(step, NK, half, home.shape[1])
+        mine_ref[c : c + step] = jnp.where(first, term[:, 0], term[:, 1])
+        other_ref[c : c + step] = jnp.where(first, term[:, 1], term[:, 0])
 
 
 VMEM = pl.BlockSpec(memory_space=pltpu.VMEM)
@@ -253,7 +298,7 @@
             pltpu.VMEM((8, rows), F32),
             pltpu.VMEM((8, rows), F32),
             pltpu.VMEM((width, rows), F32),
-            pltpu.VMEM((back * NX + 1, tok, rows), BF16),
+            pltpu.VMEM((back * NX + 2, tok, rows), BF16),
             pltpu.VMEM((rows, width), BF16),
             pltpu.VMEM((NX, (back + 1) * tok, 2 * width), BF16),
             pltpu.SemaphoreType.DMA((NX,)),
@@ -261,6 +306,20 @@
         compiler_params=LIMIT,
         name="attend",
     )(place, extra, segment_ids, queries, attn_grad, spare_q, spare_do, *pieces)
+
+
+def combine(place, got, hidden):
+    share = hidden.shape[1] // (NY * NX * NK)
+    width = got.shape[2]
+    part = jax.ShapeDtypeStruct((NY * NX, share, width), F32)
+    return pl.pallas_call(
+        combine_kernel,
+        out_shape=(jax.ShapeDtypeStruct(got.shape[1:], BF16), part, part),
+        in_specs=[SMEM, VMEM, VMEM],
+        out_specs=(VMEM, VMEM, VMEM),
+        compiler_params=LIMIT,
+        name="combine",
+    )(place, got, hidden)
 
 
 def shift(array, axis, size, step):
@@ -290,7 +349,7 @@
         send = jnp.where(x_at + s < NX, late, early)
         pieces.append(shift(send, "x", NX, s))
 
-    place = jnp.stack([y_at, x_at]).astype(jnp.int32)
+    place = jnp.stack([y_at, x_at, k_at]).astype(jnp.int32)
     main_out, spare_out, sums = attend(
         place, extras, segment_ids, queries, attn_grad, spare_q, spare_do, pieces, back
     )
@@ -305,12 +364,8 @@
     main_part = lax.dynamic_slice_in_dim(main_part, (back - y_at + NY) % NY, NY, 0)
     spare_part = got[(back + 1) * tok :].reshape(NY, spare, width)
     got = lax.all_to_all(jnp.concatenate([main_part, spare_part], axis=1), "y", 0, 0, tiled=True)
-    home = jnp.sum(got.astype(F32), axis=0).astype(BF16)
-
-    term = dot(hidden, home, ((0,), (0,))).reshape(NY * NX, NK, -1, width)
-    mine = lax.dynamic_index_in_dim(term, k_at, 1, keepdims=False)
-    other = lax.dynamic_index_in_dim(term, 1 - k_at, 1, keepdims=False).astype(BF16)
-    both = (mine + shift(other, "k", NK, 1).astype(F32)).astype(BF16)
+    home, mine, other = combine(place, got, hidden)
+    both = (mine + shift(other, "k", NK, 1)).astype(BF16)
     got = lax.all_to_all(both, ("y", "x"), 0, 0, tiled=True)
     share = jnp.sum(got.astype(F32), axis=0).astype(BF16)
 

time: 244 us -> 219 us (0.90)
  starting transfers between devices: 87.9 us -> 52.6 us
  blocking collectives: 40.4 us -> 74.1 us
  waiting for transfers between devices: 81.3 us -> 67.2 us
  local copies, waits for them, and re-layouts: 9.78 us -> 5.12 us
  matrix products: 4.31 us -> 0 us
    all_to_all x1 -> x0, starting transfers between devices: 35.9 us -> none  [body(): lax.all_to_all(jnp.concatenate([main_part, spare_part], axis=1), 'y', 0,...]
    all_to_all x0 -> x1, blocking collectives: none -> 29.2 us  [body(): lax.all_to_all(jnp.concatenate([main_part, spare_part], axis=1), 'y', 0,...]
    all_to_all x1 -> x0, waiting for transfers between devices: 14.2 us -> none  [body(): lax.all_to_all(jnp.concatenate([main_part, spare_part], axis=1), 'y', 0,...]
    all_gather x1, blocking collectives: 40.4 us -> 45 us  [body(): every = lax.all_gather(bundle, ('z', 'k'), axis=0)]
    dot_general x1 -> x0, matrix products: 4.31 us -> none  [dot(): return lax.dot_general(a, b, (dims, ((), ())), preferred_element_type=F32)]
    ppermute x8, starting transfers between devices: 28.5 us -> 32.7 us  [shift(): lax.ppermute(array, axis, [(i, (i + step) % size) for i in range(size)])]
    all_to_all x1, starting transfers between devices: 13.3 us -> 9.52 us  [body(): got = lax.all_to_all(sums, 'x', 0, 0, tiled=True)]
    dot_general x1 -> x0, local copies, waits for them, and re-layouts: 3.22 us -> none  [dot(): return lax.dot_general(a, b, (dims, ((), ())), preferred_element_type=F32)]
  transfers between devices with their start and end apart: 12 -> 11, of which waited for: 8 -> 7; matrix products, arithmetic and copies ran while one was open for 1% -> 1% of each run, Pallas kernels for 0% -> 0%
where the time goes in v2:
time: 219 us; the launch traced here: 218 us
  blocking collectives  74.1 us (34%)
  waiting for transfers between devices  67.2 us (31%)
  starting transfers between devices  52.6 us (24%)
  Pallas kernels  11.7 us (5%)
  local copies, waits for them, and re-layouts  5.12 us (2%)
  other arithmetic  4.61 us (2%)
  between operations  2.95 us (1%)
    all_gather x1, blocking collectives, body(): every = lax.all_gather(bundle, ('z', 'k'), axis=0)  45 us
    ppermute x8, starting transfers between devices, shift(): lax.ppermute(array, axis, [(i, (i + step) % size) for i in range(size)])  32.7 us
    all_to_all x1, blocking collectives, body(): lax.all_to_all(jnp.concatenate([main_part, spare_part], axis=1), 'y', 0,...  29.2 us
    all_to_all x1, waiting for transfers between devices, body(): got = lax.all_to_all(sums, 'x', 0, 0, tiled=True)  17.9 us
    ppermute x8, waiting for transfers between devices, shift(): lax.ppermute(array, axis, [(i, (i + step) % size) for i in range(size)])  17.6 us
    all_to_all x1, waiting for transfers between devices, body(): got = lax.all_to_all(both, ('y', 'x'), 0, 0, tiled=True)  16.4 us
    all_to_all x1, waiting for transfers between devices, body(): lax.all_to_all(jnp.broadcast_to(extra[None], (NY * NX,) + extra.shape), (...  15.3 us
    all_to_all x1, starting transfers between devices, body(): got = lax.all_to_all(sums, 'x', 0, 0, tiled=True)  9.52 us
  transfers between devices with their start and end apart: 11, of which 7 were waited for; matrix products, arithmetic and copies ran while one was open for 1% of the time, Pallas kernels for 0%

profile of v2, /device:TPU:1, one launch (start us, length us, event | category | flops | bytes accessed | tf_op | source)
XLA Modules:
  0.0 218.3 jit_solution(9218131169784169908)
XLA Ops:
  0.6 0.0 copy-start
  0.6 1.3 copy-done
  1.9 0.0 copy-start.3
  1.9 0.9 copy-done.3
  2.8 0.0 copy-start.4
  2.8 0.7 copy-done.4
  3.5 2.6 %project.1 = (bf16[256,256]{1,0:T(8,128)(2,1)S(1)}, bf16[16,256]{1,0:T(8,128)(2,1)S(1)}) custom-call(bf16[264,5120]{1,0:T(8,128)(2,1)} %hidden_ref.3, bf16[5120,128]{1,0:T(8,128)(2,1)S(1)} %copy-done, bf16[264,128]{1,0:T(8,128)(2,1)S(1)} %copy-done.3, s32[1,256]{1,0:T(1,128)S(1)} %copy-done.4), custom_call_target="tpu_custom_call" | custom-call | tf_op jit(solution)/shard_map/project/pallas_call | solution.py:266
  6.2 8.3 %collective-permute-start = (bf16[256,256]{1,0:T(8,128)(2,1)S(1)}, bf16[256,256]{1,0:T(8,128)(2,1)S(1)}, u32[]{:S(2)}, u32[]{:S(2)}) collective-permute-start(bf16[256,256]{1,0:T(8,128)(2,1)S(1)} %get-tuple-element.12), channel_id=1, source_target_pairs={{0,16},{4,20},{8,24},{12,28},{16,0},{20,4},{24,8},{28,12},{1,17},{... | collective-permute-start | bytes 393224 | tf_op jit(solution)/shard_map/ppermute | solution.py:326
  14.4 2.5 %collective-permute-start.1 = (bf16[256,256]{1,0:T(8,128)(2,1)S(1)}, bf16[256,256]{1,0:T(8,128)(2,1)S(1)}, u32[]{:S(2)}, u32[]{:S(2)}) collective-permute-start(bf16[256,256]{1,0:T(8,128)(2,1)S(1)} %get-tuple-element.12), channel_id=1, source_target_pairs={{0,12},{4,16},{8,20},{12,24},{16,28},{20,0},{24,4},{28,8},{1,13},{... | collective-permute-start | bytes 393224 | tf_op jit(solution)/shard_map/ppermute | solution.py:326
  17.0 2.4 %collective-permute-start.2 = (bf16[256,256]{1,0:T(8,128)(2,1)S(1)}, bf16[256,256]{1,0:T(8,128)(2,1)S(1)}, u32[]{:S(2)}, u32[]{:S(2)}) collective-permute-start(bf16[256,256]{1,0:T(8,128)(2,1)S(1)} %get-tuple-element.12), channel_id=1, source_target_pairs={{0,8},{4,12},{8,16},{12,20},{16,24},{20,28},{24,0},{28,4},{1,9},{5... | collective-permute-start | bytes 393224 | tf_op jit(solution)/shard_map/ppermute | solution.py:326
  19.4 3.2 %collective-permute-start.3 = (bf16[256,256]{1,0:T(8,128)(2,1)S(1)}, bf16[256,256]{1,0:T(8,128)(2,1)S(1)}, u32[]{:S(2)}, u32[]{:S(2)}) collective-permute-start(bf16[256,256]{1,0:T(8,128)(2,1)S(1)} %get-tuple-element.12), channel_id=1, source_target_pairs={{0,4},{4,8},{8,12},{12,16},{16,20},{20,24},{24,28},{28,0},{1,5},{5... | collective-permute-start | bytes 393224 | tf_op jit(solution)/shard_map/ppermute | solution.py:326
  22.6 0.0 collective-permute-done
  22.7 4.1 %collective-permute-done.1 = bf16[256,256]{1,0:T(8,128)(2,1)S(1)} collective-permute-done((bf16[256,256]{1,0:T(8,128)(2,1)S(1)}, bf16[256,256]{1,0:T(8,128)(2,1)S(1)}, u32[]{:S(2)}, u32[]{:S(2)}) %collective-permute-start.1) | collective-permute-done | bytes 131104 | tf_op jit(solution)/shard_map/ppermute | solution.py:326
  26.8 5.9 %collective-permute-done.2 = bf16[256,256]{1,0:T(8,128)(2,1)S(1)} collective-permute-done((bf16[256,256]{1,0:T(8,128)(2,1)S(1)}, bf16[256,256]{1,0:T(8,128)(2,1)S(1)}, u32[]{:S(2)}, u32[]{:S(2)}) %collective-permute-start.2) | collective-permute-done | bytes 131104 | tf_op jit(solution)/shard_map/ppermute | solution.py:326
  32.7 4.9 %collective-permute-done.3 = bf16[256,256]{1,0:T(8,128)(2,1)S(1)} collective-permute-done((bf16[256,256]{1,0:T(8,128)(2,1)S(1)}, bf16[256,256]{1,0:T(8,128)(2,1)S(1)}, u32[]{:S(2)}, u32[]{:S(2)}) %collective-permute-start.3) | collective-permute-done | bytes 131104 | tf_op jit(solution)/shard_map/ppermute | solution.py:326
  37.7 0.0 slice-start
  37.7 0.0 slice-start.1
  37.7 0.0 copy-start.1
  37.8 0.0 copy-start.2
  37.8 0.0 copy-start.5
  37.8 1.3 broadcast_select_fusion
  39.1 2.7 %collective-permute-start.4 = (bf16[1024,256]{1,0:T(8,128)(2,1)}, bf16[1024,256]{1,0:T(8,128)(2,1)S(1)}, u32[]{:S(2)}, u32[]{:S(2)}) collective-permute-start(bf16[1024,256]{1,0:T(8,128)(2,1)} %get-tuple-element.21), channel_id=1, source_target_pairs={{0,1},{1,2},{2,3},{3,0},{4,5},{5,6},{6,7},{7,4},{8,9},{9,10},{10,1... | collective-permute-start | bytes 1572872 | tf_op jit(solution)/shard_map/ppermute | solution.py:326
  41.7 4.4 %collective-permute-start.5 = (bf16[1024,256]{1,0:T(8,128)(2,1)}, bf16[1024,256]{1,0:T(8,128)(2,1)S(1)}, u32[]{:S(2)}, u32[]{:S(2)}) collective-permute-start(bf16[1024,256]{1,0:T(8,128)(2,1)} %get-tuple-element.20), channel_id=1, source_target_pairs={{0,2},{1,3},{2,0},{3,1},{4,6},{5,7},{6,4},{7,5},{8,10},{9,11},{10,... | collective-permute-start | bytes 1572872 | tf_op jit(solution)/shard_map/ppermute | solution.py:326
  46.1 3.1 %collective-permute-start.6 = (bf16[1024,256]{1,0:T(8,128)(2,1)}, bf16[1024,256]{1,0:T(8,128)(2,1)}, u32[]{:S(2)}, u32[]{:S(2)}) collective-permute-start(bf16[1024,256]{1,0:T(8,128)(2,1)} %get-tuple-element.19), channel_id=1, source_target_pairs={{0,3},{1,0},{2,1},{3,2},{4,7},{5,4},{6,5},{7,6},{8,11},{9,8},{10,9... | collective-permute-start | bytes 1572872 | tf_op jit(solution)/shard_map/ppermute | solution.py:326
  49.2 0.7 broadcast_in_dim.4
  49.9 6.3 %all-to-all-start = ((bf16[32,16,256]{2,1,0:T(8,128)(2,1)}), bf16[32,16,256]{2,1,0:T(8,128)(2,1)S(1)}, u32[]{:S(2)}, u32[]{:S(2)}) async-start(bf16[32,16,256]{2,1,0:T(8,128)(2,1)} %broadcast_in_dim.4), calls=%async_computation | async-start | bytes 524288 | tf_op jit(solution)/shard_map/all_to_all | solution.py:342
  56.2 0.0 slice-done
  56.2 0.0 slice-done.1
  56.3 0.1 pad_add_fusion.place_ref
  56.4 15.3 %all-to-all-done = bf16[32,16,256]{2,1,0:T(8,128)(2,1)S(1)} async-done(((bf16[32,16,256]{2,1,0:T(8,128)(2,1)}), bf16[32,16,256]{2,1,0:T(8,128)(2,1)S(1)}, u32[]{:S(2)}, u32[]{:S(2)}) %all-to-all-start) | async-done | bytes 262176 | tf_op jit(solution)/shard_map/all_to_all | solution.py:342
  71.6 0.0 collective-permute-done.4.kv1_ref
  71.6 0.0 collective-permute-done.5.kv2_ref
  71.6 0.0 collective-permute-done.6.kv3_ref
  71.6 0.0 copy-done.1
  71.7 0.0 copy-done.2
  71.7 0.0 copy-done.5
  71.7 6.0 %attend.1 = (bf16[264,1024]{1,0:T(8,128)(2,1)}, bf16[64,128]{1,0:T(8,128)(2,1)S(1)}, bf16[4,1344,128]{2,1,0:T(8,128)(2,1)}) custom-call(s32[3]{0:T(128)S(1)} %pad_add_fusion.place_ref, bf16[512,256]{1,0:T(8,128)(2,1)S(1)} %bitcast.15, s32[1,256]{1,0:T(1,128)S(1)} %copy-done.5, bf16[264,1024]{1,0:T(8,128)(2,1)S(1)} %copy-done.1, ...), custom_call_target="tpu_custom_call" | custom-call | tf_op jit(solution)/shard_map/attend/pallas_call | solution.py:285
  77.7 9.5 %all-to-all-start.1 = ((bf16[4,1344,128]{2,1,0:T(8,128)(2,1)}), bf16[4,1344,128]{2,1,0:T(8,128)(2,1)S(1)}, u32[]{:S(2)}, u32[]{:S(2)}) async-start(bf16[4,1344,128]{2,1,0:T(8,128)(2,1)} %get-tuple-element.14), calls=%async_computation.1 | async-start | bytes 2752512 | tf_op jit(solution)/shard_map/all_to_all | solution.py:357
  87.2 17.9 %all-to-all-done.1 = bf16[4,1344,128]{2,1,0:T(8,128)(2,1)S(1)} async-done(((bf16[4,1344,128]{2,1,0:T(8,128)(2,1)}), bf16[4,1344,128]{2,1,0:T(8,128)(2,1)S(1)}, u32[]{:S(2)}, u32[]{:S(2)}) %all-to-all-start.1) | async-done | bytes 1376288 | tf_op jit(solution)/shard_map/all_to_all | solution.py:357
  105.2 0.4 reduce_sum.33
  105.6 0.4 fusion.2
  106.1 29.2 %all_to_all.20.got_ref = bf16[8,264,128]{2,1,0:T(8,128)(2,1)S(1)} all-to-all(bf16[8,264,128]{2,1,0:T(8,128)(2,1)S(1)} %pad_maximum_fusion), channel_id=1, replica_groups=mesh['z'=12,'k'=2,'y'=8,'x'=4] {'y'}, dimensions={0} | all-to-all | bytes 1081344 | tf_op jit(solution)/shard_map/all_to_all | solution.py:366
  135.2 3.1 %combine.1 = (bf16[264,128]{1,0:T(8,128)(2,1)S(1)}, f32[32,80,128]{2,1,0:T(8,128)S(1)}, f32[32,80,128]{2,1,0:T(8,128)S(1)}) custom-call(s32[3]{0:T(128)S(1)} %pad_add_fusion.place_ref, bf16[8,264,128]{2,1,0:T(8,128)(2,1)S(1)} %all_to_all.20.got_ref, bf16[264,5120]{1,0:T(8,128)(2,1)} %hidden_ref.3), custom_call_target="tpu_custom_call" | custom-call | tf_op jit(solution)/shard_map/combine/pallas_call | solution.py:315
  138.3 6.2 %collective-permute-start.7 = (f32[32,80,128]{2,1,0:T(8,128)S(1)}, f32[32,80,128]{2,1,0:T(8,128)S(1)}, u32[]{:S(2)}, u32[]{:S(2)}) collective-permute-start(f32[32,80,128]{2,1,0:T(8,128)S(1)} %get-tuple-element.16), channel_id=1, source_target_pairs={{0,32},{32,0},{1,33},{33,1},{2,34},{34,2},{3,35},{35,3},{4,36},{36... | collective-permute-start | bytes 3932168 | tf_op jit(solution)/shard_map/ppermute | solution.py:326
  144.5 2.6 %collective-permute-done.7 = f32[32,80,128]{2,1,0:T(8,128)S(1)} collective-permute-done((f32[32,80,128]{2,1,0:T(8,128)S(1)}, f32[32,80,128]{2,1,0:T(8,128)S(1)}, u32[]{:S(2)}, u32[]{:S(2)}) %collective-permute-start.7) | collective-permute-done | bytes 1310752 | tf_op jit(solution)/shard_map/ppermute | solution.py:326
  147.1 1.0 add_convert_fusion
  148.1 0.0 copy-start.6
  148.1 4.0 %all-to-all-start.3 = ((bf16[32,80,128]{2,1,0:T(8,128)(2,1)}), bf16[32,80,128]{2,1,0:T(8,128)(2,1)S(1)}, u32[]{:S(2)}, u32[]{:S(2)}) async-start(bf16[32,80,128]{2,1,0:T(8,128)(2,1)} %add_convert_fusion), calls=%async_computation.3 | async-start | bytes 1310720 | tf_op jit(solution)/shard_map/all_to_all | solution.py:369
  152.2 0.0 copy-done.6
  152.2 0.6 dynamic_slice.11
  154.7 16.4 %all-to-all-done.3 = bf16[32,80,128]{2,1,0:T(8,128)(2,1)S(1)} async-done(((bf16[32,80,128]{2,1,0:T(8,128)(2,1)}), bf16[32,80,128]{2,1,0:T(8,128)(2,1)S(1)}, u32[]{:S(2)}, u32[]{:S(2)}) %all-to-all-start.3) | async-done | bytes 655392 | tf_op jit(solution)/shard_map/all_to_all | solution.py:369
  171.2 0.1 reduce_sum.34
  171.3 45.0 %all-gather = bf16[3648,128]{1,0:T(8,128)(2,1)S(1)} all-gather(bf16[152,128]{1,0:T(8,128)(2,1)S(1)} %pad_maximum_fusion.2), channel_id=2, replica_groups=mesh['z'=12,'k'=2,'y'=8,'x'=4] {'z','k'}, dimensions={0}, use_global_device_ids=true | all-gather | bytes 972800 | tf_op jit(solution)/shard_map/all_gather | solution.py:373
  216.4 0.7 convert_reduce_fusion
  217.1 0.6 pad_maximum_fusion.1
  217.7 0.6 constant_dynamic-update-slice_fusion.13
  (19 shorter events, 0.4 us)
Async XLA Ops:
  0.6 1.3 copy-start
  1.9 0.9 copy-start.3
  2.8 0.7 copy-start.4
  6.2 16.5 %collective-permute-start = (bf16[256,256]{1,0:T(8,128)(2,1)S(1)}, bf16[256,256]{1,0:T(8,128)(2,1)S(1)}, u32[]{:S(2)}, u32[]{:S(2)}) collective-permute-start(bf16[256,256]{1,0:T(8,128)(2,1)S(1)} %get-tuple-element.12), channel_id=1, source_target_pairs={{0,16},{4,20},{8,24},{12,28},{16,0},{20,4},{24,8},{28,12},{1,17},{... | collective-permute-start | bytes 393224 | tf_op jit(solution)/shard_map/ppermute | solution.py:326
  14.4 12.4 %collective-permute-start.1 = (bf16[256,256]{1,0:T(8,128)(2,1)S(1)}, bf16[256,256]{1,0:T(8,128)(2,1)S(1)}, u32[]{:S(2)}, u32[]{:S(2)}) collective-permute-start(bf16[256,256]{1,0:T(8,128)(2,1)S(1)} %get-tuple-element.12), channel_id=1, source_target_pairs={{0,12},{4,16},{8,20},{12,24},{16,28},{20,0},{24,4},{28,8},{1,13},{... | collective-permute-start | bytes 393224 | tf_op jit(solution)/shard_map/ppermute | solution.py:326
  17.0 15.7 %collective-permute-start.2 = (bf16[256,256]{1,0:T(8,128)(2,1)S(1)}, bf16[256,256]{1,0:T(8,128)(2,1)S(1)}, u32[]{:S(2)}, u32[]{:S(2)}) collective-permute-start(bf16[256,256]{1,0:T(8,128)(2,1)S(1)} %get-tuple-element.12), channel_id=1, source_target_pairs={{0,8},{4,12},{8,16},{12,20},{16,24},{20,28},{24,0},{28,4},{1,9},{5... | collective-permute-start | bytes 393224 | tf_op jit(solution)/shard_map/ppermute | solution.py:326
  19.4 18.3 %collective-permute-start.3 = (bf16[256,256]{1,0:T(8,128)(2,1)S(1)}, bf16[256,256]{1,0:T(8,128)(2,1)S(1)}, u32[]{:S(2)}, u32[]{:S(2)}) collective-permute-start(bf16[256,256]{1,0:T(8,128)(2,1)S(1)} %get-tuple-element.12), channel_id=1, source_target_pairs={{0,4},{4,8},{8,12},{12,16},{16,20},{20,24},{24,28},{28,0},{1,5},{5... | collective-permute-start | bytes 393224 | tf_op jit(solution)/shard_map/ppermute | solution.py:326
  37.7 18.5 %slice-start = ((bf16[264,1024]{1,0:T(8,128)(2,1)}), bf16[8,1024]{1,0:T(8,128)(2,1)S(1)}, s32[]{:S(2)}) async-start(bf16[264,1024]{1,0:T(8,128)(2,1)} %q_ref.1), calls=%async_computation.4 | async-start | bytes 32768 | tf_op jit(solution)/shard_map/slice | solution.py:338
  37.7 18.5 %slice-start.1 = ((bf16[264,1024]{1,0:T(8,128)(2,1)}), bf16[8,1024]{1,0:T(8,128)(2,1)S(1)}, s32[]{:S(2)}) async-start(bf16[264,1024]{1,0:T(8,128)(2,1)} %do_ref.1), calls=%async_computation.5 | async-start | bytes 32768 | tf_op jit(solution)/shard_map/slice | solution.py:339
  37.7 33.9 %copy-start.1 = (bf16[264,1024]{1,0:T(8,128)(2,1)S(1)}, bf16[264,1024]{1,0:T(8,128)(2,1)}, u32[]{:S(2)}) copy-start(bf16[264,1024]{1,0:T(8,128)(2,1)} %q_ref.1) | copy-start | bytes 1622020
  37.8 33.9 %copy-start.2 = (bf16[264,1024]{1,0:T(8,128)(2,1)S(1)}, bf16[264,1024]{1,0:T(8,128)(2,1)}, u32[]{:S(2)}) copy-start(bf16[264,1024]{1,0:T(8,128)(2,1)} %do_ref.1) | copy-start | bytes 1622020
  37.8 33.9 %copy-start.5 = (s32[1,256]{1,0:T(1,128)S(1)}, s32[1,256]{1,0:T(1,128)}, u32[]{:S(2)}) copy-start(s32[1,256]{1,0:T(1,128)} %ids_ref.3) | copy-start | bytes 3076
  39.1 32.6 %collective-permute-start.4 = (bf16[1024,256]{1,0:T(8,128)(2,1)}, bf16[1024,256]{1,0:T(8,128)(2,1)S(1)}, u32[]{:S(2)}, u32[]{:S(2)}) collective-permute-start(bf16[1024,256]{1,0:T(8,128)(2,1)} %get-tuple-element.21), channel_id=1, source_target_pairs={{0,1},{1,2},{2,3},{3,0},{4,5},{5,6},{6,7},{7,4},{8,9},{9,10},{10,1... | collective-permute-start | bytes 1572872 | tf_op jit(solution)/shard_map/ppermute | solution.py:326
  41.7 29.9 %collective-permute-start.5 = (bf16[1024,256]{1,0:T(8,128)(2,1)}, bf16[1024,256]{1,0:T(8,128)(2,1)S(1)}, u32[]{:S(2)}, u32[]{:S(2)}) collective-permute-start(bf16[1024,256]{1,0:T(8,128)(2,1)} %get-tuple-element.20), channel_id=1, source_target_pairs={{0,2},{1,3},{2,0},{3,1},{4,6},{5,7},{6,4},{7,5},{8,10},{9,11},{10,... | collective-permute-start | bytes 1572872 | tf_op jit(solution)/shard_map/ppermute | solution.py:326
  46.1 25.5 %collective-permute-start.6 = (bf16[1024,256]{1,0:T(8,128)(2,1)}, bf16[1024,256]{1,0:T(8,128)(2,1)}, u32[]{:S(2)}, u32[]{:S(2)}) collective-permute-start(bf16[1024,256]{1,0:T(8,128)(2,1)} %get-tuple-element.19), channel_id=1, source_target_pairs={{0,3},{1,0},{2,1},{3,2},{4,7},{5,4},{6,5},{7,6},{8,11},{9,8},{10,9... | collective-permute-start | bytes 1572872 | tf_op jit(solution)/shard_map/ppermute | solution.py:326
  49.9 21.7 %all-to-all-start = ((bf16[32,16,256]{2,1,0:T(8,128)(2,1)}), bf16[32,16,256]{2,1,0:T(8,128)(2,1)S(1)}, u32[]{:S(2)}, u32[]{:S(2)}) async-start(bf16[32,16,256]{2,1,0:T(8,128)(2,1)} %broadcast_in_dim.4), calls=%async_computation | async-start | bytes 524288 | tf_op jit(solution)/shard_map/all_to_all | solution.py:342
  77.7 27.4 %all-to-all-start.1 = ((bf16[4,1344,128]{2,1,0:T(8,128)(2,1)}), bf16[4,1344,128]{2,1,0:T(8,128)(2,1)S(1)}, u32[]{:S(2)}, u32[]{:S(2)}) async-start(bf16[4,1344,128]{2,1,0:T(8,128)(2,1)} %get-tuple-element.14), calls=%async_computation.1 | async-start | bytes 2752512 | tf_op jit(solution)/shard_map/all_to_all | solution.py:357
  138.3 8.9 %collective-permute-start.7 = (f32[32,80,128]{2,1,0:T(8,128)S(1)}, f32[32,80,128]{2,1,0:T(8,128)S(1)}, u32[]{:S(2)}, u32[]{:S(2)}) collective-permute-start(f32[32,80,128]{2,1,0:T(8,128)S(1)} %get-tuple-element.16), channel_id=1, source_target_pairs={{0,32},{32,0},{1,33},{33,1},{2,34},{34,2},{3,35},{35,3},{4,36},{36... | collective-permute-start | bytes 3932168 | tf_op jit(solution)/shard_map/ppermute | solution.py:326
  148.1 4.1 %copy-start.6 = (s32[24]{0:T(128)S(1)}, s32[24]{0:T(128)}, u32[]{:S(2)}) copy-start(s32[24]{0:T(128)} %param.13) | copy-start | bytes 292
  148.1 23.0 %all-to-all-start.3 = ((bf16[32,80,128]{2,1,0:T(8,128)(2,1)}), bf16[32,80,128]{2,1,0:T(8,128)(2,1)S(1)}, u32[]{:S(2)}, u32[]{:S(2)}) async-start(bf16[32,80,128]{2,1,0:T(8,128)(2,1)} %add_convert_fusion), calls=%async_computation.3 | async-start | bytes 1310720 | tf_op jit(solution)/shard_map/all_to_all | solution.py:369

commit v3 on v2

v3 whole, which is shorter than its diff:
```python
import functools
import math

import jax
import jax.numpy as jnp
from jax import lax
from jax.experimental import pallas as pl
from jax.experimental.pallas import tpu as pltpu
from jax.sharding import Mesh
from jax.sharding import PartitionSpec as P

BF16 = jnp.bfloat16
F32 = jnp.float32
NEG = -1e30
BIG = 1e30

NZ, NK, NY, NX = 12, 2, 8, 4
MAX_SEG = 4096
SAFE = 40.0
MARGIN = 1.02


def dot(a, b, dims):
    return lax.dot_general(a, b, (dims, ((), ())), preferred_element_type=F32)


def project_kernel(hidden_ref, weight_ref, keys_ref, ids_ref, out_ref, sum_ref):
    step = pl.program_id(0)
    part = dot(hidden_ref[...], weight_ref[...], ((1,), (0,)))

    @pl.when(step == 0)
    def _():
        sum_ref[...] = part

    @pl.when(step > 0)
    def _():
        sum_ref[...] += part

    @pl.when(step == pl.num_programs(0) - 1)
    def _():
        tok = ids_ref.shape[1]
        width = keys_ref.shape[1]
        values = sum_ref[...]
        keys = keys_ref[...].astype(F32)
        ids = jnp.broadcast_to(ids_ref[...], (8, tok))
        level = lax.broadcasted_iota(jnp.int32, (8, tok), 0)
        below = jnp.sum((ids < level).astype(F32), axis=1, keepdims=True)
        longest = jnp.max(jnp.sum(keys * keys, axis=1, keepdims=True)) * MARGIN
        line = lax.broadcasted_iota(jnp.int32, (8, 1), 0)
        counts = jnp.broadcast_to(jnp.where(line == 4, longest, below), (8, 2 * width))
        spare = jnp.concatenate([keys[tok:], values[tok:]], axis=1)
        main = jnp.concatenate([keys[:tok], values[:tok]], axis=1).astype(BF16)
        main = main.reshape(tok // 16, 16, 2 * width)
        extra = jnp.concatenate([spare, counts], axis=0).astype(BF16)
        for i in range(out_ref.shape[0]):
            out_ref[i, : tok // 16] = main
            out_ref[i, tok // 16] = extra


def select_kernel(place_ref, got_ref, one_ref, two_ref, three_ref, *, back):
    y_at, x_at = place_ref[0], place_ref[1]
    blocks = got_ref.shape[1] - 1
    for s, send_ref in enumerate((one_ref, two_ref, three_ref)):
        late = jnp.where(x_at + s + 1 < NX, 1, 0)
        for r in range(back):
            row = lax.rem(y_at - back + r + late + NY, NY)
            send_ref[r * blocks : (r + 1) * blocks] = got_ref[row, :blocks]
        for i in range(NY):
            send_ref[back * blocks + i] = got_ref[i, blocks]


def attend_kernel(
    place_ref,
    ids_ref,
    q_ref,
    do_ref,
    qs_ref,
    dos_ref,
    kv_ref,
    one_ref,
    two_ref,
    three_ref,
    out_ref,
    outs_ref,
    dv_ref,
    bias_ref,
    mask_max,
    mid_max,
    mid_shift,
    total_ref,
    acc_ref,
    p_ref,
    grad_ref,
    pack_ref,
    extra_ref,
    copy_sems,
    *,
    back,
):
    tok = ids_ref.shape[1]
    width = kv_ref.shape[3] // 2
    heads = q_ref.shape[1] // width
    rows = heads * tok
    group = NY * NX
    spare = 8
    blocks = tok // 16
    spare_heads = qs_ref.shape[0]
    factor = width ** (-0.5) * math.log2(math.e)
    y_at, x_at = place_ref[0], place_ref[1]
    own = y_at * NX + x_at

    copies = []

    def fetch(source, target):
        copies.append(pltpu.make_async_copy(source, target, copy_sems.at[len(copies)]))

    for s, piece in enumerate((one_ref, two_ref, three_ref)):
        column = lax.rem(x_at - s - 1 + NX, NX)
        start = jnp.where(column < x_at, blocks, 0)
        start = pl.multiple_of(start, blocks)
        fetch(piece.at[back * blocks :], extra_ref.at[column])
        fetch(piece.at[: back * blocks], pack_ref.at[column, pl.ds(start, back * blocks)])
    fetch(kv_ref.at[:, blocks], extra_ref.at[x_at])
    for r in range(back + 1):
        row = lax.rem(y_at - back + r + NY, NY)
        fetch(
            kv_ref.at[row, :blocks],
            pack_ref.at[x_at, r * blocks : (r + 1) * blocks],
        )
    for copy in copies:
        copy.start()

    dv_ref[...] = jnp.zeros_like(dv_ref)
    total_ref[...] = jnp.zeros_like(total_ref)
    acc_ref[...] = jnp.zeros_like(acc_ref)

    ones = jnp.ones((width, width), BF16)
    lengths = []
    for h in range(heads):
        part = q_ref[:tok, h * width : (h + 1) * width].astype(F32)
        lengths.append(jnp.max(dot((part * part).astype(BF16), ones, ((1,), (0,))), axis=0, keepdims=True))
    query_bound = jnp.max(jnp.concatenate(lengths, axis=0)) * MARGIN
    for copy in copies:
        copy.wait()

    extra = extra_ref[...].astype(F32).reshape(group, spare + 8, 2 * width)
    counts = jnp.sum(extra[:, spare:, :], axis=0)[:, :tok]
    ids = ids_ref[...]
    begin = jnp.zeros((1, tok), F32)
    for v in range(1, 4):
        begin = jnp.where(ids == v, counts[v : v + 1, :], begin)
    first = jnp.min(begin).astype(jnp.int32)
    begin = begin.astype(jnp.int32)
    in_first = begin == first
    first_rows = jnp.concatenate([in_first] * heads, axis=1)
    key_bound = jnp.max(extra[:, spare + 4, :])
    safe = key_bound * query_bound <= SAFE * SAFE * width

    base = (y_at - back) * NX
    last = back * NX + x_at
    low = jnp.maximum(first // tok - base, x_at)
    low = jnp.minimum(low, last)

    def set_bias(n):
        position = (base + n) * tok + lax.broadcasted_iota(jnp.int32, (tok, tok), 0)
        query = own * tok + lax.broadcasted_iota(jnp.int32, (tok, tok), 1)
        allowed = (position >= begin) & (position <= query)
        bias_ref[...] = jnp.where(allowed, 0.0, NEG)

    def chunk(n, part):
        start = pl.multiple_of(lax.div(n, NX) * blocks, blocks)
        return pack_ref[lax.rem(n, NX), pl.ds(start, blocks), :, part].reshape(tok, width)

    def scores(key_block, h):
        return dot(key_block, q_ref[:tok, h * width : (h + 1) * width], ((1,), (1,)))

    def fold(a):
        return a.reshape(tok // 8, 8, tok)

    def max_masked(n):
        set_bias(n)
        key_block = chunk(n, slice(0, width))
        for h in range(heads):
            at = slice(h * tok, (h + 1) * tok)
            s = scores(key_block, h) * factor + bias_ref[...]
            mask_max[:, at] = jnp.maximum(mask_max[:, at], jnp.max(fold(s), axis=0))

    def max_mid(n, carry):
        key_block = chunk(n, slice(0, width))
        for h in range(heads):
            at = slice(h * tok, (h + 1) * tok)
            s = scores(key_block, h)
            mid_max[:, at] = jnp.maximum(mid_max[:, at], jnp.max(fold(s), axis=0))
        return carry

    def set_shift(top):
        mask_max[...] = jnp.broadcast_to(top, mask_max.shape)
        mid_shift[...] = jnp.broadcast_to(jnp.where(first_rows, top, BIG), mid_shift.shape)

    @pl.when(safe)
    def _():
        set_shift(jnp.zeros((1, rows), F32))

    @pl.when(jnp.logical_not(safe))
    def _():
        mask_max[...] = jnp.full_like(mask_max, NEG)
        mid_max[...] = jnp.full_like(mid_max, NEG)
        pl.when(low < last)(lambda: max_masked(low))
        lax.fori_loop(low + 1, last, max_mid, 0)
        max_masked(last)
        top = jnp.max(mask_max[...], axis=0, keepdims=True)
        mid_top = jnp.max(mid_max[...], axis=0, keepdims=True) * factor
        set_shift(jnp.where(first_rows, jnp.maximum(top, mid_top), top))

    def weigh_masked(n):
        key_block = chunk(n, slice(0, width))
        for h in range(heads):
            at = slice(h * tok, (h + 1) * tok)
            s = scores(key_block, h) * factor + bias_ref[...]
            p = jnp.exp2(s - mask_max[0:1, at])
            total_ref[:, at] += jnp.sum(fold(p), axis=0)
            p_ref[n - low, :, at] = p.astype(BF16)

    def weigh_mid(n, count):
        key_block = [chunk(n + i, slice(0, width)) for i in range(count)]
        key_block = jnp.concatenate(key_block, axis=0)
        for h in range(heads):
            at = slice(h * tok, (h + 1) * tok)
            p = jnp.exp2(scores(key_block, h) * factor - mid_shift[0:1, at])
            total_ref[:, at] += jnp.sum(p.reshape(count * tok // 8, 8, tok), axis=0)
            p_ref[pl.ds(n - low, count), :, at] = p.astype(BF16).reshape(count, tok, tok)

    def weigh_two(j, carry):
        weigh_mid(low + 1 + 2 * j, 2)
        return carry

    set_bias(last)
    weigh_masked(last)
    mid_count = jnp.maximum(last - low - 1, 0)
    lax.fori_loop(0, lax.div(mid_count, 2), weigh_two, 0)
    pl.when(lax.rem(mid_count, 2) == 1)(lambda: weigh_mid(last - 1, 1))

    @pl.when(low < last)
    def _():
        set_bias(low)
        weigh_masked(low)

    share = 1.0 / jnp.sum(total_ref[...], axis=0, keepdims=True)
    for h in range(heads):
        at = slice(h * tok, (h + 1) * tok)
        part = slice(h * width, (h + 1) * width)
        head_share = jnp.broadcast_to(share[:, at], (width, tok)).T
        grad_ref[at, :] = (do_ref[:tok, part].astype(F32) * head_share).astype(BF16)

    def put(n, block):
        start = pl.multiple_of(lax.div(n, NX) * tok, tok)
        dv_ref[lax.rem(n, NX), pl.ds(start, tok), :] = block.astype(BF16)

    p_ref[last - low + 1] = jnp.zeros((tok, rows), BF16)

    def products(j, carry):
        near = low + 2 * j
        block = [chunk(n, slice(width, 2 * width)) for n in (near, jnp.minimum(near + 1, last))]
        value_t = jnp.concatenate([b.astype(F32).T.astype(BF16) for b in block], axis=1)
        weights = p_ref[pl.ds(2 * j, 2)].reshape(2 * tok, rows)
        acc_ref[...] += dot(value_t, weights, ((1,), (0,)))
        got = dot(weights, grad_ref[...], ((1,), (0,)))
        put(near, got[:tok])
        pl.when(near < last)(lambda: put(near + 1, got[tok:]))
        return carry

    lax.fori_loop(0, lax.div(last - low + 2, 2), products, 0)

    for h in range(heads):
        at = slice(h * tok, (h + 1) * tok)
        part = slice(h * width, (h + 1) * width)
        out_ref[:tok, part] = (acc_ref[:, at] * share[:, at]).T.astype(BF16)

    spare_total = group * spare
    block = extra[:, :spare, :].reshape(spare_total, 2 * width).astype(BF16)
    s = dot(block[:, :width], qs_ref[...], ((1,), (1,))) * factor
    line = lax.broadcasted_iota(jnp.int32, (spare_total, spare_heads), 0)
    column = lax.div(line, NY * spare)
    row = lax.rem(lax.div(line, spare), NY)
    key_at = (row * NX + column) * spare + lax.rem(line, spare)
    query_at = own * spare + lax.div(
        lax.broadcasted_iota(jnp.int32, (spare_total, spare_heads), 1), heads
    )
    allowed = key_at <= query_at
    s = jnp.where(allowed, s, NEG)
    p = jnp.where(allowed, jnp.exp2(s - jnp.max(s, axis=0, keepdims=True)), 0.0)
    p = (p * (1.0 / jnp.sum(p, axis=0, keepdims=True))).astype(BF16)
    outs_ref[...] = dot(p, block[:, width:], ((0,), (0,))).astype(BF16)
    got = dot(p, dos_ref[...], ((1,), (0,))).reshape(NX, NY * spare, width)
    dv_ref[:, (back + 1) * tok :, :] = got.astype(BF16)


def combine_kernel(place_ref, got_ref, hidden_ref, home_ref, mine_ref, other_ref):
    @pl.when(pl.program_id(0) == 0)
    def _():
        home_ref[...] = jnp.sum(got_ref[...].astype(F32), axis=0).astype(BF16)

    first = place_ref[2] == 0
    step, half, width = mine_ref.shape
    term = dot(hidden_ref[...], home_ref[...], ((0,), (0,))).reshape(step, NK, half, width)
    mine_ref[...] = jnp.where(first, term[:, 0], term[:, 1])
    other_ref[...] = jnp.where(first, term[:, 1], term[:, 0])


VMEM = pl.BlockSpec(memory_space=pltpu.VMEM)
SMEM = pl.BlockSpec(memory_space=pltpu.SMEM)
FULL = pltpu.CompilerParams(vmem_limit_bytes=60 * 1024 * 1024)
LIMIT = pltpu.CompilerParams(vmem_limit_bytes=50 * 1024 * 1024)


def whole(shape):
    return pl.BlockSpec(shape, lambda i: (0,) * len(shape))


def project(hidden, value_weight, keys, segment_ids):
    tok = segment_ids.shape[1]
    rows, model = hidden.shape
    width = keys.shape[1]
    steps = 5
    shape = (NY, tok // 16 + 1, 16, 2 * width)
    return pl.pallas_call(
        project_kernel,
        grid=(steps,),
        out_shape=jax.ShapeDtypeStruct(shape, BF16),
        in_specs=[
            pl.BlockSpec((rows, model // steps), lambda i: (0, i)),
            pl.BlockSpec((model // steps, width), lambda i: (i, 0)),
            whole(keys.shape),
            whole(segment_ids.shape),
        ],
        out_specs=whole(shape),
        scratch_shapes=[pltpu.VMEM((rows, width), F32)],
        compiler_params=FULL,
        name="project",
    )(hidden, value_weight, keys, segment_ids)


def select(place, got, back):
    blocks, lines, width = got.shape[1:]
    send = jax.ShapeDtypeStruct((back * (blocks - 1) + NY, lines, width), BF16)
    return pl.pallas_call(
        functools.partial(select_kernel, back=back),
        out_shape=(send,) * (NX - 1),
        in_specs=[SMEM, VMEM],
        out_specs=(VMEM,) * (NX - 1),
        compiler_params=LIMIT,
        name="select",
    )(place, got)


def attend(place, segment_ids, queries, attn_grad, spare_q, spare_do, pieces, back):
    tok = segment_ids.shape[1]
    width = spare_q.shape[1]
    heads = queries.shape[1] // width
    spare = queries.shape[0] - tok
    rows = heads * tok
    return pl.pallas_call(
        functools.partial(attend_kernel, back=back),
        out_shape=(
            jax.ShapeDtypeStruct(queries.shape, BF16),
            jax.ShapeDtypeStruct(spare_q.shape, BF16),
            jax.ShapeDtypeStruct((NX, (back + 1) * tok + NY * spare, width), BF16),
        ),
        in_specs=[SMEM] + [VMEM] * 5 + [pl.BlockSpec(memory_space=pl.ANY)] * NX,
        out_specs=(VMEM, VMEM, VMEM),
        scratch_shapes=[
            pltpu.VMEM((tok, tok), F32),
            pltpu.VMEM((8, rows), F32),
            pltpu.VMEM((8, rows), F32),
            pltpu.VMEM((8, rows), F32),
            pltpu.VMEM((8, rows), F32),
            pltpu.VMEM((width, rows), F32),
            pltpu.VMEM((back * NX + 2, tok, rows), BF16),
            pltpu.VMEM((rows, width), BF16),
            pltpu.VMEM((NX, (back + 1) * tok // 16, 16, 2 * width), BF16),
            pltpu.VMEM((NX, NY, 16, 2 * width), BF16),
            pltpu.SemaphoreType.DMA((2 * (NX - 1) + back + 2,)),
        ],
        compiler_params=LIMIT,
        name="attend",
    )(place, segment_ids, queries, attn_grad, spare_q, spare_do, *pieces)


def combine(place, got, hidden):
    rows, model = hidden.shape
    group = NY * NX
    half = model // (group * NK)
    width = got.shape[2]
    step = 4
    part = jax.ShapeDtypeStruct((group, half, width), F32)
    return pl.pallas_call(
        combine_kernel,
        grid=(group // step,),
        out_shape=(jax.ShapeDtypeStruct(got.shape[1:], BF16), part, part),
        in_specs=[
            SMEM,
            whole(got.shape),
            pl.BlockSpec((rows, model * step // group), lambda i: (0, i)),
        ],
        out_specs=(
            whole(got.shape[1:]),
            pl.BlockSpec((step, half, width), lambda i: (i, 0, 0)),
            pl.BlockSpec((step, half, width), lambda i: (i, 0, 0)),
        ),
        compiler_params=FULL,
        name="combine",
    )(place, got, hidden)


def shift(array, axis, size, step):
    return lax.ppermute(array, axis, [(i, (i + step) % size) for i in range(size)])


def body(hidden, value_weight, queries, keys, attn_grad, segment_ids, partner):
    tok = segment_ids.shape[1]
    spare = hidden.shape[0] - tok
    width = keys.shape[1]
    heads = queries.shape[1] // width
    back = MAX_SEG // (tok * NX)
    y_at, x_at, k_at = lax.axis_index("y"), lax.axis_index("x"), lax.axis_index("k")

    place = jnp.stack([y_at, x_at, k_at]).astype(jnp.int32)
    spare_q = queries[tok:].reshape(spare * heads, width)
    spare_do = attn_grad[tok:].reshape(spare * heads, width)

    column = project(hidden, value_weight, keys, segment_ids)
    column = lax.all_to_all(column, "y", 0, 0, tiled=True)
    pieces = [column]
    for s, send in enumerate(select(place, column, back)):
        pieces.append(shift(send, "x", NX, s + 1))
    main_out, spare_out, sums = attend(
        place, segment_ids, queries, attn_grad, spare_q, spare_do, pieces, back
    )

    got = lax.all_to_all(sums, "x", 0, 0, tiled=True)
    got = jnp.sum(got.astype(F32), axis=0).astype(BF16)
    main_part = got[: (back + 1) * tok].reshape(back + 1, tok, width)
    main_part = jnp.concatenate(
        [main_part, jnp.zeros((NY - back - 1, tok, width), BF16)], axis=0
    )
    main_part = jnp.concatenate([main_part, main_part], axis=0)
    main_part = lax.dynamic_slice_in_dim(main_part, (back - y_at + NY) % NY, NY, 0)
    spare_part = got[(back + 1) * tok :].reshape(NY, spare, width)
    got = lax.all_to_all(jnp.concatenate([main_part, spare_part], axis=1), "y", 0, 0, tiled=True)
    home, mine, other = combine(place, got, hidden)
    both = (mine + shift(other, "k", NK, 1)).astype(BF16)
    got = lax.all_to_all(both, ("y", "x"), 0, 0, tiled=True)
    share = jnp.sum(got.astype(F32), axis=0).astype(BF16)

    bundle = jnp.concatenate([share, home[tok:], spare_out], axis=0)
    every = lax.all_gather(bundle, ("z", "k"), axis=0)
    count = share.shape[0]
    weight_grad = jnp.sum(
        every[:, :count].astype(F32).reshape(NZ, NK * count, width), axis=0
    )
    my_partner = partner[lax.axis_index("z") * NK + k_at]
    traded = lax.dynamic_index_in_dim(every[:, count:], my_partner, 0, keepdims=False)
    attn_out = lax.dynamic_update_slice(
        main_out, traded[spare:].reshape(spare, heads * width), (tok, 0)
    )
    value_grad = jnp.concatenate([home[:tok], traded[:spare]], axis=0)
    return (attn_out, value_grad, weight_grad)


def solution(mesh):
    grid = Mesh(mesh.devices.reshape(NZ, NK, NY, NX), ("z", "k", "y", "x"))
    everywhere = P(("z", "k", "y", "x"), None)
    placed = (
        everywhere,
        P(),
        everywhere,
        everywhere,
        everywhere,
        P(("z", "k"), ("y", "x")),
        P(),
    )
    return jax.shard_map(
        body,
        mesh=grid,
        in_specs=placed,
        out_specs=(everywhere, everywhere, P(("y", "x"), None)),
        check_vma=False,
    )
```

time: 219 us -> 227 us (1.037)
  waiting for transfers between devices: 67.2 us -> 85.4 us
  blocking collectives: 74.1 us -> 62.8 us
  Pallas kernels: 11.7 us -> 21.7 us
  starting transfers between devices: 52.6 us -> 46.4 us
  local copies, waits for them, and re-layouts: 5.12 us -> 2.46 us
    all_to_all x1, waiting for transfers between devices: 15.3 us -> 26.3 us  [body(): column = lax.all_to_all(column, 'y', 0, 0, tiled=True)]
    all_to_all x1, blocking collectives: 29.2 us -> 19.5 us  [body(): lax.all_to_all(jnp.concatenate([main_part, spare_part], axis=1), 'y', 0,...]
    pallas_call x2 -> x3, Pallas kernels: 5.7 us -> 14.8 us  [the longest x1 7.39 us: combine(): pl.pallas_call(combine_kernel, grid=(group // step,), out_shape=(jax.Shap...]
    ppermute x8 -> x4, waiting for transfers between devices: 17.6 us -> 24.8 us  [shift(): lax.ppermute(array, axis, [(i, (i + step) % size) for i in range(size)])]
    ppermute x8 -> x4, starting transfers between devices: 32.7 us -> 26.2 us  [shift(): lax.ppermute(array, axis, [(i, (i + step) % size) for i in range(size)])]
  transfers between devices with their start and end apart: 11 -> 7, of which waited for: 7 -> 7; matrix products, arithmetic and copies ran while one was open for 1% -> 0% of each run, Pallas kernels for 0% -> 0%
where the time goes in v3:
time: 227 us; the launch traced here: 226 us
  waiting for transfers between devices  85.4 us (38%)
  blocking collectives  62.8 us (28%)
  starting transfers between devices  46.4 us (20%)
  Pallas kernels  21.7 us (10%)
  other arithmetic  4.67 us (2%)
  between operations  2.81 us (1%)
  local copies, waits for them, and re-layouts  2.46 us (1%)
    all_gather x1, blocking collectives, body(): every = lax.all_gather(bundle, ('z', 'k'), axis=0)  43.3 us
    all_to_all x1, waiting for transfers between devices, body(): column = lax.all_to_all(column, 'y', 0, 0, tiled=True)  26.3 us
    ppermute x4, starting transfers between devices, shift(): lax.ppermute(array, axis, [(i, (i + step) % size) for i in range(size)])  26.2 us
    ppermute x4, waiting for transfers between devices, shift(): lax.ppermute(array, axis, [(i, (i + step) % size) for i in range(size)])  24.8 us
    all_to_all x1, blocking collectives, body(): lax.all_to_all(jnp.concatenate([main_part, spare_part], axis=1), 'y', 0,...  19.5 us
    all_to_all x1, waiting for transfers between devices, body(): got = lax.all_to_all(sums, 'x', 0, 0, tiled=True)  17.9 us
    all_to_all x1, waiting for transfers between devices, body(): got = lax.all_to_all(both, ('y', 'x'), 0, 0, tiled=True)  16.4 us
    all_to_all x1, starting transfers between devices, body(): got = lax.all_to_all(sums, 'x', 0, 0, tiled=True)  8.43 us
  transfers between devices with their start and end apart: 7, of which 7 were waited for; matrix products, arithmetic and copies ran while one was open for 0% of the time, Pallas kernels for 0%

profile of v3, /device:TPU:1, one launch (start us, length us, event | category | flops | bytes accessed | tf_op | source)
XLA Modules:
  0.0 226.3 jit_solution(10764330960540412327)
XLA Ops:
  0.6 5.6 %project.1 = bf16[8,17,16,256]{3,2,1,0:T(8,128)(2,1)} custom-call(bf16[264,5120]{1,0:T(8,128)(2,1)} %hidden_ref.3, bf16[5120,128]{1,0:T(8,128)(2,1)} %weight_ref.1, bf16[264,128]{1,0:T(8,128)(2,1)} %keys_ref.1, s32[1,256]{1,0:T(1,128)} %ids_ref.3), custom_call_target="tpu_custom_call" | custom-call | tf_op jit(solution)/shard_map/project/pallas_call | solution.py:326
  6.2 0.0 slice-start
  6.2 0.0 slice-start.1
  6.2 0.0 copy-start
  6.2 0.0 copy-start.3
  6.2 7.8 %all-to-all-start = ((bf16[8,17,16,256]{3,2,1,0:T(8,128)(2,1)}), bf16[8,17,16,256]{3,2,1,0:T(8,128)(2,1)S(1)}, u32[]{:S(2)}, u32[]{:S(2)}) async-start(bf16[8,17,16,256]{3,2,1,0:T(8,128)(2,1)} %project.1), calls=%async_computation | async-start | bytes 2228224 | tf_op jit(solution)/shard_map/all_to_all | solution.py:432
  14.0 0.1 pad_add_fusion.place_ref
  14.1 0.0 copy-start.2
  14.1 26.3 %all-to-all-done.got_ref.kv_ref = bf16[8,17,16,256]{3,2,1,0:T(8,128)(2,1)S(1)} async-done(((bf16[8,17,16,256]{3,2,1,0:T(8,128)(2,1)}), bf16[8,17,16,256]{3,2,1,0:T(8,128)(2,1)S(1)}, u32[]{:S(2)}, u32[]{:S(2)}) %all-to-all-start) | async-done | bytes 1114144 | tf_op jit(solution)/shard_map/all_to_all | solution.py:432
  40.4 1.9 select.3
  42.2 7.4 %collective-permute-start = (bf16[72,16,256]{2,1,0:T(8,128)(2,1)}, bf16[72,16,256]{2,1,0:T(8,128)(2,1)S(1)}, u32[]{:S(2)}, u32[]{:S(2)}) collective-permute-start(bf16[72,16,256]{2,1,0:T(8,128)(2,1)} %get-tuple-element.12), channel_id=1, source_target_pairs={{0,1},{1,2},{2,3},{3,0},{4,5},{5,6},{6,7},{7,4},{8,9},{9,10},{10,1... | collective-permute-start | bytes 1769480 | tf_op jit(solution)/shard_map/ppermute | solution.py:416
  49.6 4.4 %collective-permute-start.1 = (bf16[72,16,256]{2,1,0:T(8,128)(2,1)}, bf16[72,16,256]{2,1,0:T(8,128)(2,1)S(1)}, u32[]{:S(2)}, u32[]{:S(2)}) collective-permute-start(bf16[72,16,256]{2,1,0:T(8,128)(2,1)} %get-tuple-element.13), channel_id=1, source_target_pairs={{0,2},{1,3},{2,0},{3,1},{4,6},{5,7},{6,4},{7,5},{8,10},{9,11},{10,... | collective-permute-start | bytes 1769480 | tf_op jit(solution)/shard_map/ppermute | solution.py:416
  54.0 3.1 %collective-permute-start.2 = (bf16[72,16,256]{2,1,0:T(8,128)(2,1)}, bf16[72,16,256]{2,1,0:T(8,128)(2,1)S(1)}, u32[]{:S(2)}, u32[]{:S(2)}) collective-permute-start(bf16[72,16,256]{2,1,0:T(8,128)(2,1)} %get-tuple-element.14), channel_id=1, source_target_pairs={{0,3},{1,0},{2,1},{3,2},{4,7},{5,4},{6,5},{7,6},{8,11},{9,8},{10,9... | collective-permute-start | bytes 1769480 | tf_op jit(solution)/shard_map/ppermute | solution.py:416
  57.1 0.0 slice-done
  57.1 0.0 slice-done.1
  57.1 6.7 %collective-permute-done.one_ref = bf16[72,16,256]{2,1,0:T(8,128)(2,1)S(1)} collective-permute-done((bf16[72,16,256]{2,1,0:T(8,128)(2,1)}, bf16[72,16,256]{2,1,0:T(8,128)(2,1)S(1)}, u32[]{:S(2)}, u32[]{:S(2)}) %collective-permute-start) | collective-permute-done | bytes 589856 | tf_op jit(solution)/shard_map/ppermute | solution.py:416
  63.8 14.0 %collective-permute-done.1.two_ref = bf16[72,16,256]{2,1,0:T(8,128)(2,1)S(1)} collective-permute-done((bf16[72,16,256]{2,1,0:T(8,128)(2,1)}, bf16[72,16,256]{2,1,0:T(8,128)(2,1)S(1)}, u32[]{:S(2)}, u32[]{:S(2)}) %collective-permute-start.1) | collective-permute-done | bytes 589856 | tf_op jit(solution)/shard_map/ppermute | solution.py:416
  77.9 1.3 collective-permute-done.2.three_ref
  79.1 0.0 copy-done
  79.1 0.0 copy-done.3
  79.1 0.0 copy-start.1
  79.1 1.0 copy-done.1
  80.2 6.9 %attend.1 = (bf16[264,1024]{1,0:T(8,128)(2,1)}, bf16[64,128]{1,0:T(8,128)(2,1)S(1)}, bf16[4,1344,128]{2,1,0:T(8,128)(2,1)}) custom-call(s32[3]{0:T(128)S(1)} %pad_add_fusion.place_ref, s32[1,256]{1,0:T(1,128)S(1)} %copy-done.3, bf16[264,1024]{1,0:T(8,128)(2,1)S(1)} %copy-done, bf16[264,1024]{1,0:T(8,128)(2,1)S(1)} %copy-done.1, ...), custom_call_target="tpu_custom_call" | custom-call | tf_op jit(solution)/shard_map/attend/pallas_call | solution.py:362
  87.1 0.0 copy-done.2
  87.1 8.4 %all-to-all-start.1 = ((bf16[4,1344,128]{2,1,0:T(8,128)(2,1)}), bf16[4,1344,128]{2,1,0:T(8,128)(2,1)S(1)}, u32[]{:S(2)}, u32[]{:S(2)}) async-start(bf16[4,1344,128]{2,1,0:T(8,128)(2,1)} %get-tuple-element.16), calls=%async_computation.1 | async-start | bytes 2752512 | tf_op jit(solution)/shard_map/all_to_all | solution.py:440
  95.5 17.9 %all-to-all-done.1 = bf16[4,1344,128]{2,1,0:T(8,128)(2,1)S(1)} async-done(((bf16[4,1344,128]{2,1,0:T(8,128)(2,1)}), bf16[4,1344,128]{2,1,0:T(8,128)(2,1)S(1)}, u32[]{:S(2)}, u32[]{:S(2)}) %all-to-all-start.1) | async-done | bytes 1376288 | tf_op jit(solution)/shard_map/all_to_all | solution.py:440
  113.5 0.4 reduce_sum.33
  113.9 0.4 fusion.2
  114.4 19.5 %all_to_all.20.got_ref = bf16[8,264,128]{2,1,0:T(8,128)(2,1)} all-to-all(bf16[8,264,128]{2,1,0:T(8,128)(2,1)S(1)} %pad_maximum_fusion), channel_id=1, replica_groups=mesh['z'=12,'k'=2,'y'=8,'x'=4] {'y'}, dimensions={0} | all-to-all | bytes 1081344 | tf_op jit(solution)/shard_map/all_to_all | solution.py:449
  133.8 7.4 %combine.1 = (bf16[264,128]{1,0:T(8,128)(2,1)}, f32[32,80,128]{2,1,0:T(8,128)}, f32[32,80,128]{2,1,0:T(8,128)}) custom-call(s32[3]{0:T(128)} %copy-done.2, bf16[8,264,128]{2,1,0:T(8,128)(2,1)} %all_to_all.20.got_ref, bf16[264,5120]{1,0:T(8,128)(2,1)} %hidden_ref.3), custom_call_target="tpu_custom_call" | custom-call | tf_op jit(solution)/shard_map/combine/pallas_call | solution.py:396
  141.2 11.3 %collective-permute-start.3 = (f32[32,80,128]{2,1,0:T(8,128)}, f32[32,80,128]{2,1,0:T(8,128)S(1)}, u32[]{:S(2)}, u32[]{:S(2)}) collective-permute-start(f32[32,80,128]{2,1,0:T(8,128)} %get-tuple-element.18), channel_id=1, source_target_pairs={{0,32},{32,0},{1,33},{33,1},{2,34},{34,2},{3,35},{35,3},{4,36},{36... | collective-permute-start | bytes 3932168 | tf_op jit(solution)/shard_map/ppermute | solution.py:416
  152.5 2.9 %collective-permute-done.3 = f32[32,80,128]{2,1,0:T(8,128)S(1)} collective-permute-done((f32[32,80,128]{2,1,0:T(8,128)}, f32[32,80,128]{2,1,0:T(8,128)S(1)}, u32[]{:S(2)}, u32[]{:S(2)}) %collective-permute-start.3) | collective-permute-done | bytes 1310752 | tf_op jit(solution)/shard_map/ppermute | solution.py:416
  155.4 2.3 %add_convert_fusion = bf16[32,80,128]{2,1,0:T(8,128)(2,1)} fusion(f32[32,80,128]{2,1,0:T(8,128)} %get-tuple-element.17, f32[32,80,128]{2,1,0:T(8,128)S(1)} %collective-permute-done.3), kind=kLoop, calls=%fused_computation | loop fusion | flops 655360 | bytes 3276800 | tf_op jit(solution)/shard_map/convert_element_type | solution.py:451
  157.7 0.0 copy-start.5
  157.7 0.0 copy-start.4
  157.7 4.0 %all-to-all-start.3 = ((bf16[32,80,128]{2,1,0:T(8,128)(2,1)}), bf16[32,80,128]{2,1,0:T(8,128)(2,1)S(1)}, u32[]{:S(2)}, u32[]{:S(2)}) async-start(bf16[32,80,128]{2,1,0:T(8,128)(2,1)} %add_convert_fusion), calls=%async_computation.3 | async-start | bytes 1310720 | tf_op jit(solution)/shard_map/all_to_all | solution.py:452
  161.8 0.0 copy-done.5
  161.8 0.6 dynamic_slice.11
  164.3 0.0 copy-done.4
  164.4 16.4 %all-to-all-done.3 = bf16[32,80,128]{2,1,0:T(8,128)(2,1)S(1)} async-done(((bf16[32,80,128]{2,1,0:T(8,128)(2,1)}), bf16[32,80,128]{2,1,0:T(8,128)(2,1)S(1)}, u32[]{:S(2)}, u32[]{:S(2)}) %all-to-all-start.3) | async-done | bytes 655392 | tf_op jit(solution)/shard_map/all_to_all | solution.py:452
  180.8 0.1 reduce_sum.34
  180.9 43.3 %all-gather = bf16[3648,128]{1,0:T(8,128)(2,1)S(1)} all-gather(bf16[152,128]{1,0:T(8,128)(2,1)S(1)} %pad_maximum_fusion.2), channel_id=2, replica_groups=mesh['z'=12,'k'=2,'y'=8,'x'=4] {'z','k'}, dimensions={0}, use_global_device_ids=true | all-gather | bytes 972800 | tf_op jit(solution)/shard_map/all_gather | solution.py:456
  224.4 0.7 convert_reduce_fusion
  225.1 0.6 pad_maximum_fusion.1
  225.7 0.6 constant_dynamic-update-slice_fusion
  (14 shorter events, 0.2 us)
Async XLA Ops:
  6.2 50.9 %slice-start = ((bf16[264,1024]{1,0:T(8,128)(2,1)}), bf16[8,1024]{1,0:T(8,128)(2,1)S(1)}, s32[]{:S(2)}) async-start(bf16[264,1024]{1,0:T(8,128)(2,1)} %q_ref.1), calls=%async_computation.4 | async-start | bytes 32768 | tf_op jit(solution)/shard_map/slice | solution.py:428
  6.2 50.9 %slice-start.1 = ((bf16[264,1024]{1,0:T(8,128)(2,1)}), bf16[8,1024]{1,0:T(8,128)(2,1)S(1)}, s32[]{:S(2)}) async-start(bf16[264,1024]{1,0:T(8,128)(2,1)} %do_ref.1), calls=%async_computation.5 | async-start | bytes 32768 | tf_op jit(solution)/shard_map/slice | solution.py:429
  6.2 72.9 %copy-start = (bf16[264,1024]{1,0:T(8,128)(2,1)S(1)}, bf16[264,1024]{1,0:T(8,128)(2,1)}, u32[]{:S(2)}) copy-start(bf16[264,1024]{1,0:T(8,128)(2,1)} %q_ref.1) | copy-start | bytes 1622020
  6.2 72.9 %copy-start.3 = (s32[1,256]{1,0:T(1,128)S(1)}, s32[1,256]{1,0:T(1,128)}, u32[]{:S(2)}) copy-start(s32[1,256]{1,0:T(1,128)} %ids_ref.3) | copy-start | bytes 3076
  6.2 34.1 %all-to-all-start = ((bf16[8,17,16,256]{3,2,1,0:T(8,128)(2,1)}), bf16[8,17,16,256]{3,2,1,0:T(8,128)(2,1)S(1)}, u32[]{:S(2)}, u32[]{:S(2)}) async-start(bf16[8,17,16,256]{3,2,1,0:T(8,128)(2,1)} %project.1), calls=%async_computation | async-start | bytes 2228224 | tf_op jit(solution)/shard_map/all_to_all | solution.py:432
  14.1 73.0 %copy-start.2 = (s32[3]{0:T(128)}, s32[3]{0:T(128)S(1)}, u32[]{:S(2)}) copy-start(s32[3]{0:T(128)S(1)} %pad_add_fusion.place_ref) | copy-start | bytes 40
  42.2 21.6 %collective-permute-start = (bf16[72,16,256]{2,1,0:T(8,128)(2,1)}, bf16[72,16,256]{2,1,0:T(8,128)(2,1)S(1)}, u32[]{:S(2)}, u32[]{:S(2)}) collective-permute-start(bf16[72,16,256]{2,1,0:T(8,128)(2,1)} %get-tuple-element.12), channel_id=1, source_target_pairs={{0,1},{1,2},{2,3},{3,0},{4,5},{5,6},{6,7},{7,4},{8,9},{9,10},{10,1... | collective-permute-start | bytes 1769480 | tf_op jit(solution)/shard_map/ppermute | solution.py:416
  49.6 28.2 %collective-permute-start.1 = (bf16[72,16,256]{2,1,0:T(8,128)(2,1)}, bf16[72,16,256]{2,1,0:T(8,128)(2,1)S(1)}, u32[]{:S(2)}, u32[]{:S(2)}) collective-permute-start(bf16[72,16,256]{2,1,0:T(8,128)(2,1)} %get-tuple-element.13), channel_id=1, source_target_pairs={{0,2},{1,3},{2,0},{3,1},{4,6},{5,7},{6,4},{7,5},{8,10},{9,11},{10,... | collective-permute-start | bytes 1769480 | tf_op jit(solution)/shard_map/ppermute | solution.py:416
  54.0 25.1 %collective-permute-start.2 = (bf16[72,16,256]{2,1,0:T(8,128)(2,1)}, bf16[72,16,256]{2,1,0:T(8,128)(2,1)S(1)}, u32[]{:S(2)}, u32[]{:S(2)}) collective-permute-start(bf16[72,16,256]{2,1,0:T(8,128)(2,1)} %get-tuple-element.14), channel_id=1, source_target_pairs={{0,3},{1,0},{2,1},{3,2},{4,7},{5,4},{6,5},{7,6},{8,11},{9,8},{10,9... | collective-permute-start | bytes 1769480 | tf_op jit(solution)/shard_map/ppermute | solution.py:416
  79.1 1.0 copy-start.1
  87.1 26.4 %all-to-all-start.1 = ((bf16[4,1344,128]{2,1,0:T(8,128)(2,1)}), bf16[4,1344,128]{2,1,0:T(8,128)(2,1)S(1)}, u32[]{:S(2)}, u32[]{:S(2)}) async-start(bf16[4,1344,128]{2,1,0:T(8,128)(2,1)} %get-tuple-element.16), calls=%async_computation.1 | async-start | bytes 2752512 | tf_op jit(solution)/shard_map/all_to_all | solution.py:440
  141.2 14.2 %collective-permute-start.3 = (f32[32,80,128]{2,1,0:T(8,128)}, f32[32,80,128]{2,1,0:T(8,128)S(1)}, u32[]{:S(2)}, u32[]{:S(2)}) collective-permute-start(f32[32,80,128]{2,1,0:T(8,128)} %get-tuple-element.18), channel_id=1, source_target_pairs={{0,32},{32,0},{1,33},{33,1},{2,34},{34,2},{3,35},{35,3},{4,36},{36... | collective-permute-start | bytes 3932168 | tf_op jit(solution)/shard_map/ppermute | solution.py:416
  157.7 4.1 %copy-start.5 = (s32[24]{0:T(128)S(1)}, s32[24]{0:T(128)}, u32[]{:S(2)}) copy-start(s32[24]{0:T(128)} %param.13) | copy-start | bytes 292
  157.7 6.6 %copy-start.4 = (bf16[264,128]{1,0:T(8,128)(2,1)S(1)}, bf16[264,128]{1,0:T(8,128)(2,1)}, u32[]{:S(2)}) copy-start(bf16[264,128]{1,0:T(8,128)(2,1)} %get-tuple-element.19) | copy-start | bytes 202756
  157.7 23.0 %all-to-all-start.3 = ((bf16[32,80,128]{2,1,0:T(8,128)(2,1)}), bf16[32,80,128]{2,1,0:T(8,128)(2,1)S(1)}, u32[]{:S(2)}, u32[]{:S(2)}) async-start(bf16[32,80,128]{2,1,0:T(8,128)(2,1)} %add_convert_fusion), calls=%async_computation.3 | async-start | bytes 1310720 | tf_op jit(solution)/shard_map/all_to_all | solution.py:452

commit v4 on v2

--- a/solution.py
+++ b/solution.py
@@ -40,20 +40,74 @@
     extra_ref[...] = jnp.concatenate([spare, counts], axis=0).astype(BF16)
 
 
-def attend_kernel(
+def prepare_kernel(
     place_ref,
     extra_ref,
     ids_ref,
     q_ref,
-    do_ref,
     qs_ref,
     dos_ref,
+    outs_ref,
+    dvs_ref,
+    begin_ref,
+    safe_ref,
+):
+    tok = ids_ref.shape[1]
+    width = qs_ref.shape[1]
+    heads = q_ref.shape[1] // width
+    group = NY * NX
+    spare_heads = qs_ref.shape[0]
+    spare = spare_heads // heads
+    factor = width ** (-0.5) * math.log2(math.e)
+    own = place_ref[0] * NX + place_ref[1]
+
+    extra = extra_ref[...].astype(F32).reshape(group, spare + 8, 2 * width)
+    counts = jnp.sum(extra[:, spare:, :], axis=0)[:, :tok]
+    ids = ids_ref[...]
+    begin = jnp.zeros((1, tok), F32)
+    for v in range(1, 4):
+        begin = jnp.where(ids == v, counts[v : v + 1, :], begin)
+    begin_ref[...] = jnp.broadcast_to(begin, begin_ref.shape)
+
+    key_bound = jnp.max(extra[:, spare + 4, :])
+    ones = jnp.ones((width, width), BF16)
+    lengths = []
+    for h in range(heads):
+        part = q_ref[:tok, h * width : (h + 1) * width].astype(F32)
+        length = dot((part * part).astype(BF16), ones, ((1,), (0,)))
+        lengths.append(jnp.max(length, axis=0, keepdims=True))
+    query_bound = jnp.max(jnp.concatenate(lengths, axis=0)) * MARGIN
+    safe_ref[0] = (key_bound * query_bound <= SAFE * SAFE * width).astype(jnp.int32)
+
+    spare_total = group * spare
+    block = extra[:, :spare, :].reshape(spare_total, 2 * width).astype(BF16)
+    s = dot(block[:, :width], qs_ref[...], ((1,), (1,))) * factor
+    key_at = lax.broadcasted_iota(jnp.int32, (spare_total, spare_heads), 0)
+    query_at = own * spare + lax.div(
+        lax.broadcasted_iota(jnp.int32, (spare_total, spare_heads), 1), heads
+    )
+    allowed = key_at <= query_at
+    s = jnp.where(allowed, s, NEG)
+    p = jnp.where(allowed, jnp.exp2(s - jnp.max(s, axis=0, keepdims=True)), 0.0)
+    p = (p * (1.0 / jnp.sum(p, axis=0, keepdims=True))).astype(BF16)
+    outs_ref[...] = dot(p, block[:, width:], ((0,), (0,))).astype(BF16)
+    got = dot(p, dos_ref[...], ((1,), (0,))).reshape(NY, NX, spare, width)
+    for xx in range(NX):
+        dvs_ref[xx] = got[:, xx].reshape(NY * spare, width).astype(BF16)
+
+
+def attend_kernel(
+    place_ref,
+    safe_ref,
+    begin_ref,
+    q_ref,
+    do_ref,
+    dvs_ref,
     kv_ref,
     kv1_ref,
     kv2_ref,
     kv3_ref,
     out_ref,
-    outs_ref,
     dv_ref,
     bias_ref,
     mask_max,
@@ -68,13 +122,10 @@
     *,
     back,
 ):
-    tok = ids_ref.shape[1]
+    tok = begin_ref.shape[1]
     width = kv_ref.shape[1] // 2
     heads = q_ref.shape[1] // width
     rows = heads * tok
-    group = NY * NX
-    spare = extra_ref.shape[0] // group - 8
-    spare_heads = qs_ref.shape[0]
     factor = width ** (-0.5) * math.log2(math.e)
     y_at, x_at = place_ref[0], place_ref[1]
     own = y_at * NX + x_at
@@ -92,24 +143,12 @@
     total_ref[...] = jnp.zeros_like(total_ref)
     acc_ref[...] = jnp.zeros_like(acc_ref)
 
-    extra = extra_ref[...].astype(F32).reshape(group, spare + 8, 2 * width)
-    counts = jnp.sum(extra[:, spare:, :], axis=0)[:, :tok]
-    ids = ids_ref[...]
-    begin = jnp.zeros((1, tok), F32)
-    for v in range(1, 4):
-        begin = jnp.where(ids == v, counts[v : v + 1, :], begin)
+    begin = begin_ref[0:1, :]
     first = jnp.min(begin).astype(jnp.int32)
     begin = begin.astype(jnp.int32)
     in_first = begin == first
     first_rows = jnp.concatenate([in_first] * heads, axis=1)
-    key_bound = jnp.max(extra[:, spare + 4, :])
-    ones = jnp.ones((width, width), BF16)
-    lengths = []
-    for h in range(heads):
-        part = q_ref[:tok, h * width : (h + 1) * width].astype(F32)
-        lengths.append(jnp.max(dot((part * part).astype(BF16), ones, ((1,), (0,))), axis=0, keepdims=True))
-    query_bound = jnp.max(jnp.concatenate(lengths, axis=0)) * MARGIN
-    safe = key_bound * query_bound <= SAFE * SAFE * width
+    safe = safe_ref[0] == 1
 
     base = (y_at - back) * NX
     last = back * NX + x_at
@@ -170,74 +209,71 @@
         mid_top = jnp.max(mid_max[...], axis=0, keepdims=True) * factor
         set_shift(jnp.where(first_rows, jnp.maximum(top, mid_top), top))
 
-    def weigh(n, shift_ref, masked):
+    def weigh_masked(n):
         key_block = chunk(n, slice(0, width))
         for h in range(heads):
             at = slice(h * tok, (h + 1) * tok)
-            s = scores(key_block, h) * factor
-            if masked:
-                s = s + bias_ref[...]
-            p = jnp.exp2(s - shift_ref[0:1, at])
+            s = scores(key_block, h) * factor + bias_ref[...]
+            p = jnp.exp2(s - mask_max[0:1, at])
             total_ref[:, at] += jnp.sum(fold(p), axis=0)
             p_ref[n - low, :, at] = p.astype(BF16)
 
-    def weigh_mid(n, carry):
-        weigh(n, mid_shift, False)
+    def weigh_mid(n, count):
+        key_block = [chunk(n + i, slice(0, width)) for i in range(count)]
+        key_block = jnp.concatenate(key_block, axis=0)
+        for h in range(heads):
+            at = slice(h * tok, (h + 1) * tok)
+            p = jnp.exp2(scores(key_block, h) * factor - mid_shift[0:1, at])
+            total_ref[:, at] += jnp.sum(p.reshape(count * tok // 8, 8, tok), axis=0)
+            p_ref[pl.ds(n - low, count), :, at] = p.astype(BF16).reshape(count, tok, tok)
+
+    def weigh_two(j, carry):
+        weigh_mid(low + 1 + 2 * j, 2)
         return carry
 
     set_bias(last)
-    weigh(last, mask_max, True)
-    lax.fori_loop(low + 1, last, weigh_mid, 0)
+    weigh_masked(last)
+    mid_count = jnp.maximum(last - low - 1, 0)
+    lax.fori_loop(0, lax.div(mid_count, 2), weigh_two, 0)
+    pl.when(lax.rem(mid_count, 2) == 1)(lambda: weigh_mid(last - 1, 1))
 
     @pl.when(low < last)
     def _():
         set_bias(low)
-        weigh(low, mask_max, True)
+        weigh_masked(low)
+
+    share = 1.0 / jnp.sum(total_ref[...], axis=0, keepdims=True)
+    for h in range(heads):
+        at = slice(h * tok, (h + 1) * tok)
+        part = slice(h * width, (h + 1) * width)
+        head_share = jnp.broadcast_to(share[:, at], (width, tok)).T
+        grad_ref[at, :] = (do_ref[:tok, part].astype(F32) * head_share).astype(BF16)
+
+    def put(n, block):
+        start = pl.multiple_of(lax.div(n, NX) * tok, tok)
+        dv_ref[lax.rem(n, NX), pl.ds(start, tok), :] = block.astype(BF16)
 
     p_ref[last - low + 1] = jnp.zeros((tok, rows), BF16)
 
-    def gather_values(j, carry):
+    def products(j, carry):
         near = low + 2 * j
         block = [chunk(n, slice(width, 2 * width)) for n in (near, jnp.minimum(near + 1, last))]
         value_t = jnp.concatenate([b.astype(F32).T.astype(BF16) for b in block], axis=1)
         weights = p_ref[pl.ds(2 * j, 2)].reshape(2 * tok, rows)
         acc_ref[...] += dot(value_t, weights, ((1,), (0,)))
+        got = dot(weights, grad_ref[...], ((1,), (0,)))
+        put(near, got[:tok])
+        pl.when(near < last)(lambda: put(near + 1, got[tok:]))
         return carry
 
-    lax.fori_loop(0, lax.div(last - low + 2, 2), gather_values, 0)
-
-    share = 1.0 / jnp.sum(total_ref[...], axis=0, keepdims=True)
+    lax.fori_loop(0, lax.div(last - low + 2, 2), products, 0)
+
     for h in range(heads):
         at = slice(h * tok, (h + 1) * tok)
         part = slice(h * width, (h + 1) * width)
-        head_share = jnp.broadcast_to(share[:, at], (width, tok))
-        out_ref[:tok, part] = (acc_ref[:, at] * head_share).T.astype(BF16)
-        grad_ref[at, :] = (do_ref[:tok, part].astype(F32) * head_share.T).astype(BF16)
-
-    def spread(n, carry):
-        got = dot(p_ref[n - low], grad_ref[...], ((1,), (0,)))
-        column = lax.rem(n, NX)
-        row = lax.div(n, NX)
-        dv_ref[column, pl.ds(pl.multiple_of(row * tok, tok), tok), :] = got.astype(BF16)
-        return carry
-
-    lax.fori_loop(low, last + 1, spread, 0)
-
-    spare_total = group * spare
-    block = extra[:, :spare, :].reshape(spare_total, 2 * width).astype(BF16)
-    s = dot(block[:, :width], qs_ref[...], ((1,), (1,))) * factor
-    key_at = lax.broadcasted_iota(jnp.int32, (spare_total, spare_heads), 0)
-    query_at = own * spare + lax.div(
-        lax.broadcasted_iota(jnp.int32, (spare_total, spare_heads), 1), heads
-    )
-    allowed = key_at <= query_at
-    s = jnp.where(allowed, s, NEG)
-    p = jnp.where(allowed, jnp.exp2(s - jnp.max(s, axis=0, keepdims=True)), 0.0)
-    p = (p * (1.0 / jnp.sum(p, axis=0, keepdims=True))).astype(BF16)
-    outs_ref[...] = dot(p, block[:, width:], ((0,), (0,))).astype(BF16)
-    got = dot(p, dos_ref[...], ((1,), (0,))).reshape(NY, NX, spare, width)
-    for xx in range(NX):
-        dv_ref[xx, (back + 1) * tok :, :] = got[:, xx].reshape(NY * spare, width).astype(BF16)
+        out_ref[:tok, part] = (acc_ref[:, at] * share[:, at]).T.astype(BF16)
+
+    dv_ref[:, (back + 1) * tok :, :] = dvs_ref[...]
 
 
 def combine_kernel(place_ref, got_ref, hidden_ref, home_ref, mine_ref, other_ref):
@@ -276,21 +312,39 @@
     )(hidden, value_weight, keys, segment_ids)
 
 
-def attend(place, extra, segment_ids, queries, attn_grad, spare_q, spare_do, pieces, back):
+def prepare(place, extra, segment_ids, queries, spare_q, spare_do):
     tok = segment_ids.shape[1]
+    width = spare_q.shape[1]
+    spare = queries.shape[0] - tok
+    return pl.pallas_call(
+        prepare_kernel,
+        out_shape=(
+            jax.ShapeDtypeStruct(spare_q.shape, BF16),
+            jax.ShapeDtypeStruct((NX, NY * spare, width), BF16),
+            jax.ShapeDtypeStruct((8, tok), F32),
+            jax.ShapeDtypeStruct((1,), jnp.int32),
+        ),
+        in_specs=[SMEM] + [VMEM] * 5,
+        out_specs=(VMEM, VMEM, VMEM, SMEM),
+        compiler_params=LIMIT,
+        name="prepare",
+    )(place, extra, segment_ids, queries, spare_q, spare_do)
+
+
+def attend(place, safe, begin, queries, attn_grad, spare_sums, pieces, back):
+    tok = begin.shape[1]
     width = pieces[0].shape[1] // 2
     heads = queries.shape[1] // width
-    spare = extra.shape[0] // (NY * NX) - 8
+    spare = queries.shape[0] - tok
     rows = heads * tok
     return pl.pallas_call(
         functools.partial(attend_kernel, back=back),
         out_shape=(
             jax.ShapeDtypeStruct(queries.shape, BF16),
-            jax.ShapeDtypeStruct(spare_q.shape, BF16),
             jax.ShapeDtypeStruct((NX, (back + 1) * tok + NY * spare, width), BF16),
         ),
-        in_specs=[SMEM] + [VMEM] * 6 + [pl.BlockSpec(memory_space=pl.ANY)] * NX,
-        out_specs=(VMEM, VMEM, VMEM),
+        in_specs=[SMEM] * 2 + [VMEM] * 4 + [pl.BlockSpec(memory_space=pl.ANY)] * NX,
+        out_specs=(VMEM, VMEM),
         scratch_shapes=[
             pltpu.VMEM((tok, tok), F32),
             pltpu.VMEM((8, rows), F32),
@@ -305,7 +359,7 @@
         ],
         compiler_params=LIMIT,
         name="attend",
-    )(place, extra, segment_ids, queries, attn_grad, spare_q, spare_do, *pieces)
+    )(place, safe, begin, queries, attn_grad, spare_sums, *pieces)
 
 
 def combine(place, got, hidden):
@@ -342,6 +396,7 @@
     extras = lax.all_to_all(
         jnp.broadcast_to(extra[None], (NY * NX,) + extra.shape), ("y", "x"), 0, 0, tiled=True
     ).reshape(NY * NX * extra.shape[0], 2 * width)
+    *rows, extras = lax.optimization_barrier((*rows, extras))
     column = jnp.concatenate(rows, axis=0)
     early, late = column[: back * tok], column[tok:]
     pieces = [column]
@@ -350,8 +405,11 @@
         pieces.append(shift(send, "x", NX, s))
 
     place = jnp.stack([y_at, x_at, k_at]).astype(jnp.int32)
-    main_out, spare_out, sums = attend(
-        place, extras, segment_ids, queries, attn_grad, spare_q, spare_do, pieces, back
+    spare_out, spare_sums, begin, safe = prepare(
+        place, extras, segment_ids, queries, spare_q, spare_do
+    )
+    main_out, sums = attend(
+        place, safe, begin, queries, attn_grad, spare_sums, pieces, back
     )
 
     got = lax.all_to_all(sums, "x", 0, 0, tiled=True)

time: 219 us -> 218 us (level)
  blocking collectives: 74.1 us -> 82 us
  starting transfers between devices: 52.6 us -> 45.6 us
  waiting for transfers between devices: 67.2 us -> 63.3 us
    ppermute x8, waiting for transfers between devices: 17.6 us -> 33 us  [shift(): lax.ppermute(array, axis, [(i, (i + step) % size) for i in range(size)])]
    all_to_all x1, waiting for transfers between devices: 15.3 us -> 0.01 us  [body(): lax.all_to_all(jnp.broadcast_to(extra[None], (NY * NX,) + extra.shape), (...]
    all_to_all x1, blocking collectives: 29.2 us -> 42.7 us  [body(): lax.all_to_all(jnp.concatenate([main_part, spare_part], axis=1), 'y', 0,...]
    ppermute x8, starting transfers between devices: 32.7 us -> 26.6 us  [shift(): lax.ppermute(array, axis, [(i, (i + step) % size) for i in range(size)])]
    all_gather x1, blocking collectives: 45 us -> 39.3 us  [body(): every = lax.all_gather(bundle, ('z', 'k'), axis=0)]
    all_to_all x1, starting transfers between devices: 9.52 us -> 4.44 us  [body(): got = lax.all_to_all(sums, 'x', 0, 0, tiled=True)]
    all_to_all x1, starting transfers between devices: 6.3 us -> 10.5 us  [body(): lax.all_to_all(jnp.broadcast_to(extra[None], (NY * NX,) + extra.shape), (...]
    all_to_all x1, waiting for transfers between devices: 17.9 us -> 13.9 us  [body(): got = lax.all_to_all(sums, 'x', 0, 0, tiled=True)]
  transfers between devices with their start and end apart: 11 -> 11, of which waited for: 7 -> 8; matrix products, arithmetic and copies ran while one was open for 1% -> 0% of each run, Pallas kernels for 0% -> 1%
where the time goes in v4:
time: 218 us; the launch traced here: 217 us
  blocking collectives  82 us (38%)
  waiting for transfers between devices  63.3 us (29%)
  starting transfers between devices  45.6 us (21%)
  Pallas kernels  13.7 us (6%)
  local copies, waits for them, and re-layouts  5.13 us (2%)
  other arithmetic  4.64 us (2%)
  between operations  2.93 us (1%)
    all_to_all x1, blocking collectives, body(): lax.all_to_all(jnp.concatenate([main_part, spare_part], axis=1), 'y', 0,...  42.7 us
    all_gather x1, blocking collectives, body(): every = lax.all_gather(bundle, ('z', 'k'), axis=0)  39.3 us
    ppermute x8, waiting for transfers between devices, shift(): lax.ppermute(array, axis, [(i, (i + step) % size) for i in range(size)])  33 us
    ppermute x8, starting transfers between devices, shift(): lax.ppermute(array, axis, [(i, (i + step) % size) for i in range(size)])  26.6 us
    all_to_all x1, waiting for transfers between devices, body(): got = lax.all_to_all(both, ('y', 'x'), 0, 0, tiled=True)  16.4 us
    all_to_all x1, waiting for transfers between devices, body(): got = lax.all_to_all(sums, 'x', 0, 0, tiled=True)  13.9 us
    all_to_all x1, starting transfers between devices, body(): lax.all_to_all(jnp.broadcast_to(extra[None], (NY * NX,) + extra.shape), (...  10.5 us
    pallas_call x1, Pallas kernels, attend(): pl.pallas_call(functools.partial(attend_kernel, back=back), out_shape=(ja...  6.36 us
  transfers between devices with their start and end apart: 11, of which 8 were waited for; matrix products, arithmetic and copies ran while one was open for 0% of the time, Pallas kernels for 1%

profile of v4, /device:TPU:1, one launch (start us, length us, event | category | flops | bytes accessed | tf_op | source)
XLA Modules:
  0.0 217.2 jit_solution(10050313075279074615)
XLA Ops:
  0.6 0.0 copy-start.1
  0.6 1.3 copy-done.1
  1.9 0.0 copy-start.3
  1.9 0.9 copy-done.3
  2.8 0.0 copy-start.4
  2.8 0.7 copy-done.4
  3.5 2.6 %project.1 = (bf16[256,256]{1,0:T(8,128)(2,1)S(1)}, bf16[16,256]{1,0:T(8,128)(2,1)S(1)}) custom-call(bf16[264,5120]{1,0:T(8,128)(2,1)} %hidden_ref.3, bf16[5120,128]{1,0:T(8,128)(2,1)S(1)} %copy-done.1, bf16[264,128]{1,0:T(8,128)(2,1)S(1)} %copy-done.3, s32[1,256]{1,0:T(1,128)S(1)} %copy-done.4), custom_call_target="tpu_custom_call" | custom-call | tf_op jit(solution)/shard_map/project/pallas_call | solution.py:302
  6.2 0.7 broadcast_in_dim.4
  6.9 10.5 %all-to-all-start = ((bf16[32,16,256]{2,1,0:T(8,128)(2,1)}), bf16[32,16,256]{2,1,0:T(8,128)(2,1)S(1)}, u32[]{:S(2)}, u32[]{:S(2)}) async-start(bf16[32,16,256]{2,1,0:T(8,128)(2,1)} %broadcast_in_dim.4), calls=%async_computation | async-start | bytes 524288 | tf_op jit(solution)/shard_map/all_to_all | solution.py:396
  17.4 3.1 %collective-permute-start.3 = (bf16[256,256]{1,0:T(8,128)(2,1)S(1)}, bf16[256,256]{1,0:T(8,128)(2,1)S(1)}, u32[]{:S(2)}, u32[]{:S(2)}) collective-permute-start(bf16[256,256]{1,0:T(8,128)(2,1)S(1)} %get-tuple-element.30), channel_id=1, source_target_pairs={{0,4},{4,8},{8,12},{12,16},{16,20},{20,24},{24,28},{28,0},{1,5},{5... | collective-permute-start | bytes 393224 | tf_op jit(solution)/shard_map/ppermute | solution.py:380
  20.5 4.0 %collective-permute-start.2 = (bf16[256,256]{1,0:T(8,128)(2,1)S(1)}, bf16[256,256]{1,0:T(8,128)(2,1)S(1)}, u32[]{:S(2)}, u32[]{:S(2)}) collective-permute-start(bf16[256,256]{1,0:T(8,128)(2,1)S(1)} %get-tuple-element.30), channel_id=1, source_target_pairs={{0,8},{4,12},{8,16},{12,20},{16,24},{20,28},{24,0},{28,4},{1,9},{5... | collective-permute-start | bytes 393224 | tf_op jit(solution)/shard_map/ppermute | solution.py:380
  24.5 4.3 %collective-permute-start.1 = (bf16[256,256]{1,0:T(8,128)(2,1)S(1)}, bf16[256,256]{1,0:T(8,128)(2,1)S(1)}, u32[]{:S(2)}, u32[]{:S(2)}) collective-permute-start(bf16[256,256]{1,0:T(8,128)(2,1)S(1)} %get-tuple-element.30), channel_id=1, source_target_pairs={{0,12},{4,16},{8,20},{12,24},{16,28},{20,0},{24,4},{28,8},{1,13},{... | collective-permute-start | bytes 393224 | tf_op jit(solution)/shard_map/ppermute | solution.py:380
  28.9 3.9 %collective-permute-start = (bf16[256,256]{1,0:T(8,128)(2,1)S(1)}, bf16[256,256]{1,0:T(8,128)(2,1)S(1)}, u32[]{:S(2)}, u32[]{:S(2)}) collective-permute-start(bf16[256,256]{1,0:T(8,128)(2,1)S(1)} %get-tuple-element.30), channel_id=1, source_target_pairs={{0,16},{4,20},{8,24},{12,28},{16,0},{20,4},{24,8},{28,12},{1,17},{... | collective-permute-start | bytes 393224 | tf_op jit(solution)/shard_map/ppermute | solution.py:380
  32.9 0.0 collective-permute-done.3
  32.9 0.0 collective-permute-done.2
  32.9 5.6 %collective-permute-done.1 = bf16[256,256]{1,0:T(8,128)(2,1)S(1)} collective-permute-done((bf16[256,256]{1,0:T(8,128)(2,1)S(1)}, bf16[256,256]{1,0:T(8,128)(2,1)S(1)}, u32[]{:S(2)}, u32[]{:S(2)}) %collective-permute-start.1) | collective-permute-done | bytes 131104 | tf_op jit(solution)/shard_map/ppermute | solution.py:380
  38.4 5.1 %collective-permute-done = bf16[256,256]{1,0:T(8,128)(2,1)S(1)} collective-permute-done((bf16[256,256]{1,0:T(8,128)(2,1)S(1)}, bf16[256,256]{1,0:T(8,128)(2,1)S(1)}, u32[]{:S(2)}, u32[]{:S(2)}) %collective-permute-start) | collective-permute-done | bytes 131104 | tf_op jit(solution)/shard_map/ppermute | solution.py:380
  43.5 0.0 all-to-all-done
  43.7 0.0 slice-start.1
  43.7 0.0 slice-start
  43.7 0.0 copy-start
  43.7 0.0 copy-start.5
  43.7 0.0 copy-start.2
  43.7 1.3 broadcast_select_fusion
  45.0 4.2 %collective-permute-start.6 = (bf16[1024,256]{1,0:T(8,128)(2,1)}, bf16[1024,256]{1,0:T(8,128)(2,1)S(1)}, u32[]{:S(2)}, u32[]{:S(2)}) collective-permute-start(bf16[1024,256]{1,0:T(8,128)(2,1)} %get-tuple-element.37), channel_id=1, source_target_pairs={{0,3},{1,0},{2,1},{3,2},{4,7},{5,4},{6,5},{7,6},{8,11},{9,8},{10,9... | collective-permute-start | bytes 1572872 | tf_op jit(solution)/shard_map/ppermute | solution.py:380
  49.3 2.2 collective-permute-start.5
  51.4 2.5 %collective-permute-start.4 = (bf16[1024,256]{1,0:T(8,128)(2,1)}, bf16[1024,256]{1,0:T(8,128)(2,1)}, u32[]{:S(2)}, u32[]{:S(2)}) collective-permute-start(bf16[1024,256]{1,0:T(8,128)(2,1)} %get-tuple-element.39), channel_id=1, source_target_pairs={{0,1},{1,2},{2,3},{3,0},{4,5},{5,6},{6,7},{7,4},{8,9},{9,10},{10,1... | collective-permute-start | bytes 1572872 | tf_op jit(solution)/shard_map/ppermute | solution.py:380
  53.9 0.0 slice-done.1
  54.0 0.0 slice-done
  54.0 0.1 pad_add_fusion.place_ref
  54.1 0.0 copy-done
  54.1 0.0 copy-done.5
  54.1 1.6 prepare.1
  55.7 2.5 %collective-permute-done.6.kv3_ref = bf16[1024,256]{1,0:T(8,128)(2,1)S(1)} collective-permute-done((bf16[1024,256]{1,0:T(8,128)(2,1)}, bf16[1024,256]{1,0:T(8,128)(2,1)S(1)}, u32[]{:S(2)}, u32[]{:S(2)}) %collective-permute-start.6) | collective-permute-done | bytes 524320 | tf_op jit(solution)/shard_map/ppermute | solution.py:380
  58.2 2.8 %collective-permute-done.5.kv2_ref = bf16[1024,256]{1,0:T(8,128)(2,1)S(1)} collective-permute-done((bf16[1024,256]{1,0:T(8,128)(2,1)}, bf16[1024,256]{1,0:T(8,128)(2,1)S(1)}, u32[]{:S(2)}, u32[]{:S(2)}) %collective-permute-start.5) | collective-permute-done | bytes 524320 | tf_op jit(solution)/shard_map/ppermute | solution.py:380
  61.0 14.4 %collective-permute-done.4.kv1_ref = bf16[1024,256]{1,0:T(8,128)(2,1)} collective-permute-done((bf16[1024,256]{1,0:T(8,128)(2,1)}, bf16[1024,256]{1,0:T(8,128)(2,1)}, u32[]{:S(2)}, u32[]{:S(2)}) %collective-permute-start.4) | collective-permute-done | bytes 524320 | tf_op jit(solution)/shard_map/ppermute | solution.py:380
  75.4 0.0 copy-done.2
  75.4 6.4 %attend.1 = (bf16[264,1024]{1,0:T(8,128)(2,1)}, bf16[4,1344,128]{2,1,0:T(8,128)(2,1)}) custom-call(s32[3]{0:T(128)S(1)} %pad_add_fusion.place_ref, s32[1]{0:T(128)} %get-tuple-element.23.safe_ref, f32[8,256]{1,0:T(8,128)S(1)} %get-tuple-element.24.begin_ref, bf16[264,1024]{1,0:T(8,128)(2,1)S(1)} %copy-done, bf16[264,1024]{1,0:T(8,128)(2,1)S(1)} %copy-done.2, ...), custom_call_target="tpu_custom_call" | custom-call | tf_op jit(solution)/shard_map/attend/pallas_call | solution.py:340
  81.8 4.4 %all-to-all-start.1 = ((bf16[4,1344,128]{2,1,0:T(8,128)(2,1)}), bf16[4,1344,128]{2,1,0:T(8,128)(2,1)S(1)}, u32[]{:S(2)}, u32[]{:S(2)}) async-start(bf16[4,1344,128]{2,1,0:T(8,128)(2,1)} %get-tuple-element.32), calls=%async_computation.1 | async-start | bytes 2752512 | tf_op jit(solution)/shard_map/all_to_all | solution.py:415
  86.2 13.9 %all-to-all-done.1 = bf16[4,1344,128]{2,1,0:T(8,128)(2,1)S(1)} async-done(((bf16[4,1344,128]{2,1,0:T(8,128)(2,1)}), bf16[4,1344,128]{2,1,0:T(8,128)(2,1)S(1)}, u32[]{:S(2)}, u32[]{:S(2)}) %all-to-all-start.1) | async-done | bytes 1376288 | tf_op jit(solution)/shard_map/all_to_all | solution.py:415
  100.1 0.4 reduce_sum.33
  100.6 0.4 fusion.2
  101.0 42.7 %all_to_all.20.got_ref = bf16[8,264,128]{2,1,0:T(8,128)(2,1)S(1)} all-to-all(bf16[8,264,128]{2,1,0:T(8,128)(2,1)S(1)} %pad_maximum_fusion), channel_id=1, replica_groups=mesh['z'=12,'k'=2,'y'=8,'x'=4] {'y'}, dimensions={0} | all-to-all | bytes 1081344 | tf_op jit(solution)/shard_map/all_to_all | solution.py:424
  143.7 3.1 %combine.1 = (bf16[264,128]{1,0:T(8,128)(2,1)S(1)}, f32[32,80,128]{2,1,0:T(8,128)S(1)}, f32[32,80,128]{2,1,0:T(8,128)S(1)}) custom-call(s32[3]{0:T(128)S(1)} %pad_add_fusion.place_ref, bf16[8,264,128]{2,1,0:T(8,128)(2,1)S(1)} %all_to_all.20.got_ref, bf16[264,5120]{1,0:T(8,128)(2,1)} %hidden_ref.3), custom_call_target="tpu_custom_call" | custom-call | tf_op jit(solution)/shard_map/combine/pallas_call | solution.py:369
  146.8 2.3 %collective-permute-start.7 = (f32[32,80,128]{2,1,0:T(8,128)S(1)}, f32[32,80,128]{2,1,0:T(8,128)S(1)}, u32[]{:S(2)}, u32[]{:S(2)}) collective-permute-start(f32[32,80,128]{2,1,0:T(8,128)S(1)} %get-tuple-element.34), channel_id=1, source_target_pairs={{0,32},{32,0},{1,33},{33,1},{2,34},{34,2},{3,35},{35,3},{4,36},{36... | collective-permute-start | bytes 3932168 | tf_op jit(solution)/shard_map/ppermute | solution.py:380
  149.1 2.6 %collective-permute-done.7 = f32[32,80,128]{2,1,0:T(8,128)S(1)} collective-permute-done((f32[32,80,128]{2,1,0:T(8,128)S(1)}, f32[32,80,128]{2,1,0:T(8,128)S(1)}, u32[]{:S(2)}, u32[]{:S(2)}) %collective-permute-start.7) | collective-permute-done | bytes 1310752 | tf_op jit(solution)/shard_map/ppermute | solution.py:380
  151.7 1.0 add_convert_fusion
  152.8 0.0 copy-start.6
  152.8 4.0 %all-to-all-start.3 = ((bf16[32,80,128]{2,1,0:T(8,128)(2,1)}), bf16[32,80,128]{2,1,0:T(8,128)(2,1)S(1)}, u32[]{:S(2)}, u32[]{:S(2)}) async-start(bf16[32,80,128]{2,1,0:T(8,128)(2,1)} %add_convert_fusion), calls=%async_computation.3 | async-start | bytes 1310720 | tf_op jit(solution)/shard_map/all_to_all | solution.py:427
  156.8 0.0 copy-done.6
  156.8 0.6 dynamic_slice.11
  159.4 16.4 %all-to-all-done.3 = bf16[32,80,128]{2,1,0:T(8,128)(2,1)S(1)} async-done(((bf16[32,80,128]{2,1,0:T(8,128)(2,1)}), bf16[32,80,128]{2,1,0:T(8,128)(2,1)S(1)}, u32[]{:S(2)}, u32[]{:S(2)}) %all-to-all-start.3) | async-done | bytes 655392 | tf_op jit(solution)/shard_map/all_to_all | solution.py:427
  175.8 0.1 reduce_sum.34
  175.9 39.3 %all-gather = bf16[3648,128]{1,0:T(8,128)(2,1)S(1)} all-gather(bf16[152,128]{1,0:T(8,128)(2,1)S(1)} %pad_maximum_fusion.2), channel_id=2, replica_groups=mesh['z'=12,'k'=2,'y'=8,'x'=4] {'z','k'}, dimensions={0}, use_global_device_ids=true | all-gather | bytes 972800 | tf_op jit(solution)/shard_map/all_gather | solution.py:431
  215.3 0.7 convert_reduce_fusion
  216.0 0.6 constant_dynamic-update-slice_fusion.13
  216.6 0.6 pad_maximum_fusion.1
  (19 shorter events, 0.4 us)
Async XLA Ops:
  0.6 1.3 copy-start.1
  1.9 0.9 copy-start.3
  2.8 0.7 copy-start.4
  6.9 36.6 %all-to-all-start = ((bf16[32,16,256]{2,1,0:T(8,128)(2,1)}), bf16[32,16,256]{2,1,0:T(8,128)(2,1)S(1)}, u32[]{:S(2)}, u32[]{:S(2)}) async-start(bf16[32,16,256]{2,1,0:T(8,128)(2,1)} %broadcast_in_dim.4), calls=%async_computation | async-start | bytes 524288 | tf_op jit(solution)/shard_map/all_to_all | solution.py:396
  17.4 15.5 %collective-permute-start.3 = (bf16[256,256]{1,0:T(8,128)(2,1)S(1)}, bf16[256,256]{1,0:T(8,128)(2,1)S(1)}, u32[]{:S(2)}, u32[]{:S(2)}) collective-permute-start(bf16[256,256]{1,0:T(8,128)(2,1)S(1)} %get-tuple-element.30), channel_id=1, source_target_pairs={{0,4},{4,8},{8,12},{12,16},{16,20},{20,24},{24,28},{28,0},{1,5},{5... | collective-permute-start | bytes 393224 | tf_op jit(solution)/shard_map/ppermute | solution.py:380
  20.5 12.3 %collective-permute-start.2 = (bf16[256,256]{1,0:T(8,128)(2,1)S(1)}, bf16[256,256]{1,0:T(8,128)(2,1)S(1)}, u32[]{:S(2)}, u32[]{:S(2)}) collective-permute-start(bf16[256,256]{1,0:T(8,128)(2,1)S(1)} %get-tuple-element.30), channel_id=1, source_target_pairs={{0,8},{4,12},{8,16},{12,20},{16,24},{20,28},{24,0},{28,4},{1,9},{5... | collective-permute-start | bytes 393224 | tf_op jit(solution)/shard_map/ppermute | solution.py:380
  24.5 13.9 %collective-permute-start.1 = (bf16[256,256]{1,0:T(8,128)(2,1)S(1)}, bf16[256,256]{1,0:T(8,128)(2,1)S(1)}, u32[]{:S(2)}, u32[]{:S(2)}) collective-permute-start(bf16[256,256]{1,0:T(8,128)(2,1)S(1)} %get-tuple-element.30), channel_id=1, source_target_pairs={{0,12},{4,16},{8,20},{12,24},{16,28},{20,0},{24,4},{28,8},{1,13},{... | collective-permute-start | bytes 393224 | tf_op jit(solution)/shard_map/ppermute | solution.py:380
  28.9 14.6 %collective-permute-start = (bf16[256,256]{1,0:T(8,128)(2,1)S(1)}, bf16[256,256]{1,0:T(8,128)(2,1)S(1)}, u32[]{:S(2)}, u32[]{:S(2)}) collective-permute-start(bf16[256,256]{1,0:T(8,128)(2,1)S(1)} %get-tuple-element.30), channel_id=1, source_target_pairs={{0,16},{4,20},{8,24},{12,28},{16,0},{20,4},{24,8},{28,12},{1,17},{... | collective-permute-start | bytes 393224 | tf_op jit(solution)/shard_map/ppermute | solution.py:380
  43.7 10.3 %slice-start.1 = ((bf16[264,1024]{1,0:T(8,128)(2,1)}), bf16[8,1024]{1,0:T(8,128)(2,1)S(1)}, s32[]{:S(2)}) async-start(bf16[264,1024]{1,0:T(8,128)(2,1)} %do_ref.1), calls=%async_computation.5 | async-start | bytes 32768 | tf_op jit(solution)/shard_map/slice | solution.py:393
  43.7 10.3 %slice-start = ((bf16[264,1024]{1,0:T(8,128)(2,1)}), bf16[8,1024]{1,0:T(8,128)(2,1)S(1)}, s32[]{:S(2)}) async-start(bf16[264,1024]{1,0:T(8,128)(2,1)} %q_ref.3), calls=%async_computation.4 | async-start | bytes 32768 | tf_op jit(solution)/shard_map/slice | solution.py:392
  43.7 10.4 %copy-start = (bf16[264,1024]{1,0:T(8,128)(2,1)S(1)}, bf16[264,1024]{1,0:T(8,128)(2,1)}, u32[]{:S(2)}) copy-start(bf16[264,1024]{1,0:T(8,128)(2,1)} %q_ref.3) | copy-start | bytes 1622020
  43.7 10.4 %copy-start.5 = (s32[1,256]{1,0:T(1,128)S(1)}, s32[1,256]{1,0:T(1,128)}, u32[]{:S(2)}) copy-start(s32[1,256]{1,0:T(1,128)} %ids_ref.3) | copy-start | bytes 3076
  43.7 31.7 %copy-start.2 = (bf16[264,1024]{1,0:T(8,128)(2,1)S(1)}, bf16[264,1024]{1,0:T(8,128)(2,1)}, u32[]{:S(2)}) copy-start(bf16[264,1024]{1,0:T(8,128)(2,1)} %do_ref.1) | copy-start | bytes 1622020
  45.0 13.2 %collective-permute-start.6 = (bf16[1024,256]{1,0:T(8,128)(2,1)}, bf16[1024,256]{1,0:T(8,128)(2,1)S(1)}, u32[]{:S(2)}, u32[]{:S(2)}) collective-permute-start(bf16[1024,256]{1,0:T(8,128)(2,1)} %get-tuple-element.37), channel_id=1, source_target_pairs={{0,3},{1,0},{2,1},{3,2},{4,7},{5,4},{6,5},{7,6},{8,11},{9,8},{10,9... | collective-permute-start | bytes 1572872 | tf_op jit(solution)/shard_map/ppermute | solution.py:380
  49.3 11.7 %collective-permute-start.5 = (bf16[1024,256]{1,0:T(8,128)(2,1)}, bf16[1024,256]{1,0:T(8,128)(2,1)S(1)}, u32[]{:S(2)}, u32[]{:S(2)}) collective-permute-start(bf16[1024,256]{1,0:T(8,128)(2,1)} %get-tuple-element.38), channel_id=1, source_target_pairs={{0,2},{1,3},{2,0},{3,1},{4,6},{5,7},{6,4},{7,5},{8,10},{9,11},{10,... | collective-permute-start | bytes 1572872 | tf_op jit(solution)/shard_map/ppermute | solution.py:380
  51.4 24.0 %collective-permute-start.4 = (bf16[1024,256]{1,0:T(8,128)(2,1)}, bf16[1024,256]{1,0:T(8,128)(2,1)}, u32[]{:S(2)}, u32[]{:S(2)}) collective-permute-start(bf16[1024,256]{1,0:T(8,128)(2,1)} %get-tuple-element.39), channel_id=1, source_target_pairs={{0,1},{1,2},{2,3},{3,0},{4,5},{5,6},{6,7},{7,4},{8,9},{9,10},{10,1... | collective-permute-start | bytes 1572872 | tf_op jit(solution)/shard_map/ppermute | solution.py:380
  81.8 18.3 %all-to-all-start.1 = ((bf16[4,1344,128]{2,1,0:T(8,128)(2,1)}), bf16[4,1344,128]{2,1,0:T(8,128)(2,1)S(1)}, u32[]{:S(2)}, u32[]{:S(2)}) async-start(bf16[4,1344,128]{2,1,0:T(8,128)(2,1)} %get-tuple-element.32), calls=%async_computation.1 | async-start | bytes 2752512 | tf_op jit(solution)/shard_map/all_to_all | solution.py:415
  146.8 5.0 %collective-permute-start.7 = (f32[32,80,128]{2,1,0:T(8,128)S(1)}, f32[32,80,128]{2,1,0:T(8,128)S(1)}, u32[]{:S(2)}, u32[]{:S(2)}) collective-permute-start(f32[32,80,128]{2,1,0:T(8,128)S(1)} %get-tuple-element.34), channel_id=1, source_target_pairs={{0,32},{32,0},{1,33},{33,1},{2,34},{34,2},{3,35},{35,3},{4,36},{36... | collective-permute-start | bytes 3932168 | tf_op jit(solution)/shard_map/ppermute | solution.py:380
  152.8 4.1 %copy-start.6 = (s32[24]{0:T(128)S(1)}, s32[24]{0:T(128)}, u32[]{:S(2)}) copy-start(s32[24]{0:T(128)} %param.13) | copy-start | bytes 292
  152.8 23.0 %all-to-all-start.3 = ((bf16[32,80,128]{2,1,0:T(8,128)(2,1)}), bf16[32,80,128]{2,1,0:T(8,128)(2,1)S(1)}, u32[]{:S(2)}, u32[]{:S(2)}) async-start(bf16[32,80,128]{2,1,0:T(8,128)(2,1)} %add_convert_fusion), calls=%async_computation.3 | async-start | bytes 1310720 | tf_op jit(solution)/shard_map/all_to_all | solution.py:427

commit v5 on v2

--- a/solution.py
+++ b/solution.py
@@ -55,6 +55,7 @@
     out_ref,
     outs_ref,
     dv_ref,
+    own_ref,
     bias_ref,
     mask_max,
     mid_max,
@@ -89,6 +90,7 @@
         copy.start()
 
     dv_ref[...] = jnp.zeros_like(dv_ref)
+    own_ref[...] = jnp.zeros_like(own_ref)
     total_ref[...] = jnp.zeros_like(total_ref)
     acc_ref[...] = jnp.zeros_like(acc_ref)
 
@@ -170,58 +172,79 @@
         mid_top = jnp.max(mid_max[...], axis=0, keepdims=True) * factor
         set_shift(jnp.where(first_rows, jnp.maximum(top, mid_top), top))
 
-    def weigh(n, shift_ref, masked):
+    def weigh_masked(n):
         key_block = chunk(n, slice(0, width))
         for h in range(heads):
             at = slice(h * tok, (h + 1) * tok)
-            s = scores(key_block, h) * factor
-            if masked:
-                s = s + bias_ref[...]
-            p = jnp.exp2(s - shift_ref[0:1, at])
+            s = scores(key_block, h) * factor + bias_ref[...]
+            p = jnp.exp2(s - mask_max[0:1, at])
             total_ref[:, at] += jnp.sum(fold(p), axis=0)
             p_ref[n - low, :, at] = p.astype(BF16)
 
-    def weigh_mid(n, carry):
-        weigh(n, mid_shift, False)
+    def weigh_mid(n, count):
+        key_block = [chunk(n + i, slice(0, width)) for i in range(count)]
+        key_block = jnp.concatenate(key_block, axis=0)
+        for h in range(heads):
+            at = slice(h * tok, (h + 1) * tok)
+            p = jnp.exp2(scores(key_block, h) * factor - mid_shift[0:1, at])
+            total_ref[:, at] += jnp.sum(p.reshape(count * tok // 8, 8, tok), axis=0)
+            p_ref[pl.ds(n - low, count), :, at] = p.astype(BF16).reshape(count, tok, tok)
+
+    def weigh_two(j, carry):
+        weigh_mid(low + 1 + 2 * j, 2)
         return carry
 
     set_bias(last)
-    weigh(last, mask_max, True)
-    lax.fori_loop(low + 1, last, weigh_mid, 0)
+    weigh_masked(last)
+    mid_count = jnp.maximum(last - low - 1, 0)
+    lax.fori_loop(0, lax.div(mid_count, 2), weigh_two, 0)
+    pl.when(lax.rem(mid_count, 2) == 1)(lambda: weigh_mid(last - 1, 1))
 
     @pl.when(low < last)
     def _():
         set_bias(low)
-        weigh(low, mask_max, True)
+        weigh_masked(low)
+
+    share = 1.0 / jnp.sum(total_ref[...], axis=0, keepdims=True)
+    for h in range(heads):
+        at = slice(h * tok, (h + 1) * tok)
+        part = slice(h * width, (h + 1) * width)
+        head_share = jnp.broadcast_to(share[:, at], (width, tok)).T
+        grad_ref[at, :] = (do_ref[:tok, part].astype(F32) * head_share).astype(BF16)
+
+    def put(n, block):
+        column = lax.rem(n, NX)
+        row = lax.div(n, NX)
+        block = block.astype(BF16)
+
+        @pl.when(column == x_at)
+        def _():
+            own_ref[pl.ds(pl.multiple_of(row * tok, tok), tok), :] = block
+
+        @pl.when(column != x_at)
+        def _():
+            start = (row - jnp.where(column < x_at, 1, 0)) * tok
+            dv_ref[column, pl.ds(pl.multiple_of(start, tok), tok), :] = block
 
     p_ref[last - low + 1] = jnp.zeros((tok, rows), BF16)
 
-    def gather_values(j, carry):
+    def products(j, carry):
         near = low + 2 * j
         block = [chunk(n, slice(width, 2 * width)) for n in (near, jnp.minimum(near + 1, last))]
         value_t = jnp.concatenate([b.astype(F32).T.astype(BF16) for b in block], axis=1)
         weights = p_ref[pl.ds(2 * j, 2)].reshape(2 * tok, rows)
         acc_ref[...] += dot(value_t, weights, ((1,), (0,)))
+        got = dot(weights, grad_ref[...], ((1,), (0,)))
+        put(near, got[:tok])
+        pl.when(near < last)(lambda: put(near + 1, got[tok:]))
         return carry
 
-    lax.fori_loop(0, lax.div(last - low + 2, 2), gather_values, 0)
-
-    share = 1.0 / jnp.sum(total_ref[...], axis=0, keepdims=True)
+    lax.fori_loop(0, lax.div(last - low + 2, 2), products, 0)
+
     for h in range(heads):
         at = slice(h * tok, (h + 1) * tok)
         part = slice(h * width, (h + 1) * width)
-        head_share = jnp.broadcast_to(share[:, at], (width, tok))
-        out_ref[:tok, part] = (acc_ref[:, at] * head_share).T.astype(BF16)
-        grad_ref[at, :] = (do_ref[:tok, part].astype(F32) * head_share.T).astype(BF16)
-
-    def spread(n, carry):
-        got = dot(p_ref[n - low], grad_ref[...], ((1,), (0,)))
-        column = lax.rem(n, NX)
-        row = lax.div(n, NX)
-        dv_ref[column, pl.ds(pl.multiple_of(row * tok, tok), tok), :] = got.astype(BF16)
-        return carry
-
-    lax.fori_loop(low, last + 1, spread, 0)
+        out_ref[:tok, part] = (acc_ref[:, at] * share[:, at]).T.astype(BF16)
 
     spare_total = group * spare
     block = extra[:, :spare, :].reshape(spare_total, 2 * width).astype(BF16)
@@ -237,7 +260,35 @@
     outs_ref[...] = dot(p, block[:, width:], ((0,), (0,))).astype(BF16)
     got = dot(p, dos_ref[...], ((1,), (0,))).reshape(NY, NX, spare, width)
     for xx in range(NX):
-        dv_ref[xx, (back + 1) * tok :, :] = got[:, xx].reshape(NY * spare, width).astype(BF16)
+        block_sum = got[:, xx].reshape(NY * spare, width).astype(BF16)
+        dv_ref[xx, back * tok :, :] = block_sum
+
+        @pl.when(x_at == xx)
+        def _(block_sum=block_sum):
+            own_ref[(back + 1) * tok :, :] = block_sum
+
+
+def fold_kernel(place_ref, got_ref, own_ref, out_ref, *, back):
+    y_at, x_at = place_ref[0], place_ref[1]
+    tok = own_ref.shape[0] - got_ref.shape[1]
+    spare = (got_ref.shape[1] - back * tok) // NY
+    extra = own_ref[(back + 1) * tok :, :].astype(F32)
+    for xx in range(NX):
+        part = got_ref[xx, back * tok :, :].astype(F32)
+        extra = extra + jnp.where(x_at == xx, 0.0, part)
+    for i in range(NY):
+        r = lax.rem(i - y_at + back + NY, NY)
+        start = pl.multiple_of(jnp.minimum(r, back) * tok, tok)
+        total = own_ref[pl.ds(start, tok), :].astype(F32)
+        for xx in range(NX):
+            at = r - jnp.where(x_at < xx, 1, 0)
+            seen = (x_at != xx) & (at >= 0) & (at < back)
+            start = pl.multiple_of(jnp.clip(at, 0, back - 1) * tok, tok)
+            part = got_ref[xx, pl.ds(start, tok), :].astype(F32)
+            total = total + jnp.where(seen, part, 0.0)
+        total = jnp.where(r <= back, total, 0.0)
+        total = jnp.concatenate([total, extra[i * spare : (i + 1) * spare]], axis=0)
+        out_ref[i] = total.astype(BF16)
 
 
 def combine_kernel(place_ref, got_ref, hidden_ref, home_ref, mine_ref, other_ref):
@@ -287,10 +338,11 @@
         out_shape=(
             jax.ShapeDtypeStruct(queries.shape, BF16),
             jax.ShapeDtypeStruct(spare_q.shape, BF16),
-            jax.ShapeDtypeStruct((NX, (back + 1) * tok + NY * spare, width), BF16),
+            jax.ShapeDtypeStruct((NX, back * tok + NY * spare, width), BF16),
+            jax.ShapeDtypeStruct(((back + 1) * tok + NY * spare, width), BF16),
         ),
         in_specs=[SMEM] + [VMEM] * 6 + [pl.BlockSpec(memory_space=pl.ANY)] * NX,
-        out_specs=(VMEM, VMEM, VMEM),
+        out_specs=(VMEM,) * 4,
         scratch_shapes=[
             pltpu.VMEM((tok, tok), F32),
             pltpu.VMEM((8, rows), F32),
@@ -308,6 +360,18 @@
     )(place, extra, segment_ids, queries, attn_grad, spare_q, spare_do, *pieces)
 
 
+def fold(place, got, own, tok, back):
+    spare = (got.shape[1] - back * tok) // NY
+    return pl.pallas_call(
+        functools.partial(fold_kernel, back=back),
+        out_shape=jax.ShapeDtypeStruct((NY, tok + spare, got.shape[2]), BF16),
+        in_specs=[SMEM, VMEM, VMEM],
+        out_specs=VMEM,
+        compiler_params=LIMIT,
+        name="fold",
+    )(place, got, own)
+
+
 def combine(place, got, hidden):
     share = hidden.shape[1] // (NY * NX * NK)
     width = got.shape[2]
@@ -350,20 +414,12 @@
         pieces.append(shift(send, "x", NX, s))
 
     place = jnp.stack([y_at, x_at, k_at]).astype(jnp.int32)
-    main_out, spare_out, sums = attend(
+    main_out, spare_out, sums, own_sums = attend(
         place, extras, segment_ids, queries, attn_grad, spare_q, spare_do, pieces, back
     )
 
     got = lax.all_to_all(sums, "x", 0, 0, tiled=True)
-    got = jnp.sum(got.astype(F32), axis=0).astype(BF16)
-    main_part = got[: (back + 1) * tok].reshape(back + 1, tok, width)
-    main_part = jnp.concatenate(
-        [main_part, jnp.zeros((NY - back - 1, tok, width), BF16)], axis=0
-    )
-    main_part = jnp.concatenate([main_part, main_part], axis=0)
-    main_part = lax.dynamic_slice_in_dim(main_part, (back - y_at + NY) % NY, NY, 0)
-    spare_part = got[(back + 1) * tok :].reshape(NY, spare, width)
-    got = lax.all_to_all(jnp.concatenate([main_part, spare_part], axis=1), "y", 0, 0, tiled=True)
+    got = lax.all_to_all(fold(place, got, own_sums, tok, back), "y", 0, 0, tiled=True)
     home, mine, other = combine(place, got, hidden)
     both = (mine + shift(other, "k", NK, 1)).astype(BF16)
     got = lax.all_to_all(both, ("y", "x"), 0, 0, tiled=True)

time: 219 us -> 211 us (0.963)
  blocking collectives: 74.1 us -> 93.8 us
  waiting for transfers between devices: 67.2 us -> 48.5 us
  starting transfers between devices: 52.6 us -> 42.3 us
    all_to_all x1 -> x2, blocking collectives: 29.2 us -> 58.1 us  [the longest x1 38.7 us: body(): lax.all_to_all(fold(place, got, own_sums, tok, back), 'y', 0, 0, tiled=True)]
    all_to_all x1 -> x0, waiting for transfers between devices: 17.9 us -> none  [body(): got = lax.all_to_all(sums, 'x', 0, 0, tiled=True)]
    all_to_all x1 -> x0, starting transfers between devices: 9.52 us -> none  [body(): got = lax.all_to_all(sums, 'x', 0, 0, tiled=True)]
    all_gather x1, blocking collectives: 45 us -> 35.7 us  [body(): every = lax.all_gather(bundle, ('z', 'k'), axis=0)]
    ppermute x8, starting transfers between devices: 32.7 us -> 28.3 us  [shift(): lax.ppermute(array, axis, [(i, (i + step) % size) for i in range(size)])]
    all_to_all x1, starting transfers between devices: 6.3 us -> 9.99 us  [body(): lax.all_to_all(jnp.broadcast_to(extra[None], (NY * NX,) + extra.shape), (...]
  transfers between devices with their start and end apart: 11 -> 10, of which waited for: 7 -> 5; matrix products, arithmetic and copies ran while one was open for 1% -> 1% of each run, Pallas kernels for 0% -> 0%
where the time goes in v5:
time: 211 us; the launch traced here: 209 us
  blocking collectives  93.8 us (44%)
  waiting for transfers between devices  48.5 us (23%)
  starting transfers between devices  42.3 us (20%)
  Pallas kernels  12.8 us (6%)
  local copies, waits for them, and re-layouts  5.09 us (2%)
  other arithmetic  3.81 us (2%)
  between operations  2.91 us (1%)
    all_to_all x1, blocking collectives, body(): lax.all_to_all(fold(place, got, own_sums, tok, back), 'y', 0, 0, tiled=True)  38.7 us
    all_gather x1, blocking collectives, body(): every = lax.all_gather(bundle, ('z', 'k'), axis=0)  35.7 us
    ppermute x8, starting transfers between devices, shift(): lax.ppermute(array, axis, [(i, (i + step) % size) for i in range(size)])  28.3 us
    all_to_all x1, blocking collectives, body(): got = lax.all_to_all(sums, 'x', 0, 0, tiled=True)  19.4 us
    all_to_all x1, waiting for transfers between devices, body(): got = lax.all_to_all(both, ('y', 'x'), 0, 0, tiled=True)  16.4 us
    ppermute x8, waiting for transfers between devices, shift(): lax.ppermute(array, axis, [(i, (i + step) % size) for i in range(size)])  16.4 us
    all_to_all x1, waiting for transfers between devices, body(): lax.all_to_all(jnp.broadcast_to(extra[None], (NY * NX,) + extra.shape), (...  15.7 us
    all_to_all x1, starting transfers between devices, body(): lax.all_to_all(jnp.broadcast_to(extra[None], (NY * NX,) + extra.shape), (...  9.99 us
  transfers between devices with their start and end apart: 10, of which 5 were waited for; matrix products, arithmetic and copies ran while one was open for 1% of the time, Pallas kernels for 0%

profile of v5, /device:TPU:1, one launch (start us, length us, event | category | flops | bytes accessed | tf_op | source)
XLA Modules:
  0.0 209.2 jit_solution(10252442920899164613)
XLA Ops:
  0.6 0.0 copy-start
  0.6 1.3 copy-done
  1.9 0.0 copy-start.3
  1.9 0.9 copy-done.3
  2.8 0.0 copy-start.4
  2.8 0.7 copy-done.4
  3.5 2.6 %project.1 = (bf16[256,256]{1,0:T(8,128)(2,1)S(1)}, bf16[16,256]{1,0:T(8,128)(2,1)S(1)}) custom-call(bf16[264,5120]{1,0:T(8,128)(2,1)} %hidden_ref.3, bf16[5120,128]{1,0:T(8,128)(2,1)S(1)} %copy-done, bf16[264,128]{1,0:T(8,128)(2,1)S(1)} %copy-done.3, s32[1,256]{1,0:T(1,128)S(1)} %copy-done.4), custom_call_target="tpu_custom_call" | custom-call | tf_op jit(solution)/shard_map/project/pallas_call | solution.py:317
  6.2 8.3 %collective-permute-start = (bf16[256,256]{1,0:T(8,128)(2,1)S(1)}, bf16[256,256]{1,0:T(8,128)(2,1)S(1)}, u32[]{:S(2)}, u32[]{:S(2)}) collective-permute-start(bf16[256,256]{1,0:T(8,128)(2,1)S(1)} %get-tuple-element.13), channel_id=1, source_target_pairs={{0,16},{4,20},{8,24},{12,28},{16,0},{20,4},{24,8},{28,12},{1,17},{... | collective-permute-start | bytes 393224 | tf_op jit(solution)/shard_map/ppermute | solution.py:390
  14.4 2.5 %collective-permute-start.1 = (bf16[256,256]{1,0:T(8,128)(2,1)S(1)}, bf16[256,256]{1,0:T(8,128)(2,1)S(1)}, u32[]{:S(2)}, u32[]{:S(2)}) collective-permute-start(bf16[256,256]{1,0:T(8,128)(2,1)S(1)} %get-tuple-element.13), channel_id=1, source_target_pairs={{0,12},{4,16},{8,20},{12,24},{16,28},{20,0},{24,4},{28,8},{1,13},{... | collective-permute-start | bytes 393224 | tf_op jit(solution)/shard_map/ppermute | solution.py:390
  17.0 1.9 collective-permute-start.3
  18.9 3.7 %collective-permute-start.2 = (bf16[256,256]{1,0:T(8,128)(2,1)S(1)}, bf16[256,256]{1,0:T(8,128)(2,1)S(1)}, u32[]{:S(2)}, u32[]{:S(2)}) collective-permute-start(bf16[256,256]{1,0:T(8,128)(2,1)S(1)} %get-tuple-element.13), channel_id=1, source_target_pairs={{0,8},{4,12},{8,16},{12,20},{16,24},{20,28},{24,0},{28,4},{1,9},{5... | collective-permute-start | bytes 393224 | tf_op jit(solution)/shard_map/ppermute | solution.py:390
  22.6 0.0 collective-permute-done
  22.7 4.0 %collective-permute-done.1 = bf16[256,256]{1,0:T(8,128)(2,1)S(1)} collective-permute-done((bf16[256,256]{1,0:T(8,128)(2,1)S(1)}, bf16[256,256]{1,0:T(8,128)(2,1)S(1)}, u32[]{:S(2)}, u32[]{:S(2)}) %collective-permute-start.1) | collective-permute-done | bytes 131104 | tf_op jit(solution)/shard_map/ppermute | solution.py:390
  26.7 9.7 %collective-permute-done.2 = bf16[256,256]{1,0:T(8,128)(2,1)S(1)} collective-permute-done((bf16[256,256]{1,0:T(8,128)(2,1)S(1)}, bf16[256,256]{1,0:T(8,128)(2,1)S(1)}, u32[]{:S(2)}, u32[]{:S(2)}) %collective-permute-start.2) | collective-permute-done | bytes 131104 | tf_op jit(solution)/shard_map/ppermute | solution.py:390
  36.4 0.0 collective-permute-done.3
  36.5 0.0 slice-start
  36.5 0.0 slice-start.1
  36.5 0.0 copy-start.1
  36.5 0.0 copy-start.2
  36.6 0.0 copy-start.5
  36.6 1.3 broadcast_select_fusion
  37.9 3.3 %collective-permute-start.6 = (bf16[1024,256]{1,0:T(8,128)(2,1)}, bf16[1024,256]{1,0:T(8,128)(2,1)S(1)}, u32[]{:S(2)}, u32[]{:S(2)}) collective-permute-start(bf16[1024,256]{1,0:T(8,128)(2,1)} %get-tuple-element.21), channel_id=1, source_target_pairs={{0,3},{1,0},{2,1},{3,2},{4,7},{5,4},{6,5},{7,6},{8,11},{9,8},{10,9... | collective-permute-start | bytes 1572872 | tf_op jit(solution)/shard_map/ppermute | solution.py:390
  41.1 2.4 %collective-permute-start.5 = (bf16[1024,256]{1,0:T(8,128)(2,1)}, bf16[1024,256]{1,0:T(8,128)(2,1)S(1)}, u32[]{:S(2)}, u32[]{:S(2)}) collective-permute-start(bf16[1024,256]{1,0:T(8,128)(2,1)} %get-tuple-element.22), channel_id=1, source_target_pairs={{0,2},{1,3},{2,0},{3,1},{4,6},{5,7},{6,4},{7,5},{8,10},{9,11},{10,... | collective-permute-start | bytes 1572872 | tf_op jit(solution)/shard_map/ppermute | solution.py:390
  43.6 2.5 %collective-permute-start.4 = (bf16[1024,256]{1,0:T(8,128)(2,1)}, bf16[1024,256]{1,0:T(8,128)(2,1)}, u32[]{:S(2)}, u32[]{:S(2)}) collective-permute-start(bf16[1024,256]{1,0:T(8,128)(2,1)} %get-tuple-element.23), channel_id=1, source_target_pairs={{0,1},{1,2},{2,3},{3,0},{4,5},{5,6},{6,7},{7,4},{8,9},{9,10},{10,1... | collective-permute-start | bytes 1572872 | tf_op jit(solution)/shard_map/ppermute | solution.py:390
  46.1 0.7 broadcast_in_dim.2
  46.8 10.0 %all-to-all-start = ((bf16[32,16,256]{2,1,0:T(8,128)(2,1)}), bf16[32,16,256]{2,1,0:T(8,128)(2,1)S(1)}, u32[]{:S(2)}, u32[]{:S(2)}) async-start(bf16[32,16,256]{2,1,0:T(8,128)(2,1)} %broadcast_in_dim.2), calls=%async_computation | async-start | bytes 524288 | tf_op jit(solution)/shard_map/all_to_all | solution.py:406
  56.9 0.0 slice-done
  56.9 0.0 slice-done.1
  56.9 0.1 pad_add_fusion.place_ref
  57.0 15.7 %all-to-all-done = bf16[32,16,256]{2,1,0:T(8,128)(2,1)S(1)} async-done(((bf16[32,16,256]{2,1,0:T(8,128)(2,1)}), bf16[32,16,256]{2,1,0:T(8,128)(2,1)S(1)}, u32[]{:S(2)}, u32[]{:S(2)}) %all-to-all-start) | async-done | bytes 262176 | tf_op jit(solution)/shard_map/all_to_all | solution.py:406
  72.7 0.0 collective-permute-done.6.kv3_ref
  72.7 0.0 collective-permute-done.5.kv2_ref
  72.7 0.0 collective-permute-done.4.kv1_ref
  72.7 0.0 copy-done.1
  72.7 0.0 copy-done.2
  72.7 0.0 copy-done.5
  72.7 6.1 %attend.1 = (bf16[264,1024]{1,0:T(8,128)(2,1)}, bf16[64,128]{1,0:T(8,128)(2,1)S(1)}, bf16[4,1088,128]{2,1,0:T(8,128)(2,1)}, bf16[1344,128]{1,0:T(8,128)(2,1)S(1)}) custom-call(s32[3]{0:T(128)S(1)} %pad_add_fusion.place_ref, bf16[512,256]{1,0:T(8,128)(2,1)S(1)} %bitcast.12, s32[1,256]{1,0:T(1,128)S(1)} %copy-done.5, bf16[264,1024]{1,0:T(8,128)(2,1)S(1)} %copy-done.1, ...), custom_call_target="tpu_custom_call" | custom-call | tf_op jit(solution)/shard_map/attend/pallas_call | solution.py:336
  78.8 19.4 %all_to_all.20.got_ref = bf16[4,1088,128]{2,1,0:T(8,128)(2,1)S(1)} all-to-all(bf16[4,1088,128]{2,1,0:T(8,128)(2,1)} %get-tuple-element.15), channel_id=1, replica_groups=mesh['z'=12,'k'=2,'y'=8,'x'=4] {'x'}, dimensions={0} | all-to-all | bytes 2228224 | tf_op jit(solution)/shard_map/all_to_all | solution.py:421
  98.2 1.1 fold.1
  99.2 38.7 %all_to_all.21.got_ref = bf16[8,264,128]{2,1,0:T(8,128)(2,1)S(1)} all-to-all(bf16[8,264,128]{2,1,0:T(8,128)(2,1)S(1)} %fold.1), channel_id=1, replica_groups=mesh['z'=12,'k'=2,'y'=8,'x'=4] {'y'}, dimensions={0} | all-to-all | bytes 1081344 | tf_op jit(solution)/shard_map/all_to_all | solution.py:422
  137.9 3.1 %combine.1 = (bf16[264,128]{1,0:T(8,128)(2,1)S(1)}, f32[32,80,128]{2,1,0:T(8,128)S(1)}, f32[32,80,128]{2,1,0:T(8,128)S(1)}) custom-call(s32[3]{0:T(128)S(1)} %pad_add_fusion.place_ref, bf16[8,264,128]{2,1,0:T(8,128)(2,1)S(1)} %all_to_all.21.got_ref, bf16[264,5120]{1,0:T(8,128)(2,1)} %hidden_ref.3), custom_call_target="tpu_custom_call" | custom-call | tf_op jit(solution)/shard_map/combine/pallas_call | solution.py:379
  141.0 3.6 %collective-permute-start.7 = (f32[32,80,128]{2,1,0:T(8,128)S(1)}, f32[32,80,128]{2,1,0:T(8,128)S(1)}, u32[]{:S(2)}, u32[]{:S(2)}) collective-permute-start(f32[32,80,128]{2,1,0:T(8,128)S(1)} %get-tuple-element.18), channel_id=1, source_target_pairs={{0,32},{32,0},{1,33},{33,1},{2,34},{34,2},{3,35},{35,3},{4,36},{36... | collective-permute-start | bytes 3932168 | tf_op jit(solution)/shard_map/ppermute | solution.py:390
  144.6 2.6 %collective-permute-done.7 = f32[32,80,128]{2,1,0:T(8,128)S(1)} collective-permute-done((f32[32,80,128]{2,1,0:T(8,128)S(1)}, f32[32,80,128]{2,1,0:T(8,128)S(1)}, u32[]{:S(2)}, u32[]{:S(2)}) %collective-permute-start.7) | collective-permute-done | bytes 1310752 | tf_op jit(solution)/shard_map/ppermute | solution.py:390
  147.2 1.0 add_convert_fusion
  148.2 0.0 copy-start.6
  148.2 4.0 %all-to-all-start.3 = ((bf16[32,80,128]{2,1,0:T(8,128)(2,1)}), bf16[32,80,128]{2,1,0:T(8,128)(2,1)S(1)}, u32[]{:S(2)}, u32[]{:S(2)}) async-start(bf16[32,80,128]{2,1,0:T(8,128)(2,1)} %add_convert_fusion), calls=%async_computation.3 | async-start | bytes 1310720 | tf_op jit(solution)/shard_map/all_to_all | solution.py:425
  152.3 0.0 copy-done.6
  152.3 0.6 dynamic_slice.7
  154.8 16.4 %all-to-all-done.3 = bf16[32,80,128]{2,1,0:T(8,128)(2,1)S(1)} async-done(((bf16[32,80,128]{2,1,0:T(8,128)(2,1)}), bf16[32,80,128]{2,1,0:T(8,128)(2,1)S(1)}, u32[]{:S(2)}, u32[]{:S(2)}) %all-to-all-start.3) | async-done | bytes 655392 | tf_op jit(solution)/shard_map/all_to_all | solution.py:425
  171.3 0.1 reduce_sum.21
  171.4 35.7 %all-gather = bf16[3648,128]{1,0:T(8,128)(2,1)S(1)} all-gather(bf16[152,128]{1,0:T(8,128)(2,1)S(1)} %pad_maximum_fusion.1), channel_id=2, replica_groups=mesh['z'=12,'k'=2,'y'=8,'x'=4] {'z','k'}, dimensions={0}, use_global_device_ids=true | all-gather | bytes 972800 | tf_op jit(solution)/shard_map/all_gather | solution.py:429
  207.2 0.7 convert_reduce_fusion
  207.9 0.6 constant_dynamic-update-slice_fusion.13
  208.5 0.6 pad_maximum_fusion
  (15 shorter events, 0.3 us)
Async XLA Ops:
  0.6 1.3 copy-start
  1.9 0.9 copy-start.3
  2.8 0.7 copy-start.4
  6.2 16.5 %collective-permute-start = (bf16[256,256]{1,0:T(8,128)(2,1)S(1)}, bf16[256,256]{1,0:T(8,128)(2,1)S(1)}, u32[]{:S(2)}, u32[]{:S(2)}) collective-permute-start(bf16[256,256]{1,0:T(8,128)(2,1)S(1)} %get-tuple-element.13), channel_id=1, source_target_pairs={{0,16},{4,20},{8,24},{12,28},{16,0},{20,4},{24,8},{28,12},{1,17},{... | collective-permute-start | bytes 393224 | tf_op jit(solution)/shard_map/ppermute | solution.py:390
  14.4 12.2 %collective-permute-start.1 = (bf16[256,256]{1,0:T(8,128)(2,1)S(1)}, bf16[256,256]{1,0:T(8,128)(2,1)S(1)}, u32[]{:S(2)}, u32[]{:S(2)}) collective-permute-start(bf16[256,256]{1,0:T(8,128)(2,1)S(1)} %get-tuple-element.13), channel_id=1, source_target_pairs={{0,12},{4,16},{8,20},{12,24},{16,28},{20,0},{24,4},{28,8},{1,13},{... | collective-permute-start | bytes 393224 | tf_op jit(solution)/shard_map/ppermute | solution.py:390
  17.0 19.5 %collective-permute-start.3 = (bf16[256,256]{1,0:T(8,128)(2,1)S(1)}, bf16[256,256]{1,0:T(8,128)(2,1)S(1)}, u32[]{:S(2)}, u32[]{:S(2)}) collective-permute-start(bf16[256,256]{1,0:T(8,128)(2,1)S(1)} %get-tuple-element.13), channel_id=1, source_target_pairs={{0,4},{4,8},{8,12},{12,16},{16,20},{20,24},{24,28},{28,0},{1,5},{5... | collective-permute-start | bytes 393224 | tf_op jit(solution)/shard_map/ppermute | solution.py:390
  18.9 17.5 %collective-permute-start.2 = (bf16[256,256]{1,0:T(8,128)(2,1)S(1)}, bf16[256,256]{1,0:T(8,128)(2,1)S(1)}, u32[]{:S(2)}, u32[]{:S(2)}) collective-permute-start(bf16[256,256]{1,0:T(8,128)(2,1)S(1)} %get-tuple-element.13), channel_id=1, source_target_pairs={{0,8},{4,12},{8,16},{12,20},{16,24},{20,28},{24,0},{28,4},{1,9},{5... | collective-permute-start | bytes 393224 | tf_op jit(solution)/shard_map/ppermute | solution.py:390
  36.5 20.3 %slice-start = ((bf16[264,1024]{1,0:T(8,128)(2,1)}), bf16[8,1024]{1,0:T(8,128)(2,1)S(1)}, s32[]{:S(2)}) async-start(bf16[264,1024]{1,0:T(8,128)(2,1)} %q_ref.1), calls=%async_computation.4 | async-start | bytes 32768 | tf_op jit(solution)/shard_map/slice | solution.py:402
  36.5 20.4 %slice-start.1 = ((bf16[264,1024]{1,0:T(8,128)(2,1)}), bf16[8,1024]{1,0:T(8,128)(2,1)S(1)}, s32[]{:S(2)}) async-start(bf16[264,1024]{1,0:T(8,128)(2,1)} %do_ref.1), calls=%async_computation.5 | async-start | bytes 32768 | tf_op jit(solution)/shard_map/slice | solution.py:403
  36.5 36.1 %copy-start.1 = (bf16[264,1024]{1,0:T(8,128)(2,1)S(1)}, bf16[264,1024]{1,0:T(8,128)(2,1)}, u32[]{:S(2)}) copy-start(bf16[264,1024]{1,0:T(8,128)(2,1)} %q_ref.1) | copy-start | bytes 1622020
  36.5 36.1 %copy-start.2 = (bf16[264,1024]{1,0:T(8,128)(2,1)S(1)}, bf16[264,1024]{1,0:T(8,128)(2,1)}, u32[]{:S(2)}) copy-start(bf16[264,1024]{1,0:T(8,128)(2,1)} %do_ref.1) | copy-start | bytes 1622020
  36.6 36.1 %copy-start.5 = (s32[1,256]{1,0:T(1,128)S(1)}, s32[1,256]{1,0:T(1,128)}, u32[]{:S(2)}) copy-start(s32[1,256]{1,0:T(1,128)} %ids_ref.3) | copy-start | bytes 3076
  37.9 34.8 %collective-permute-start.6 = (bf16[1024,256]{1,0:T(8,128)(2,1)}, bf16[1024,256]{1,0:T(8,128)(2,1)S(1)}, u32[]{:S(2)}, u32[]{:S(2)}) collective-permute-start(bf16[1024,256]{1,0:T(8,128)(2,1)} %get-tuple-element.21), channel_id=1, source_target_pairs={{0,3},{1,0},{2,1},{3,2},{4,7},{5,4},{6,5},{7,6},{8,11},{9,8},{10,9... | collective-permute-start | bytes 1572872 | tf_op jit(solution)/shard_map/ppermute | solution.py:390
  41.1 31.5 %collective-permute-start.5 = (bf16[1024,256]{1,0:T(8,128)(2,1)}, bf16[1024,256]{1,0:T(8,128)(2,1)S(1)}, u32[]{:S(2)}, u32[]{:S(2)}) collective-permute-start(bf16[1024,256]{1,0:T(8,128)(2,1)} %get-tuple-element.22), channel_id=1, source_target_pairs={{0,2},{1,3},{2,0},{3,1},{4,6},{5,7},{6,4},{7,5},{8,10},{9,11},{10,... | collective-permute-start | bytes 1572872 | tf_op jit(solution)/shard_map/ppermute | solution.py:390
  43.6 29.1 %collective-permute-start.4 = (bf16[1024,256]{1,0:T(8,128)(2,1)}, bf16[1024,256]{1,0:T(8,128)(2,1)}, u32[]{:S(2)}, u32[]{:S(2)}) collective-permute-start(bf16[1024,256]{1,0:T(8,128)(2,1)} %get-tuple-element.23), channel_id=1, source_target_pairs={{0,1},{1,2},{2,3},{3,0},{4,5},{5,6},{6,7},{7,4},{8,9},{9,10},{10,1... | collective-permute-start | bytes 1572872 | tf_op jit(solution)/shard_map/ppermute | solution.py:390
  46.8 25.8 %all-to-all-start = ((bf16[32,16,256]{2,1,0:T(8,128)(2,1)}), bf16[32,16,256]{2,1,0:T(8,128)(2,1)S(1)}, u32[]{:S(2)}, u32[]{:S(2)}) async-start(bf16[32,16,256]{2,1,0:T(8,128)(2,1)} %broadcast_in_dim.2), calls=%async_computation | async-start | bytes 524288 | tf_op jit(solution)/shard_map/all_to_all | solution.py:406
  141.0 6.3 %collective-permute-start.7 = (f32[32,80,128]{2,1,0:T(8,128)S(1)}, f32[32,80,128]{2,1,0:T(8,128)S(1)}, u32[]{:S(2)}, u32[]{:S(2)}) collective-permute-start(f32[32,80,128]{2,1,0:T(8,128)S(1)} %get-tuple-element.18), channel_id=1, source_target_pairs={{0,32},{32,0},{1,33},{33,1},{2,34},{34,2},{3,35},{35,3},{4,36},{36... | collective-permute-start | bytes 3932168 | tf_op jit(solution)/shard_map/ppermute | solution.py:390
  148.2 4.1 %copy-start.6 = (s32[24]{0:T(128)S(1)}, s32[24]{0:T(128)}, u32[]{:S(2)}) copy-start(s32[24]{0:T(128)} %param.13) | copy-start | bytes 292
  148.2 23.0 %all-to-all-start.3 = ((bf16[32,80,128]{2,1,0:T(8,128)(2,1)}), bf16[32,80,128]{2,1,0:T(8,128)(2,1)S(1)}, u32[]{:S(2)}, u32[]{:S(2)}) async-start(bf16[32,80,128]{2,1,0:T(8,128)(2,1)} %add_convert_fusion), calls=%async_computation.3 | async-start | bytes 1310720 | tf_op jit(solution)/shard_map/all_to_all | solution.py:425
